TPU v7x, 32 devices: a whole 2x2x4 slice. The times are simulated.
32 devices in a mesh: seq: 8 (over z, y), head: 4 (over x, core).
Axes of the slice: x: 2, y: 2, z: 4, core: 2. Of those that a mesh axis runs over, the one named last changes fastest.
Arguments:
- queries: bfloat16 [256, 64, 128], P(None, 'head'), may hold values from -64 to 64
- keys: bfloat16 [512, 16, 8, 128], P('seq', None, 'head'), may hold values from -6 to 6
- values: bfloat16 [512, 16, 8, 128], P('seq', None, 'head'), may hold values from -6 to 6
- page_table: int32 [512], P('seq'), may hold values from 0 to 63, as said below
- offset: int32 [1], replicated, may hold values from 4096 to 7936
- conv_kernel: float32 [64, 6, 11], P('head'), may hold values from -0.6 to 1.6
- head_mix: float32 [64, 2], P('head'), may hold values from -0.8 to 1.8
- out_weight: bfloat16 [8192, 8192], P('head', 'seq'), may hold values from -0.0625 to 0.0625
Outputs:
- projected: bfloat16 [256, 8192], P('head', 'seq')
Inputs may be any that keep to these rules, and one draw needn't show every extreme that they name: `page_table`: each aligned block of 64 entries that starts at a multiple of 64 is a permutation of 0 to 63.
All inputs are finite; a program needn't handle non-finite values.
Results may differ from a plain program's by a relative error of at most 0.02.
Values may be sent and summed in bfloat16 or wider, within the bound.
No kernel may reach another device: no remote copies, remote signals or barrier semaphores. Data moves between devices by JAX's collectives and lax.ppermute only.
A program may use at most 192 MiB of HBM per device.

v0:
```python
import math

import jax
import jax.numpy as jnp
from jax import lax
from jax.sharding import PartitionSpec as P

NEGATIVE = -1e30
PAD_EDGE = 64


def padded(cells, sides, width):
    for axis, dim in sides:
        count = lax.axis_size(axis)
        ends = count - 1
        head = lax.slice_in_dim(cells, 0, width, axis=dim)
        tail = lax.slice_in_dim(cells, cells.shape[dim] - width, cells.shape[dim], axis=dim)
        cells = jnp.concatenate(
            [
                lax.ppermute(tail, axis, [(i, (i + 1) % count) for i in range(ends)]),
                cells,
                lax.ppermute(head, axis, [((i + 1) % count, i) for i in range(ends)]),
            ],
            axis=dim,
        )
    return cells


def per_device(queries, keys, values, page_table, offset, conv_kernel, head_mix, out_weight):
    num_queries = queries.shape[0]
    heads_here = queries.shape[1]
    head_dim = queries.shape[2]
    page_len = keys.shape[1]
    kv_here = keys.shape[2]
    keys_here = keys.shape[0] * page_len
    query_taps = conv_kernel.shape[1]
    key_taps = conv_kernel.shape[2]
    rim_width = (key_taps - 1) // 2
    group_size = head_mix.shape[1]
    per_kv = heads_here // kv_here
    block_len = math.gcd(512, keys_here)
    ext_len = block_len + 2 * PAD_EDGE
    scale = 1.0 / math.sqrt(head_dim)
    logical_keys = jnp.take(keys, page_table, axis=0).reshape(keys_here, kv_here, head_dim)
    logical_values = jnp.take(values, page_table, axis=0).reshape(keys_here, kv_here, head_dim)
    rimmed = padded(logical_keys, (("seq", 0),), rim_width)
    padded_keys = jnp.pad(rimmed, ((PAD_EDGE - rim_width, PAD_EDGE - rim_width), (0, 0), (0, 0)))
    grouped_q = queries.reshape(num_queries, kv_here, per_kv, head_dim)
    first_key = lax.axis_index("seq") * keys_here
    query_pos = offset[0] + jnp.arange(num_queries, dtype=jnp.int32)
    mix_table = head_mix.reshape(heads_here // group_size, group_size, group_size)

    def one_block(carry, block_id):
        peak, total, accum = carry
        block_start = block_id * block_len
        key_block = lax.dynamic_slice_in_dim(padded_keys, block_start, ext_len, 0)
        scores = jnp.einsum(
            "qvgd,kvd->vgqk", grouped_q, key_block, preferred_element_type=jnp.float32
        )
        scores = scores.reshape(heads_here, num_queries, ext_len) * scale
        key_pos = first_key + block_start - PAD_EDGE + jnp.arange(ext_len, dtype=jnp.int32)
        visible = (key_pos[None, :] <= query_pos[:, None]) & (key_pos[None, :] >= 0)
        zeroed = jnp.where(visible[None], scores, 0.0)
        shifted = jnp.pad(zeroed, ((0, 0), (query_taps - 1, 0), (0, 0)))
        convolved = jnp.zeros((heads_here, num_queries, block_len), jnp.float32)
        for qtap in range(query_taps):
            rows = shifted[:, query_taps - 1 - qtap : query_taps - 1 - qtap + num_queries, :]
            for ktap in range(key_taps):
                start_col = PAD_EDGE - rim_width + ktap
                convolved = (
                    convolved
                    + conv_kernel[:, qtap, ktap][:, None, None]
                    * rows[:, :, start_col : start_col + block_len]
                )
        grouped = convolved.reshape(heads_here // group_size, group_size, num_queries, block_len)
        mixed = jnp.zeros_like(grouped)
        for source in range(group_size):
            mixed = mixed + mix_table[:, :, source][:, :, None, None] * grouped[:, source][:, None]
        mixed = mixed.reshape(heads_here, num_queries, block_len)
        inside = visible[:, PAD_EDGE : PAD_EDGE + block_len]
        masked = jnp.where(inside[None], mixed, NEGATIVE)
        new_peak = jnp.maximum(peak, jnp.max(masked, axis=2))
        exps = jnp.where(inside[None], jnp.exp(masked - new_peak[:, :, None]), 0.0)
        decay = jnp.exp(peak - new_peak)
        total = total * decay + jnp.sum(exps, axis=2)
        value_block = lax.dynamic_slice_in_dim(logical_values, block_start, block_len, 0)
        grouped_w = exps.astype(jnp.bfloat16).reshape(kv_here, per_kv, num_queries, block_len)
        product = jnp.einsum(
            "vgqk,kvd->qvgd", grouped_w, value_block, preferred_element_type=jnp.float32
        )
        product = product.reshape(num_queries, heads_here, head_dim)
        accum = accum * decay.T[:, :, None] + product
        return ((new_peak, total, accum), None)

    start_state = (
        jnp.full((heads_here, num_queries), NEGATIVE, jnp.float32),
        jnp.zeros((heads_here, num_queries), jnp.float32),
        jnp.zeros((num_queries, heads_here, head_dim), jnp.float32),
    )
    block_ids = jnp.arange(keys_here // block_len, dtype=jnp.int32)
    (peak, total, accum), unused = lax.scan(one_block, start_state, block_ids)
    peak_rows = peak.T
    total_rows = total.T
    out_rows = accum.reshape(num_queries, heads_here * head_dim)

    def spread(factor):
        return jnp.repeat(factor, head_dim, axis=1)

    peak_all = lax.pmax(peak_rows, "seq")
    factor = jnp.exp(peak_rows - peak_all)
    total_share, out_share = (
        lax.psum_scatter(
            (total_rows * factor).astype(jnp.bfloat16), "seq", scatter_dimension=0, tiled=True
        ).astype(jnp.float32),
        lax.psum_scatter(
            (out_rows * spread(factor)).astype(jnp.bfloat16), "seq", scatter_dimension=0, tiled=True
        ).astype(jnp.float32),
    )
    piece = (out_share / spread(total_share)).astype(jnp.bfloat16)
    attended = lax.all_gather(piece, "seq", axis=0, tiled=True)
    rows = attended
    return lax.psum_scatter(
        jnp.dot(rows, out_weight, preferred_element_type=jnp.float32).astype(jnp.bfloat16),
        "head",
        scatter_dimension=0,
        tiled=True,
    )


def solution(mesh):
    placed = (
        P(None, "head", None),
        P("seq", None, "head", None),
        P("seq", None, "head", None),
        P("seq"),
        P(),
        P("head", None, None),
        P("head", None),
        P("head", "seq"),
    )
    return jax.shard_map(
        per_device, mesh=mesh, in_specs=placed, out_specs=P("head", "seq"), check_vma=False
    )
```

profile of v0, /device:TPU:0, one launch (start us, length us, event | category | flops | bytes accessed | tf_op | source)
XLA Modules:
  0.0 1303.1 jit_solution(143581452694959003)
XLA Ops:
  7.9 1.6 gather_fusion.1
  9.5 2.7 gather_fusion
  12.2 1.9 broadcast_select_fusion
  14.2 4.9 collective-permute-start
  19.1 1.3 collective-permute-start.1
  20.4 0.8 reshape.158
  21.2 0.8 copy.41
  22.0 2.5 copy.39
  24.6 5.5 concatenate.3
  30.1 1.2 pad.11
  31.3 1035.0 %while.17 = (s32[]{:T(128)}, f32[16,256]{1,0:T(8,128)S(1)}, f32[16,256]{1,0:T(8,128)S(1)}, f32[256,16,128]{0,2,1:T(8,128)S(1)}, s32[2]{0:T(128)S(1)}, /*index=5*...) while((s32[]{:T(128)}, f32[16,256]{1,0:T(8,128)S(1)}, ...), condition=%wide.region_3.5_spmd.clone, body=%wide.region_0.4_spmd.clone.sunk | while | flops 1529702528 | bytes 281925696 | solution.py:101
  32.7 6.6 broadcast_multiply_fusion.2
  40.2 9.2 bitcast_select_fusion.2
  49.4 472.8 %multiply_add_fusion.2 = f32[16,256,512]{2,1,0:T(8,128)} fusion(f32[16,256,640]{2,1,0:T(8,128)} %bitcast_select_fusion.2, f32[16]{0:T(128)S(1)} %get-tuple-element.502, f32[16]{0:T(128)S(1)} %get-tuple-element.503, f32[16]{0:T(128)S(1)} %get-tuple-element.504, f32[16]{0:T(128)S(1)} %get-tuple-element.505, f32[16]{0:T(128)S(1)} %get-tuple-element.506, ...), kind=kLoop, calls=%fused_computation.59.clone.1 | loop fusion | flops 274726912 | bytes 111153280 | tf_op jit(solution)/shard_map/while/body/eval_jaxpr/add | solution.py:71
  522.3 4.5 slice_bitcast_fusion.79
  527.0 1.7 copy-done.2
  528.7 1.3 copy-done.4
  530.0 2.4 fusion.79
  532.5 5.7 select_reduce_fusion.2
  538.4 1.1 constant_dynamic-slice_fusion.2
  539.5 0.9 copy.56
  540.4 3.6 mul.2226
  544.0 1.2 mul.2227
  545.3 2.8 fusion.82
  550.0 6.6 broadcast_multiply_fusion.2
  557.5 9.2 bitcast_select_fusion.2
  566.7 472.8 %multiply_add_fusion.2 = f32[16,256,512]{2,1,0:T(8,128)} fusion(f32[16,256,640]{2,1,0:T(8,128)} %bitcast_select_fusion.2, f32[16]{0:T(128)S(1)} %get-tuple-element.502, f32[16]{0:T(128)S(1)} %get-tuple-element.503, f32[16]{0:T(128)S(1)} %get-tuple-element.504, f32[16]{0:T(128)S(1)} %get-tuple-element.505, f32[16]{0:T(128)S(1)} %get-tuple-element.506, ...), kind=kLoop, calls=%fused_computation.59.clone.1 | loop fusion | flops 274726912 | bytes 111153280 | tf_op jit(solution)/shard_map/while/body/eval_jaxpr/add | solution.py:71
  1039.5 4.5 slice_bitcast_fusion.79
  1044.3 1.7 copy-done.2
  1046.0 1.3 copy-done.4
  1047.3 2.4 fusion.79
  1049.8 5.7 select_reduce_fusion.2
  1055.7 1.1 constant_dynamic-slice_fusion.2
  1056.8 0.9 copy.56
  1057.7 3.6 mul.2226
  1061.3 1.2 mul.2227
  1062.6 2.8 fusion.82
  1066.3 38.4 %pmax.7 = f32[256,16]{0,1:T(8,128)S(1)} all-reduce(f32[256,16]{0,1:T(8,128)S(1)} %bitcast.253), channel_id=1, replica_groups=mesh['seq'=8,'head'=4] {'seq'}, use_global_device_ids=true, to_apply=%region_4.6 | all-reduce | flops 4096 | bytes 32768 | tf_op jit(solution)/shard_map/pmax | solution.py:109
  1105.5 1.2 multiply_convert_fusion
  1106.7 2.3 copy.50
  1109.0 55.0 %reduce-scatter.12.cloned.1.call-done = bf16[32,16]{1,0:T(8,128)(2,1)} async-done(((bf16[256,16]{1,0:T(8,128)(2,1)}), bf16[32,16]{1,0:T(8,128)(2,1)}) %reduce-scatter.12.cloned.1.call-update) | async-done | bytes 1040
  1164.1 0.8 copy.53
  1164.8 65.1 %reduce-scatter.10.cloned.1.call-done = bf16[32,2048]{1,0:T(8,128)(2,1)} async-done(((bf16[256,2048]{1,0:T(8,128)(2,1)}), bf16[32,2048]{1,0:T(8,128)(2,1)}) %reduce-scatter.10.cloned.1.call-update) | async-done | bytes 131088
  1229.9 1.2 copy.51
  1231.2 0.8 copy.43
  1232.1 39.3 %all-gather.2.cloned.1.call-done = bf16[256,2048]{1,0:T(8,128)(2,1)} async-done(((bf16[32,2048]{1,0:T(8,128)(2,1)}), bf16[256,2048]{1,0:T(8,128)(2,1)}) %all-gather.2.cloned.1.call-update) | async-done | bytes 1048592 | tf_op jit(solution)/shard_map/all_gather | solution.py:120
  1271.4 4.6 convolution_convert_fusion
  1276.1 20.5 %reduce-scatter.8.cloned.1.call-done = bf16[64,1024]{1,0:T(8,128)(2,1)} async-done(((bf16[256,1024]{1,0:T(8,128)(2,1)}), bf16[64,1024]{1,0:T(8,128)(2,1)}) %reduce-scatter.8.cloned.1.call-update) | async-done | bytes 131088 | tf_op jit(solution)/shard_map/reduce_scatter | solution.py:122
  (79 shorter events, 8.0 us)
Async XLA Ops:
  6.5 1.4 copy-start
  6.5 1157.5 %reduce-scatter.12.cloned.1.call-start = ((), (), s32[]{:S(2)}) async-start(), calls=%async_computation.6 | async-start | bytes 73728
  14.2 10.2 collective-permute-start
  19.1 5.5 collective-permute-start.1
  526.8 1.9 copy-start.2
  526.8 3.2 copy-start.4
  540.4 3.6 copy-start.3
  544.0 1.3 copy-start.5
  1044.0 1.9 copy-start.2
  1044.1 3.2 copy-start.4
  1057.7 3.6 copy-start.3
  1061.3 1.3 copy-start.5
  1105.4 124.5 %reduce-scatter.10.cloned.1.call-start = ((), (), s32[]{:S(2)}) async-start(), calls=%async_computation.5 | async-start | bytes 1179648
  1105.5 191.1 %copy-start.1 = (bf16[64,16,2,128]{3,2,1,0:T(2,128)(2,1)S(1)}, bf16[64,16,2,128]{3,2,1,0:T(2,128)(2,1)}, u32[]{:S(2)}) copy-start(bf16[64,16,2,128]{3,2,1,0:T(2,128)(2,1)} %param.14) | copy-start | bytes 1572868
  1109.0 162.5 %all-gather.2.cloned.1.call-start = ((), (), s32[]{:S(2)}) async-start(), calls=%async_computation.3 | async-start | bytes 1179648 | tf_op jit(solution)/shard_map/all_gather | solution.py:120
  1232.1 64.5 %reduce-scatter.8.cloned.1.call-start = ((), (), s32[]{:S(2)}) async-start(), calls=%async_computation.4 | async-start | bytes 655360 | tf_op jit(solution)/shard_map/reduce_scatter | solution.py:122
Sparse Core Ops, SparseCore 0:
  1105.5 58.4 reduce-scatter.11
  1167.5 62.4 reduce-scatter.9
  1232.3 39.1 all-gather.1
  1276.2 20.3 reduce-scatter.7
where the time goes:
time: 1300 us
  other arithmetic  988 us (76%)
  waiting for transfers between devices  180 us (14%)
  local copies, waits for them, and re-layouts  51.6 us (4%)
  blocking collectives  38.4 us (3%)
  matrix products  23.3 us (2%)
  between operations  13.3 us (1%)
    add x2, other arithmetic, one_block(): convolved + conv_kernel[:, qtap, ktap][:, None, None] * rows[:, :, start_...  946 us
    unnamed x6, waiting for transfers between devices  120 us
    all_gather x1, waiting for transfers between devices, per_device(): attended = lax.all_gather(piece, 'seq', axis=0, tiled=True)  39.3 us
    pmax x1, blocking collectives, per_device(): peak_all = lax.pmax(peak_rows, 'seq')  38.4 us
  transfers between devices with their start and end apart: 6, of which 5 were waited for; matrix products, arithmetic and copies ran while one was open for 1% of the time, Pallas kernels for 0%

commit v1 on v0

v1 whole, which is shorter than its diff:
```python
import functools
import math

import jax
import jax.numpy as jnp
from jax import lax
from jax.experimental import pallas as pl
from jax.experimental.pallas import tpu as pltpu
from jax.sharding import PartitionSpec as P

NEG = -1e30
BF = jnp.bfloat16
F32 = jnp.float32
LANES = 128
BAND = 32
HEAD_PAD = 272
TAIL_PAD = 416
VPAD = 128
LOG2E = 1.4426950408889634


def nt(a, b, **kw):
    return lax.dot_general(a, b, (((1,), (1,)), ((), ())), preferred_element_type=F32, **kw)


def iota(shape, dim):
    return lax.broadcasted_iota(jnp.int32, shape, dim)


def skew(x, shift):
    return pltpu.roll(x, shift, 1, stride=1, stride_axis=0)


def pack_stats(lse, heads):
    hi = lse.astype(BF).astype(F32)
    mid = (lse - hi).astype(BF).astype(F32)
    low = lse - hi - mid
    return hi + pltpu.roll(mid, heads, 1) + pltpu.roll(low, 2 * heads, 1)


def unpack_stats(x, heads):
    x = x.astype(F32)
    return x + pltpu.roll(x, LANES - heads, 1) + pltpu.roll(x, LANES - 2 * heads, 1)


def attend_kernel(dims, kv, off_ref, table_ref, q_ref, k_ref, v_ref, left_ref, right_ref,
                  toep_ref, band_ref, keep_ref, send_ref,
                  kext, krot, kwrap, vext, khat, vhat, qhat, toep, s_ref, out, stat, fsc, msc):
    rows, heads, kvs, pages, page, qtaps, ktaps, keys_here, split_bit = dims
    hk = heads // kvs
    pairs = hk // 2
    rim = (ktaps - 1) // 2
    nblk = keys_here // LANES
    base = HEAD_PAD
    seq = lax.axis_index("seq")
    diag = off_ref[0] - seq * keys_here
    has_diag = (diag >= 1 - rows) & (diag <= keys_here + 8)
    shift = jnp.where(has_diag, lax.rem(diag + 2 * LANES, LANES), 0)

    kext[pl.ds(0, base - page), :] = jnp.zeros((base - page, LANES), F32)
    kext[pl.ds(base + keys_here + page, TAIL_PAD - page), :] = jnp.zeros((TAIL_PAD - page, LANES), F32)
    kext[pl.ds(base - page, page), :] = left_ref[pl.ds(kv, page, stride=kvs), :]
    kext[pl.ds(base + keys_here, page), :] = right_ref[pl.ds(kv, page, stride=kvs), :]
    vext[pl.ds(0, VPAD), :] = jnp.zeros((VPAD, LANES), F32)
    vext[pl.ds(VPAD + keys_here, VPAD), :] = jnp.zeros((VPAD, LANES), F32)
    for p in range(pages):
        src = table_ref[p] * (page * kvs) + kv
        kext[pl.ds(base + p * page, page), :] = k_ref[pl.ds(src, page, stride=kvs), :]
        vext[pl.ds(VPAD + p * page, page), :] = v_ref[pl.ds(src, page, stride=kvs), :]
    krot[...] = kext[pl.ds(base - 8 + shift, keys_here + 16), :]
    kwrap[...] = kext[pl.ds(base - 8 - LANES + shift, LANES + 16), :]
    first = iota((LANES, LANES), 0) < LANES - shift
    for n in range(nblk):
        for b in range(ktaps):
            part = krot[pl.ds(n * LANES + 8 + b - rim, LANES), :]
            if n == nblk - 1:
                part = jnp.where(first, part, kwrap[pl.ds(8 + b - rim, LANES), :])
            khat[pl.ds(n * LANES, LANES), b * LANES:(b + 1) * LANES] = part.astype(BF)
        part = vext[pl.ds(VPAD + n * LANES + shift, LANES), :]
        if n == nblk - 1:
            part = jnp.where(first, part, vext[pl.ds(shift, LANES), :])
        vhat[pl.ds(n * LANES, LANES), 0:LANES] = part.astype(BF)
    vhat[:, LANES:] = jnp.ones((keys_here, LANES), BF)

    def make_queries(p):
        per = ktaps * BAND
        for h in range(2):
            for b in range(ktaps):
                row = toep_ref[pl.ds((p * 2 + h) * ktaps + b, 1), :]
                t32 = skew(jnp.broadcast_to(row, (BAND, LANES)), 0)
                hi = t32.astype(BF)
                low = (t32 - hi.astype(F32)).astype(BF)
                at = h * per + b * BAND
                toep[pl.ds(at, BAND), 0:LANES] = hi
                toep[pl.ds(at, BAND), LANES:] = low
        for t in range(rows // (2 * BAND)):
            r0 = t * 2 * BAND
            halves = []
            for g in range(2):
                col = pl.multiple_of(((kv * pairs + p) * 2 + g) * LANES, LANES)
                two = q_ref[pl.ds(r0, 2 * BAND), pl.ds(col, LANES)]
                if t == 0:
                    one = jnp.concatenate([jnp.zeros((BAND, LANES), BF), two[:BAND]], axis=0)
                else:
                    one = q_ref[pl.ds(r0 - BAND, 2 * BAND), pl.ds(col, LANES)]
                halves.append(jnp.concatenate([one, two], axis=1))
            rhs = jnp.concatenate(halves + halves, axis=0)
            y = jnp.dot(toep[...], rhs, preferred_element_type=F32)
            for h in range(2):
                for b in range(ktaps):
                    at = h * per + b * BAND
                    for e in range(2):
                        qhat[h, pl.ds(r0 + e * BAND, BAND), b * LANES:(b + 1) * LANES] = (
                            y[at:at + BAND, e * LANES:(e + 1) * LANES].astype(BF))

    def finish(p, h, s):
        peak = jnp.max(s, axis=1, keepdims=True)
        w = jnp.exp2(s - peak).astype(BF)
        o = jnp.dot(w, vhat[...], preferred_element_type=F32)
        total = o[:, LANES:]
        head = p * 2 + h
        out[:, pl.ds(pl.multiple_of(head * LANES, LANES), LANES)] = (o[:, :LANES] / total).astype(BF)
        lse = peak + jnp.log2(total)
        stat[...] = jnp.where(iota((rows, LANES), 1) == head, lse, stat[...])

    stat[...] = jnp.zeros((rows, LANES), F32)

    @pl.when(diag > keys_here + 8)
    def _():
        def body(p, c):
            make_queries(p)
            for h in range(2):
                finish(p, h, nt(qhat[h], khat[...]))
            return c
        lax.fori_loop(0, pairs, body, 0)

    @pl.when(has_diag)
    def _():
        nwin = 3 * LANES
        win = kext[pl.ds(base + diag, nwin), :].astype(BF)
        flip = (iota((nwin, nwin), 0) + iota((nwin, nwin), 1) == nwin - 1).astype(F32).astype(BF)
        rev = jnp.dot(flip, win, preferred_element_type=F32).astype(BF)
        lane = iota((LANES, LANES), 1)
        row = iota((LANES, LANES), 0)
        future = (lane >= 127 - 10) & (lane <= 126)
        fsc[:, 0:8, :] = jnp.zeros((2, 8, LANES), F32)
        msc[...] = jnp.zeros((2, 2 * LANES, LANES), F32)
        block0 = (diag + 2 * LANES - shift) // LANES - 2

        def body(p, c):
            make_queries(p)
            for g in range(2):
                col = pl.multiple_of(((kv * pairs + p) * 2 + g) * LANES, LANES)
                w = nt(q_ref[:, pl.ds(col, LANES)], rev)
                for f in range(rows // LANES):
                    sub = w[f * LANES:(f + 1) * LANES]
                    near = skew(sub[:, (2 - f) * LANES:(3 - f) * LANES], 0)
                    far = skew(sub[:, (1 - f) * LANES:(2 - f) * LANES], 0)
                    both = jnp.where(row <= lane, near, far)
                    fsc[g, pl.ds(8 + f * LANES, LANES), :] = jnp.where(future, both, 0.0)
            tiles = [None, None]
            for g in range(2):
                for a in range(qtaps):
                    slot = qtaps * g + a
                    part = pltpu.roll(fsc[g, pl.ds(8 - a, rows), :], (16 * slot + 16) % LANES, 1)
                    i = slot // 8
                    tiles[i] = part if tiles[i] is None else tiles[i] + part
            fst = jnp.concatenate(tiles, axis=1)
            for h in range(2):
                taps = band_ref[p * 2 + h]
                for u in range(5, 15):
                    msc[h, pl.ds(u, 16, stride=16), :] = pltpu.roll(taps, 21 - u, 1)
            col_key = iota((1, keys_here), 1) + shift
            col_key = jnp.where(col_key >= keys_here, col_key - keys_here, col_key)
            visible = col_key <= diag + iota((rows, 1), 0)
            for h in range(2):
                s_ref[...] = nt(qhat[h], khat[...])
                corr = jnp.dot(fst, msc[h], preferred_element_type=F32, precision=lax.Precision.HIGHEST)
                for f in range(rows // LANES):
                    r = skew(corr[f * LANES:(f + 1) * LANES], 112)
                    for e in range(2):
                        y = lane - row + (16 if e else -112)
                        n = block0 - 1 + f + e
                        low = jnp.where(n == -1, LANES - shift, 0)
                        high = jnp.where(n == nblk - 1, LANES - shift, LANES)
                        high = jnp.where((n >= -1) & (n < nblk), high, 0)
                        at = jnp.where(n == -1, nblk - 1, jnp.clip(n, 0, nblk - 1))
                        ok = (y >= 7) & (y <= 16) & (lane >= low) & (lane < high)
                        where = (pl.ds(f * LANES, LANES), pl.ds(pl.multiple_of(at * LANES, LANES), LANES))
                        s_ref[where] = s_ref[where] - jnp.where(ok, r, 0.0)
                finish(p, h, jnp.where(visible, s_ref[...], NEG))
            return c
        lax.fori_loop(0, pairs, body, 0)

    @pl.when(diag < 1 - rows)
    def _():
        out[...] = jnp.zeros_like(out)
        stat[...] = jnp.where(iota((rows, LANES), 1) < hk, NEG, 0.0)

    half = rows // 2
    side = lax.rem(seq // split_bit, 2)
    stats = pack_stats(stat[...], hk)
    stat[...] = stats
    for ref, part in ((keep_ref, side), (send_ref, 1 - side)):
        at = pl.multiple_of(part * half, half)
        ref[:, :hk * LANES] = out[pl.ds(at, half), :]
        ref[:, hk * LANES:] = stat[pl.ds(at, half), :].astype(BF)


def attend(kv, offset, table, q2, k2, v2, left, right, toep_rows, band_rows, kvs, page, conv_shape):
    rows = q2.shape[0]
    heads, qtaps, ktaps = conv_shape
    hk = heads // kvs
    pages = table.shape[0]
    keys_here = pages * page
    dims = (rows, heads, kvs, pages, page, qtaps, ktaps, keys_here, 1)
    smem = pl.BlockSpec(memory_space=pltpu.SMEM)
    vmem = pl.BlockSpec(memory_space=pltpu.VMEM)
    width = hk * LANES + LANES
    shape = jax.ShapeDtypeStruct((rows // 2, width), BF)
    flops = 2 * hk * rows * keys_here * (ktaps + 2) * LANES
    return pl.pallas_call(
        functools.partial(attend_kernel, dims, kv),
        out_shape=(shape, shape),
        in_specs=[smem, smem] + [vmem] * 7,
        out_specs=(vmem, vmem),
        scratch_shapes=[
            pltpu.VMEM((HEAD_PAD + keys_here + TAIL_PAD, LANES), F32),
            pltpu.VMEM((keys_here + 16, LANES), F32),
            pltpu.VMEM((LANES + 16, LANES), F32),
            pltpu.VMEM((keys_here + 2 * VPAD, LANES), F32),
            pltpu.VMEM((keys_here, ktaps * LANES), BF),
            pltpu.VMEM((keys_here, 2 * LANES), BF),
            pltpu.VMEM((2, rows, ktaps * LANES), BF),
            pltpu.VMEM((2 * ktaps * BAND, 2 * LANES), BF),
            pltpu.VMEM((rows, keys_here), F32),
            pltpu.VMEM((rows, hk * LANES), BF),
            pltpu.VMEM((rows, LANES), F32),
            pltpu.VMEM((2, rows + 8, LANES), F32),
            pltpu.VMEM((2, 2 * LANES, LANES), F32),
        ],
        compiler_params=pltpu.CompilerParams(vmem_limit_bytes=40 * 2**20),
        cost_estimate=pl.CostEstimate(flops=flops, bytes_accessed=4 * 2**20, transcendentals=hk * rows * keys_here),
        name=f"attend{kv}",
    )(offset, table, q2, k2, v2, left, right, toep_rows, band_rows)


def merge_kernel(hk, bit, last, a_ref, b_ref, *rest):
    if last:
        (keep_ref,) = rest
    else:
        keep_ref, send_ref, buf = rest
    wide = hk * LANES
    la = unpack_stats(a_ref[:, wide:], hk)
    lb = unpack_stats(b_ref[:, wide:], hk)
    top = jnp.maximum(la, lb)
    lse = top + jnp.log2(jnp.exp2(la - top) + jnp.exp2(lb - top))
    wa = jnp.exp2(la - lse)
    wb = jnp.exp2(lb - lse)
    rows = a_ref.shape[0]
    for h in range(hk):
        cols = slice(h * LANES, (h + 1) * LANES)
        mixed = a_ref[:, cols].astype(F32) * wa[:, h:h + 1] + b_ref[:, cols].astype(F32) * wb[:, h:h + 1]
        if last:
            keep_ref[:, cols] = mixed.astype(BF)
        else:
            buf[:, cols] = mixed
    if not last:
        lse = jnp.where(iota((rows, LANES), 1) < hk, lse, 0.0)
        buf[:, wide:] = pack_stats(lse, hk)
        side = lax.rem(lax.axis_index("seq") // bit, 2)
        half = rows // 2
        keep_ref[...] = buf[pl.ds(pl.multiple_of(side * half, half), half), :].astype(BF)
        send_ref[...] = buf[pl.ds(pl.multiple_of((1 - side) * half, half), half), :].astype(BF)


def merge(a, b, hk, bit, last):
    rows, width = a.shape
    vmem = pl.BlockSpec(memory_space=pltpu.VMEM)
    if last:
        shapes = jax.ShapeDtypeStruct((rows, hk * LANES), BF)
        specs, scratch = vmem, []
    else:
        one = jax.ShapeDtypeStruct((rows // 2, width), BF)
        shapes, specs = (one, one), (vmem, vmem)
        scratch = [pltpu.VMEM((rows, width), F32)]
    return pl.pallas_call(
        functools.partial(merge_kernel, hk, bit, last),
        out_shape=shapes,
        in_specs=[vmem, vmem],
        out_specs=specs,
        scratch_shapes=scratch,
        cost_estimate=pl.CostEstimate(flops=4 * rows * width, bytes_accessed=6 * rows * width, transcendentals=rows * LANES * 5),
        name=f"merge{bit}",
    )(a, b)


def project_kernel(pieces, heads_axis, *refs):
    xs = refs[:pieces]
    w_ref, keep_ref, send_ref, xbuf = refs[pieces:]
    seq = lax.axis_index("seq")
    count = lax.axis_size("seq")
    bits = count.bit_length() - 1
    mine = 0
    for i in range(bits):
        mine = mine * 2 + lax.rem(seq // (1 << i), 2)
    rows = xbuf.shape[0]
    unit = rows // count
    per = pieces // (bits + 1)
    width = xs[0].shape[1]
    for c in range(pieces // (bits + 1)):
        cols = slice(c * width, (c + 1) * width)
        held = 0
        for x_ref in xs[c * (bits + 1):(c + 1) * (bits + 1)]:
            for k in range(x_ref.shape[0] // unit):
                to = jnp.bitwise_xor(mine, held)
                xbuf[pl.ds(pl.multiple_of(to * unit, unit), unit), cols] = x_ref[pl.ds(k * unit, unit), :].astype(xbuf.dtype)
                held += 1
    y = jnp.dot(xbuf[...].astype(BF), w_ref[...], preferred_element_type=F32)
    core = lax.rem(lax.axis_index("head"), 2)
    block = rows // heads_axis
    for g in range(heads_axis // 2):
        even = y[(2 * g) * block:(2 * g + 1) * block]
        odd = y[(2 * g + 1) * block:(2 * g + 2) * block]
        keep_ref[pl.ds(g * block, block), :] = jnp.where(core == 0, even, odd)
        send_ref[pl.ds(g * block, block), :] = jnp.where(core == 0, odd, even).astype(BF)


def project(pieces, weight, rows):
    heads_axis = lax.axis_size("head")
    vmem = pl.BlockSpec(memory_space=pltpu.VMEM)
    depth, cols = weight.shape
    unit = rows // lax.axis_size("seq")
    return pl.pallas_call(
        functools.partial(project_kernel, len(pieces), heads_axis),
        out_shape=(jax.ShapeDtypeStruct((rows // 2, cols), F32), jax.ShapeDtypeStruct((rows // 2, cols), BF)),
        in_specs=[vmem] * (len(pieces) + 1),
        out_specs=(vmem, vmem),
        scratch_shapes=[pltpu.VMEM((rows, depth), BF if unit % 16 == 0 else F32)],
        compiler_params=pltpu.CompilerParams(vmem_limit_bytes=40 * 2**20),
        cost_estimate=pl.CostEstimate(flops=2 * rows * depth * cols, bytes_accessed=2 * depth * cols, transcendentals=0),
        name="project",
    )(*pieces, weight)


def swap(x, axis, bit):
    count = lax.axis_size(axis)
    return lax.ppermute(x, axis, [(i, i ^ bit) for i in range(count)])


def per_device(queries, keys, values, page_table, offset, conv_kernel, head_mix, out_weight):
    rows, heads, head_dim = queries.shape
    pages, page, kvs, _ = keys.shape
    qtaps, ktaps = conv_kernel.shape[1:]
    group = head_mix.shape[1]
    hk = heads // kvs
    seq_count = lax.axis_size("seq")
    head_count = lax.axis_size("head")

    flat = pages * page * kvs
    ends = seq_count - 1

    def page_of(p):
        return lax.dynamic_slice_in_dim(keys, page_table[p], 1, 0).reshape(page * kvs, head_dim).astype(F32)

    left = lax.ppermute(page_of(pages - 1).astype(BF), "seq", [(i, i + 1) for i in range(ends)]).astype(F32)
    right = lax.ppermute(page_of(0).astype(BF), "seq", [(i + 1, i) for i in range(ends)]).astype(F32)

    k2 = keys.astype(F32).reshape(flat, head_dim)
    v2 = values.astype(F32).reshape(flat, head_dim)
    q2 = queries.reshape(rows, heads * head_dim)

    scale = LOG2E / math.sqrt(head_dim)
    taps = (head_mix * scale).reshape(heads // group, group, group, 1, 1) * conv_kernel.reshape(
        heads // group, 1, group, qtaps, ktaps)
    rows_t = jnp.flip(jnp.transpose(taps, (0, 1, 4, 2, 3)), 4)
    lead = BAND - (qtaps - 1)
    rows_t = jnp.pad(rows_t, ((0, 0),) * 4 + ((lead, 2 * BAND - lead - qtaps),)).reshape(heads * ktaps, 4 * BAND)
    band = jnp.flip(taps, 4)
    band = jnp.stack(
        [jnp.pad(band[:, :, :, a], ((0, 0),) * 3 + ((qtaps - 1 - a, LANES - ktaps - (qtaps - 1 - a)),)) for a in range(qtaps)],
        axis=3,
    ).reshape(heads, group * qtaps, LANES)
    band = jnp.pad(band, ((0, 0), (0, 16 - group * qtaps), (0, 0)))

    bits = [1 << i for i in range(seq_count.bit_length() - 1)]
    pieces = []
    for kv in range(kvs):
        toep_rows = rows_t[kv * hk * ktaps:(kv + 1) * hk * ktaps]
        band_rows = band[kv * hk:(kv + 1) * hk]
        keep, send = attend(kv, offset, page_table, q2, k2, v2, left, right, toep_rows, band_rows,
                            kvs, page, conv_kernel.shape)
        for i, bit in enumerate(bits):
            got = swap(send, "seq", bit)
            if i + 1 < len(bits):
                keep, send = merge(keep, got, hk, bits[i + 1], False)
            else:
                piece = merge(keep, got, hk, 0, True)
        held = [piece]
        for bit in reversed(bits):
            whole = held[0] if len(held) == 1 else jnp.concatenate(held, axis=0)
            held.append(swap(whole, "seq", bit))
        pieces += held

    keep, send = project(pieces, out_weight, rows)
    me = lax.axis_index("head")
    got = swap(send, "head", 1)
    total = keep + got.astype(F32)
    block = rows // head_count
    bit = 2
    while bit < head_count:
        parts = total.reshape(-1, 2, block, total.shape[1])
        high = (me // bit) % 2 == 1
        mine = jnp.where(high, parts[:, 1], parts[:, 0])
        other = jnp.where(high, parts[:, 0], parts[:, 1]).astype(BF)
        got = swap(other, "head", bit)
        total = (mine + got.astype(F32)).reshape(-1, total.shape[1])
        bit *= 2
    return total.astype(BF)


def solution(mesh):
    placed = (
        P(None, "head", None),
        P("seq", None, "head", None),
        P("seq", None, "head", None),
        P("seq"),
        P(),
        P("head", None, None),
        P("head", None),
        P("head", "seq"),
    )
    return jax.shard_map(
        per_device, mesh=mesh, in_specs=placed, out_specs=P("head", "seq"), check_vma=False
    )
```

time: 1300 us -> 126 us (0.10)
  other arithmetic: 988 us -> 6.28 us
  waiting for transfers between devices: 180 us -> 20.7 us
  Pallas kernels: 0 us -> 41.9 us
  blocking collectives: 38.4 us -> 0 us
  local copies, waits for them, and re-layouts: 51.6 us -> 16.7 us
  starting transfers between devices: 6.29 us -> 35.1 us
  matrix products: 23.3 us -> 0 us
    add x10 -> x1, other arithmetic: 948 us -> 0.06 us  [per_device(): total = keep + got.astype(F32)]
    unnamed x6 -> x0, waiting for transfers between devices: 120 us -> none
    pallas_call x0 -> x9, Pallas kernels: none -> 41.9 us  [the longest x2 28.4 us: attend(): pl.pallas_call(functools.partial(attend_kernel, dims, kv), out_shape=(sha...]
    all_gather x1 -> x0, waiting for transfers between devices: 39.3 us -> none  [per_device(): attended = lax.all_gather(piece, 'seq', axis=0, tiled=True)]
    pmax x1 -> x0, blocking collectives: 38.4 us -> none  [per_device(): peak_all = lax.pmax(peak_rows, 'seq')]
    ppermute x2 -> x16, starting transfers between devices: 6.16 us -> 35.1 us  [the longest x14 29 us: swap(): return lax.ppermute(x, axis, [(i, i ^ bit) for i in range(count)])]
    dot_general x5 -> x0, matrix products: 23.3 us -> none  [the longest x2 13.2 us: one_block(): jnp.einsum('qvgd,kvd->vgqk', grouped_q, key_block, preferred_element_type...]
    select_n x4 -> x0, other arithmetic: 21 us -> none  [the longest x2 18.4 us: one_block(): zeroed = jnp.where(visible[None], scores, 0.0)]
  transfers between devices with their start and end apart: 6 -> 16, of which waited for: 5 -> 10; matrix products, arithmetic and copies ran while one was open for 1% -> 9% of each run, Pallas kernels for 0% -> 21%
where the time goes in v1:
time: 126 us; the launch traced here: 125 us
  Pallas kernels  41.9 us (33%)
  starting transfers between devices  35.1 us (28%)
  waiting for transfers between devices  20.7 us (16%)
  local copies, waits for them, and re-layouts  16.7 us (13%)
  other arithmetic  6.28 us (5%)
  between operations  4.77 us (4%)
    ppermute x14, starting transfers between devices, swap(): return lax.ppermute(x, axis, [(i, i ^ bit) for i in range(count)])  29 us
    pallas_call x2, Pallas kernels, attend(): pl.pallas_call(functools.partial(attend_kernel, dims, kv), out_shape=(sha...  28.4 us
    ppermute x14, waiting for transfers between devices, swap(): return lax.ppermute(x, axis, [(i, i ^ bit) for i in range(count)])  20.7 us
    pallas_call x6, Pallas kernels, merge(): pl.pallas_call(functools.partial(merge_kernel, hk, bit, last), out_shape=...  12.2 us
    unnamed x33, local copies, waits for them, and re-layouts  12.1 us
    ppermute x1, starting transfers between devices, per_device(): lax.ppermute(page_of(pages - 1).astype(BF), 'seq', [(i, i + 1) for i in r...  4.87 us
    concatenate x4, other arithmetic, per_device(): whole = held[0] if len(held) == 1 else jnp.concatenate(held, axis=0)  3.41 us
  transfers between devices with their start and end apart: 16, of which 10 were waited for; matrix products, arithmetic and copies ran while one was open for 9% of the time, Pallas kernels for 21%

profile of v1, /device:TPU:0, one launch (start us, length us, event | category | flops | bytes accessed | tf_op | source)
XLA Modules:
  0.0 125.5 jit_solution(1286788758254905601)
XLA Ops:
  0.0 1.4 %fusion.4 = (s32[1]{0:T(128)}, s32[1]{0:T(128)}) fusion(s32[64]{0:T(128)} %table_ref.3), kind=kLoop, calls=%fused_computation.27 | loop fusion | bytes 16 | tf_op jit(solution)/shard_map/slice | solution.py:364
  5.2 0.7 constant_dynamic-slice_fusion
  6.0 4.9 %collective-permute-start = (bf16[32,128]{1,0:T(8,128)(2,1)S(1)}, bf16[32,128]{1,0:T(8,128)(2,1)S(1)}, u32[]{:S(2)}, u32[]{:S(2)}) collective-permute-start(bf16[32,128]{1,0:T(8,128)(2,1)S(1)} %bitcast.74), channel_id=1, source_target_pairs={{0,4},{4,8},{8,12},{12,16},{16,20},{20,24},{24,28},{1,5},{5,9},{9,... | collective-permute-start | bytes 24584 | tf_op jit(solution)/shard_map/ppermute | solution.py:366
  10.9 1.3 %collective-permute-start.1 = (bf16[32,128]{1,0:T(8,128)(2,1)S(1)}, bf16[32,128]{1,0:T(8,128)(2,1)S(1)}, u32[]{:S(2)}, u32[]{:S(2)}) collective-permute-start(bf16[32,128]{1,0:T(8,128)(2,1)S(1)} %bitcast.73), channel_id=1, source_target_pairs={{4,0},{8,4},{12,8},{16,12},{20,16},{24,20},{28,24},{5,1},{9,5},{13... | collective-permute-start | bytes 24584 | tf_op jit(solution)/shard_map/ppermute | solution.py:367
  12.2 0.9 copy.19
  15.7 0.8 rev.6
  16.8 1.5 %copy.30 = bf16[32,8,16,128]{3,1,2,0:T(8,128)(2,1)S(1)} copy(bf16[32,8,16,128]{3,2,1,0:T(8,128)(2,1)} %bitcast.61) | data formatting | bytes 2097152
  18.4 1.1 convert.3.v_ref
  20.3 13.7 %attend1.1 = (bf16[128,1152]{1,0:T(8,128)(2,1)S(1)}, bf16[128,1152]{1,0:T(8,128)(2,1)S(1)}) custom-call(s32[1]{0:T(128)S(6)} %copy.36.off_ref, s32[64]{0:T(128)S(1)} %copy-done.5, bf16[256,2048]{1,0:T(8,128)(2,1)S(1)} %bitcast.57, f32[2048,128]{1,0:T(8,128)S(1)} %convert.2.k_ref, f32[2048,128]{1,0:T(8,128)S(1)} %convert.3.v_ref, ...), custom_call_target="tpu_custom_call" | custom-call | flops 6979321856 | bytes 4194304 | tf_op jit(solution)/shard_map/attend1/pallas_call | solution.py:222
  34.1 0.7 copy-done.4
  34.8 2.6 %collective-permute-start.8 = (bf16[128,1152]{1,0:T(8,128)(2,1)S(1)}, bf16[128,1152]{1,0:T(8,128)(2,1)S(1)}, u32[]{:S(2)}, u32[]{:S(2)}) collective-permute-start(bf16[128,1152]{1,0:T(8,128)(2,1)S(1)} %get-tuple-element.26), channel_id=1, source_target_pairs={{0,4},{4,0},{8,12},{12,8},{16,20},{20,16},{24,28},{28,24},{1,5},{5... | collective-permute-start | bytes 884744 | tf_op jit(solution)/shard_map/ppermute | solution.py:348
  37.5 14.6 %attend0.1 = (bf16[128,1152]{1,0:T(8,128)(2,1)S(1)}, bf16[128,1152]{1,0:T(8,128)(2,1)}) custom-call(s32[1]{0:T(128)S(6)} %copy.36.off_ref, s32[64]{0:T(128)S(1)} %copy-done.5, bf16[256,2048]{1,0:T(8,128)(2,1)S(1)} %bitcast.58, f32[2048,128]{1,0:T(8,128)S(1)} %convert.2.k_ref, f32[2048,128]{1,0:T(8,128)S(1)} %convert.3.v_ref, ...), custom_call_target="tpu_custom_call" | custom-call | flops 6979321856 | bytes 4194304 | tf_op jit(solution)/shard_map/attend0/pallas_call | solution.py:222
  52.1 0.7 copy-done.3
  52.8 0.7 copy-done.7
  53.5 2.3 %merge2.3 = (bf16[64,1152]{1,0:T(8,128)(2,1)}, bf16[64,1152]{1,0:T(8,128)(2,1)}) custom-call(bf16[128,1152]{1,0:T(8,128)(2,1)} %copy-done.4, bf16[128,1152]{1,0:T(8,128)(2,1)} %copy-done.7), custom_call_target="tpu_custom_call" | custom-call | flops 589824 | bytes 884736 | tf_op jit(solution)/shard_map/merge2/pallas_call | solution.py:287
  55.8 3.0 %collective-permute-start.9 = (bf16[64,1152]{1,0:T(8,128)(2,1)}, bf16[64,1152]{1,0:T(8,128)(2,1)S(1)}, u32[]{:S(2)}, u32[]{:S(2)}) collective-permute-start(bf16[64,1152]{1,0:T(8,128)(2,1)} %get-tuple-element.28), channel_id=1, source_target_pairs={{0,8},{4,12},{8,0},{12,4},{16,24},{20,28},{24,16},{28,20},{1,9},{5... | collective-permute-start | bytes 442376 | tf_op jit(solution)/shard_map/ppermute | solution.py:348
  58.8 2.1 %collective-permute-done.2.b_ref = bf16[128,1152]{1,0:T(8,128)(2,1)S(1)} collective-permute-done((bf16[128,1152]{1,0:T(8,128)(2,1)}, bf16[128,1152]{1,0:T(8,128)(2,1)S(1)}, u32[]{:S(2)}, u32[]{:S(2)}) %collective-permute-start.2) | collective-permute-done | bytes 294944 | tf_op jit(solution)/shard_map/ppermute | solution.py:348
  60.9 0.7 copy-done.8
  61.6 2.3 %merge2.2 = (bf16[64,1152]{1,0:T(8,128)(2,1)}, bf16[64,1152]{1,0:T(8,128)(2,1)}) custom-call(bf16[128,1152]{1,0:T(8,128)(2,1)} %copy-done.3, bf16[128,1152]{1,0:T(8,128)(2,1)} %copy-done.8), custom_call_target="tpu_custom_call" | custom-call | flops 589824 | bytes 884736 | tf_op jit(solution)/shard_map/merge2/pallas_call | solution.py:287
  64.0 1.6 %collective-permute-start.3 = (bf16[64,1152]{1,0:T(8,128)(2,1)}, bf16[64,1152]{1,0:T(8,128)(2,1)S(1)}, u32[]{:S(2)}, u32[]{:S(2)}) collective-permute-start(bf16[64,1152]{1,0:T(8,128)(2,1)} %get-tuple-element.22), channel_id=1, source_target_pairs={{0,8},{4,12},{8,0},{12,4},{16,24},{20,28},{24,16},{28,20},{1,9},{5... | collective-permute-start | bytes 442376 | tf_op jit(solution)/shard_map/ppermute | solution.py:348
  66.2 2.0 %merge4.3 = (bf16[32,1152]{1,0:T(8,128)(2,1)}, bf16[32,1152]{1,0:T(8,128)(2,1)}) custom-call(bf16[64,1152]{1,0:T(8,128)(2,1)} %get-tuple-element.27.a_ref, bf16[64,1152]{1,0:T(8,128)(2,1)} %copy-done.9), custom_call_target="tpu_custom_call" | custom-call | flops 294912 | bytes 442368 | tf_op jit(solution)/shard_map/merge4/pallas_call | solution.py:287
  68.2 12.0 %collective-permute-start.10 = (bf16[32,1152]{1,0:T(8,128)(2,1)}, bf16[32,1152]{1,0:T(8,128)(2,1)S(1)}, u32[]{:S(2)}, u32[]{:S(2)}) collective-permute-start(bf16[32,1152]{1,0:T(8,128)(2,1)} %get-tuple-element.30), channel_id=1, source_target_pairs={{0,16},{4,20},{8,24},{12,28},{16,0},{20,4},{24,8},{28,12},{1,17},{... | collective-permute-start | bytes 221192 | tf_op jit(solution)/shard_map/ppermute | solution.py:348
  80.9 2.0 %merge4.2 = (bf16[32,1152]{1,0:T(8,128)(2,1)}, bf16[32,1152]{1,0:T(8,128)(2,1)}) custom-call(bf16[64,1152]{1,0:T(8,128)(2,1)} %get-tuple-element.21.a_ref, bf16[64,1152]{1,0:T(8,128)(2,1)} %copy-done.10), custom_call_target="tpu_custom_call" | custom-call | flops 294912 | bytes 442368 | tf_op jit(solution)/shard_map/merge4/pallas_call | solution.py:287
  82.8 1.5 %collective-permute-start.4 = (bf16[32,1152]{1,0:T(8,128)(2,1)}, bf16[32,1152]{1,0:T(8,128)(2,1)S(1)}, u32[]{:S(2)}, u32[]{:S(2)}) collective-permute-start(bf16[32,1152]{1,0:T(8,128)(2,1)} %get-tuple-element.24), channel_id=1, source_target_pairs={{0,16},{4,20},{8,24},{12,28},{16,0},{20,4},{24,8},{28,12},{1,17},{... | collective-permute-start | bytes 221192 | tf_op jit(solution)/shard_map/ppermute | solution.py:348
  84.9 1.8 %merge0.3.refs_4_ = bf16[32,1024]{1,0:T(8,128)(2,1)} custom-call(bf16[32,1152]{1,0:T(8,128)(2,1)} %get-tuple-element.29.a_ref, bf16[32,1152]{1,0:T(8,128)(2,1)} %copy-done.11), custom_call_target="tpu_custom_call" | custom-call | flops 147456 | bytes 221184 | tf_op jit(solution)/shard_map/merge0/pallas_call | solution.py:287
  86.7 2.1 %collective-permute-start.11 = (bf16[32,1024]{1,0:T(8,128)(2,1)}, bf16[32,1024]{1,0:T(8,128)(2,1)S(1)}, u32[]{:S(2)}, u32[]{:S(2)}) collective-permute-start(bf16[32,1024]{1,0:T(8,128)(2,1)} %merge0.3.refs_4_), channel_id=1, source_target_pairs={{0,16},{4,20},{8,24},{12,28},{16,0},{20,4},{24,8},{28,12},{1,17},{... | collective-permute-start | bytes 196616 | tf_op jit(solution)/shard_map/ppermute | solution.py:348
  88.9 1.3 %collective-permute-done.4.b_ref = bf16[32,1152]{1,0:T(8,128)(2,1)S(1)} collective-permute-done((bf16[32,1152]{1,0:T(8,128)(2,1)}, bf16[32,1152]{1,0:T(8,128)(2,1)S(1)}, u32[]{:S(2)}, u32[]{:S(2)}) %collective-permute-start.4) | collective-permute-done | bytes 73760 | tf_op jit(solution)/shard_map/ppermute | solution.py:348
  90.8 1.8 %merge0.2.refs_0_ = bf16[32,1024]{1,0:T(8,128)(2,1)} custom-call(bf16[32,1152]{1,0:T(8,128)(2,1)} %get-tuple-element.23.a_ref, bf16[32,1152]{1,0:T(8,128)(2,1)} %copy-done.12), custom_call_target="tpu_custom_call" | custom-call | flops 147456 | bytes 221184 | tf_op jit(solution)/shard_map/merge0/pallas_call | solution.py:287
  92.5 1.5 %collective-permute-done.11.refs_5_ = bf16[32,1024]{1,0:T(8,128)(2,1)S(1)} collective-permute-done((bf16[32,1024]{1,0:T(8,128)(2,1)}, bf16[32,1024]{1,0:T(8,128)(2,1)S(1)}, u32[]{:S(2)}, u32[]{:S(2)}) %collective-permute-start.11) | collective-permute-done | bytes 65568 | tf_op jit(solution)/shard_map/ppermute | solution.py:348
  94.1 0.8 pad_maximum_fusion.3
  94.9 1.4 %collective-permute-start.12 = (bf16[64,1024]{1,0:T(8,128)(2,1)S(1)}, bf16[64,1024]{1,0:T(8,128)(2,1)S(1)}, u32[]{:S(2)}, u32[]{:S(2)}) collective-permute-start(bf16[64,1024]{1,0:T(8,128)(2,1)S(1)} %pad_maximum_fusion.3), channel_id=1, source_target_pairs={{0,8},{4,12},{8,0},{12,4},{16,24},{20,28},{24,16},{28,20},{1,9},{5... | collective-permute-start | bytes 393224 | tf_op jit(solution)/shard_map/ppermute | solution.py:348
  96.3 1.7 %collective-permute-done.5.refs_1_ = bf16[32,1024]{1,0:T(8,128)(2,1)S(1)} collective-permute-done((bf16[32,1024]{1,0:T(8,128)(2,1)}, bf16[32,1024]{1,0:T(8,128)(2,1)S(1)}, u32[]{:S(2)}, u32[]{:S(2)}) %collective-permute-start.5) | collective-permute-done | bytes 65568 | tf_op jit(solution)/shard_map/ppermute | solution.py:348
  98.0 0.8 pad_maximum_fusion.2
  98.9 1.8 %collective-permute-done.12.refs_6_ = bf16[64,1024]{1,0:T(8,128)(2,1)S(1)} collective-permute-done((bf16[64,1024]{1,0:T(8,128)(2,1)S(1)}, bf16[64,1024]{1,0:T(8,128)(2,1)S(1)}, u32[]{:S(2)}, u32[]{:S(2)}) %collective-permute-start.12) | collective-permute-done | bytes 131104 | tf_op jit(solution)/shard_map/ppermute | solution.py:348
  100.8 0.9 pad_maximum_fusion.1
  101.7 1.6 %collective-permute-start.13 = (bf16[128,1024]{1,0:T(8,128)(2,1)S(1)}, bf16[128,1024]{1,0:T(8,128)(2,1)S(1)}, u32[]{:S(2)}, u32[]{:S(2)}) collective-permute-start(bf16[128,1024]{1,0:T(8,128)(2,1)S(1)} %pad_maximum_fusion.1), channel_id=1, source_target_pairs={{0,4},{4,0},{8,12},{12,8},{16,20},{20,16},{24,28},{28,24},{1,5},{5... | collective-permute-start | bytes 786440 | tf_op jit(solution)/shard_map/ppermute | solution.py:348
  103.9 0.9 pad_maximum_fusion
  104.8 1.5 %collective-permute-start.7 = (bf16[128,1024]{1,0:T(8,128)(2,1)S(1)}, bf16[128,1024]{1,0:T(8,128)(2,1)S(1)}, u32[]{:S(2)}, u32[]{:S(2)}) collective-permute-start(bf16[128,1024]{1,0:T(8,128)(2,1)S(1)} %pad_maximum_fusion), channel_id=1, source_target_pairs={{0,4},{4,0},{8,12},{12,8},{16,20},{20,16},{24,28},{28,24},{1,5},{5... | collective-permute-start | bytes 786440 | tf_op jit(solution)/shard_map/ppermute | solution.py:348
  106.3 3.2 %collective-permute-done.13.refs_7_ = bf16[128,1024]{1,0:T(8,128)(2,1)S(1)} collective-permute-done((bf16[128,1024]{1,0:T(8,128)(2,1)S(1)}, bf16[128,1024]{1,0:T(8,128)(2,1)S(1)}, u32[]{:S(2)}, u32[]{:S(2)}) %collective-permute-start.13) | collective-permute-done | bytes 262176 | tf_op jit(solution)/shard_map/ppermute | solution.py:348
  109.5 2.8 %collective-permute-done.7.refs_3_ = bf16[128,1024]{1,0:T(8,128)(2,1)S(1)} collective-permute-done((bf16[128,1024]{1,0:T(8,128)(2,1)S(1)}, bf16[128,1024]{1,0:T(8,128)(2,1)S(1)}, u32[]{:S(2)}, u32[]{:S(2)}) %collective-permute-start.7) | collective-permute-done | bytes 262176 | tf_op jit(solution)/shard_map/ppermute | solution.py:348
  112.3 2.2 %copy-done = bf16[2048,1024]{1,0:T(8,128)(2,1)S(1)} copy-done((bf16[2048,1024]{1,0:T(8,128)(2,1)S(1)}, bf16[2048,1024]{1,0:T(8,128)(2,1)}, u32[]{:S(2)}) %copy-start) | copy-done | bytes 4194328
  114.5 0.8 copy-done.1
  115.3 0.8 copy-done.2
  116.2 1.3 %project.1 = (f32[128,1024]{1,0:T(8,128)S(1)}, bf16[128,1024]{1,0:T(8,128)(2,1)S(1)}) custom-call(bf16[32,1024]{1,0:T(8,128)(2,1)S(1)} %copy-done.2, bf16[32,1024]{1,0:T(8,128)(2,1)S(1)} %collective-permute-done.5.refs_1_, bf16[64,1024]{1,0:T(8,128)(2,1)S(1)} %collective-permute-done.6.refs_2_, bf16[128,1024]{1,0:T(8,128)(2,1)S(1)} %collective-permute-done.7.refs_3_, ...), custom_call_target="tpu_custom_call" | custom-call | flops 1073741824 | bytes 4194304 | tf_op jit(solution)/shard_map/project/pallas_call | solution.py:334
  117.6 1.5 %collective-permute-done.14 = bf16[128,1024]{1,0:T(8,128)(2,1)S(1)} collective-permute-done((bf16[128,1024]{1,0:T(8,128)(2,1)S(1)}, bf16[128,1024]{1,0:T(8,128)(2,1)S(1)}, u32[]{:S(2)}, u32[]{:S(2)}) %collective-permute-start.14) | collective-permute-done | bytes 262176 | tf_op jit(solution)/shard_map/ppermute | solution.py:348
  119.2 1.6 %collective-permute-start.15 = (bf16[1,64,1024]{2,1,0:T(8,128)(2,1)S(1)}, bf16[1,64,1024]{2,1,0:T(8,128)(2,1)S(1)}, u32[]{:S(2)}, u32[]{:S(2)}) collective-permute-start(bf16[1,64,1024]{2,1,0:T(8,128)(2,1)S(1)} %fusion.1), channel_id=1, source_target_pairs={{0,2},{1,3},{2,0},{3,1},{4,6},{5,7},{6,4},{7,5},{8,10},{9,11},{10,... | collective-permute-start | bytes 393224 | tf_op jit(solution)/shard_map/ppermute | solution.py:348
  120.8 4.0 %collective-permute-done.15 = bf16[1,64,1024]{2,1,0:T(8,128)(2,1)S(1)} collective-permute-done((bf16[1,64,1024]{2,1,0:T(8,128)(2,1)S(1)}, bf16[1,64,1024]{2,1,0:T(8,128)(2,1)S(1)}, u32[]{:S(2)}, u32[]{:S(2)}) %collective-permute-start.15) | collective-permute-done | bytes 131104 | tf_op jit(solution)/shard_map/ppermute | solution.py:348
  124.8 0.7 fusion.2
  (60 shorter events, 6.6 us)
Async XLA Ops:
  0.0 20.3 %copy-start.5 = (s32[64]{0:T(128)S(1)}, s32[64]{0:T(128)}, u32[]{:S(2)}) copy-start(s32[64]{0:T(128)} %table_ref.3) | copy-start | bytes 772
  0.0 18.3 %copy-start.6 = (bf16[64,16,2,128]{3,2,1,0:T(2,128)(2,1)S(1)}, bf16[64,16,2,128]{3,2,1,0:T(2,128)(2,1)}, u32[]{:S(2)}) copy-start(bf16[64,16,2,128]{3,2,1,0:T(2,128)(2,1)} %param.9) | copy-start | bytes 1572868
  6.0 14.3 %collective-permute-start = (bf16[32,128]{1,0:T(8,128)(2,1)S(1)}, bf16[32,128]{1,0:T(8,128)(2,1)S(1)}, u32[]{:S(2)}, u32[]{:S(2)}) collective-permute-start(bf16[32,128]{1,0:T(8,128)(2,1)S(1)} %bitcast.74), channel_id=1, source_target_pairs={{0,4},{4,8},{8,12},{12,16},{16,20},{20,24},{24,28},{1,5},{5,9},{9,... | collective-permute-start | bytes 24584 | tf_op jit(solution)/shard_map/ppermute | solution.py:366
  10.9 9.5 %collective-permute-start.1 = (bf16[32,128]{1,0:T(8,128)(2,1)S(1)}, bf16[32,128]{1,0:T(8,128)(2,1)S(1)}, u32[]{:S(2)}, u32[]{:S(2)}) collective-permute-start(bf16[32,128]{1,0:T(8,128)(2,1)S(1)} %bitcast.73), channel_id=1, source_target_pairs={{4,0},{8,4},{12,8},{16,12},{20,16},{24,20},{28,24},{5,1},{9,5},{13... | collective-permute-start | bytes 24584 | tf_op jit(solution)/shard_map/ppermute | solution.py:367
  34.1 0.7 copy-start.4
  34.8 18.0 %collective-permute-start.8 = (bf16[128,1152]{1,0:T(8,128)(2,1)S(1)}, bf16[128,1152]{1,0:T(8,128)(2,1)S(1)}, u32[]{:S(2)}, u32[]{:S(2)}) collective-permute-start(bf16[128,1152]{1,0:T(8,128)(2,1)S(1)} %get-tuple-element.26), channel_id=1, source_target_pairs={{0,4},{4,0},{8,12},{12,8},{16,20},{20,16},{24,28},{28,24},{1,5},{5... | collective-permute-start | bytes 884744 | tf_op jit(solution)/shard_map/ppermute | solution.py:348
  52.1 0.7 copy-start.3
  52.8 8.1 %collective-permute-start.2 = (bf16[128,1152]{1,0:T(8,128)(2,1)}, bf16[128,1152]{1,0:T(8,128)(2,1)S(1)}, u32[]{:S(2)}, u32[]{:S(2)}) collective-permute-start(bf16[128,1152]{1,0:T(8,128)(2,1)} %get-tuple-element.20), channel_id=1, source_target_pairs={{0,4},{4,0},{8,12},{12,8},{16,20},{20,16},{24,28},{28,24},{1,5},{5... | collective-permute-start | bytes 884744 | tf_op jit(solution)/shard_map/ppermute | solution.py:348
  52.8 0.7 copy-start.7
  55.8 9.7 %collective-permute-start.9 = (bf16[64,1152]{1,0:T(8,128)(2,1)}, bf16[64,1152]{1,0:T(8,128)(2,1)S(1)}, u32[]{:S(2)}, u32[]{:S(2)}) collective-permute-start(bf16[64,1152]{1,0:T(8,128)(2,1)} %get-tuple-element.28), channel_id=1, source_target_pairs={{0,8},{4,12},{8,0},{12,4},{16,24},{20,28},{24,16},{28,20},{1,9},{5... | collective-permute-start | bytes 442376 | tf_op jit(solution)/shard_map/ppermute | solution.py:348
  60.9 0.7 copy-start.8
  64.0 16.2 %collective-permute-start.3 = (bf16[64,1152]{1,0:T(8,128)(2,1)}, bf16[64,1152]{1,0:T(8,128)(2,1)S(1)}, u32[]{:S(2)}, u32[]{:S(2)}) collective-permute-start(bf16[64,1152]{1,0:T(8,128)(2,1)} %get-tuple-element.22), channel_id=1, source_target_pairs={{0,8},{4,12},{8,0},{12,4},{16,24},{20,28},{24,16},{28,20},{1,9},{5... | collective-permute-start | bytes 442376 | tf_op jit(solution)/shard_map/ppermute | solution.py:348
  65.6 0.7 copy-start.9
  68.2 16.1 %collective-permute-start.10 = (bf16[32,1152]{1,0:T(8,128)(2,1)}, bf16[32,1152]{1,0:T(8,128)(2,1)S(1)}, u32[]{:S(2)}, u32[]{:S(2)}) collective-permute-start(bf16[32,1152]{1,0:T(8,128)(2,1)} %get-tuple-element.30), channel_id=1, source_target_pairs={{0,16},{4,20},{8,24},{12,28},{16,0},{20,4},{24,8},{28,12},{1,17},{... | collective-permute-start | bytes 221192 | tf_op jit(solution)/shard_map/ppermute | solution.py:348
  80.2 0.7 copy-start.10
  82.8 7.3 %collective-permute-start.4 = (bf16[32,1152]{1,0:T(8,128)(2,1)}, bf16[32,1152]{1,0:T(8,128)(2,1)S(1)}, u32[]{:S(2)}, u32[]{:S(2)}) collective-permute-start(bf16[32,1152]{1,0:T(8,128)(2,1)} %get-tuple-element.24), channel_id=1, source_target_pairs={{0,16},{4,20},{8,24},{12,28},{16,0},{20,4},{24,8},{28,12},{1,17},{... | collective-permute-start | bytes 221192 | tf_op jit(solution)/shard_map/ppermute | solution.py:348
  84.3 0.6 copy-start.11
  86.7 7.3 %collective-permute-start.11 = (bf16[32,1024]{1,0:T(8,128)(2,1)}, bf16[32,1024]{1,0:T(8,128)(2,1)S(1)}, u32[]{:S(2)}, u32[]{:S(2)}) collective-permute-start(bf16[32,1024]{1,0:T(8,128)(2,1)} %merge0.3.refs_4_), channel_id=1, source_target_pairs={{0,16},{4,20},{8,24},{12,28},{16,0},{20,4},{24,8},{28,12},{1,17},{... | collective-permute-start | bytes 196616 | tf_op jit(solution)/shard_map/ppermute | solution.py:348
  90.1 0.6 copy-start.12
  92.5 5.5 %collective-permute-start.5 = (bf16[32,1024]{1,0:T(8,128)(2,1)}, bf16[32,1024]{1,0:T(8,128)(2,1)S(1)}, u32[]{:S(2)}, u32[]{:S(2)}) collective-permute-start(bf16[32,1024]{1,0:T(8,128)(2,1)} %merge0.2.refs_0_), channel_id=1, source_target_pairs={{0,16},{4,20},{8,24},{12,28},{16,0},{20,4},{24,8},{28,12},{1,17},{... | collective-permute-start | bytes 196616 | tf_op jit(solution)/shard_map/ppermute | solution.py:348
  94.9 5.9 %collective-permute-start.12 = (bf16[64,1024]{1,0:T(8,128)(2,1)S(1)}, bf16[64,1024]{1,0:T(8,128)(2,1)S(1)}, u32[]{:S(2)}, u32[]{:S(2)}) collective-permute-start(bf16[64,1024]{1,0:T(8,128)(2,1)S(1)} %pad_maximum_fusion.3), channel_id=1, source_target_pairs={{0,8},{4,12},{8,0},{12,4},{16,24},{20,28},{24,16},{28,20},{1,9},{5... | collective-permute-start | bytes 393224 | tf_op jit(solution)/shard_map/ppermute | solution.py:348
  98.9 5.0 %collective-permute-start.6 = (bf16[64,1024]{1,0:T(8,128)(2,1)S(1)}, bf16[64,1024]{1,0:T(8,128)(2,1)S(1)}, u32[]{:S(2)}, u32[]{:S(2)}) collective-permute-start(bf16[64,1024]{1,0:T(8,128)(2,1)S(1)} %pad_maximum_fusion.2), channel_id=1, source_target_pairs={{0,8},{4,12},{8,0},{12,4},{16,24},{20,28},{24,16},{28,20},{1,9},{5... | collective-permute-start | bytes 393224 | tf_op jit(solution)/shard_map/ppermute | solution.py:348
  101.7 7.8 %collective-permute-start.13 = (bf16[128,1024]{1,0:T(8,128)(2,1)S(1)}, bf16[128,1024]{1,0:T(8,128)(2,1)S(1)}, u32[]{:S(2)}, u32[]{:S(2)}) collective-permute-start(bf16[128,1024]{1,0:T(8,128)(2,1)S(1)} %pad_maximum_fusion.1), channel_id=1, source_target_pairs={{0,4},{4,0},{8,12},{12,8},{16,20},{20,16},{24,28},{28,24},{1,5},{5... | collective-permute-start | bytes 786440 | tf_op jit(solution)/shard_map/ppermute | solution.py:348
  104.8 7.5 %collective-permute-start.7 = (bf16[128,1024]{1,0:T(8,128)(2,1)S(1)}, bf16[128,1024]{1,0:T(8,128)(2,1)S(1)}, u32[]{:S(2)}, u32[]{:S(2)}) collective-permute-start(bf16[128,1024]{1,0:T(8,128)(2,1)S(1)} %pad_maximum_fusion), channel_id=1, source_target_pairs={{0,4},{4,0},{8,12},{12,8},{16,20},{20,16},{24,28},{28,24},{1,5},{5... | collective-permute-start | bytes 786440 | tf_op jit(solution)/shard_map/ppermute | solution.py:348
  112.3 2.2 %copy-start = (bf16[2048,1024]{1,0:T(8,128)(2,1)S(1)}, bf16[2048,1024]{1,0:T(8,128)(2,1)}, u32[]{:S(2)}) copy-start(bf16[2048,1024]{1,0:T(8,128)(2,1)} %refs_8_.1) | copy-start | bytes 12582916
  114.5 0.8 copy-start.1
  115.3 0.8 copy-start.2
  117.5 1.6 %collective-permute-start.14 = (bf16[128,1024]{1,0:T(8,128)(2,1)S(1)}, bf16[128,1024]{1,0:T(8,128)(2,1)S(1)}, u32[]{:S(2)}, u32[]{:S(2)}) collective-permute-start(bf16[128,1024]{1,0:T(8,128)(2,1)S(1)} %get-tuple-element.32), channel_id=1, source_target_pairs={{0,1},{1,0},{2,3},{3,2},{4,5},{5,4},{6,7},{7,6},{8,9},{9,8},{10,11... | collective-permute-start | bytes 786440 | tf_op jit(solution)/shard_map/ppermute | solution.py:348
  119.2 5.6 %collective-permute-start.15 = (bf16[1,64,1024]{2,1,0:T(8,128)(2,1)S(1)}, bf16[1,64,1024]{2,1,0:T(8,128)(2,1)S(1)}, u32[]{:S(2)}, u32[]{:S(2)}) collective-permute-start(bf16[1,64,1024]{2,1,0:T(8,128)(2,1)S(1)} %fusion.1), channel_id=1, source_target_pairs={{0,2},{1,3},{2,0},{3,1},{4,6},{5,7},{6,4},{7,5},{8,10},{9,11},{10,... | collective-permute-start | bytes 393224 | tf_op jit(solution)/shard_map/ppermute | solution.py:348

commit v2 on v1

v2 whole, which is shorter than its diff:
```python
import functools
import math

import jax
import jax.numpy as jnp
from jax import lax
from jax.experimental import pallas as pl
from jax.experimental.pallas import tpu as pltpu
from jax.sharding import PartitionSpec as P

NEG = -1e30
BF = jnp.bfloat16
F32 = jnp.float32
LANES = 128
BAND = 32
HEAD_PAD = 272
TAIL_PAD = 416
VPAD = 128
LOG2E = 1.4426950408889634


def nt(a, b, **kw):
    return lax.dot_general(a, b, (((1,), (1,)), ((), ())), preferred_element_type=F32, **kw)


def iota(shape, dim):
    return lax.broadcasted_iota(jnp.int32, shape, dim)


def skew(x, shift):
    return pltpu.roll(x, shift, 1, stride=1, stride_axis=0)


def pack_stats(lse, heads):
    hi = lse.astype(BF).astype(F32)
    mid = (lse - hi).astype(BF).astype(F32)
    low = lse - hi - mid
    return hi + pltpu.roll(mid, heads, 1) + pltpu.roll(low, 2 * heads, 1)


def unpack_stats(x, heads):
    x = x.astype(F32)
    return x + pltpu.roll(x, LANES - heads, 1) + pltpu.roll(x, LANES - 2 * heads, 1)


def prepare_kernel(dims, table_ref, mix_ref, conv_ref, q_ref, k_ref, v_ref,
                   q2_ref, k2_ref, v2_ref, band_ref, *rest):
    rows, heads, kvs, pages, page, qtaps, ktaps = dims
    qhats, (q32, rows_sc, base_sc, *toeps) = rest[:kvs], rest[kvs:]
    pairs = heads // 2
    scale = LOG2E / math.sqrt(LANES)
    q32[...] = q_ref[...].reshape(rows * heads, LANES).astype(F32)
    for h in range(heads):
        q2_ref[:, h * LANES:(h + 1) * LANES] = q32[pl.ds(h, rows, stride=heads), :].astype(BF)
    conv = conv_ref[...]
    turned = jnp.swapaxes(conv, 0, 1)
    lane = iota((ktaps, LANES), 1)
    lane2 = iota((qtaps, LANES), 1) + iota((qtaps, LANES), 0)
    rows_all = []
    for h in range(heads):
        rows_all.append(sum(jnp.where(lane == BAND - a, conv[a][:, h:h + 1], 0.0) for a in range(qtaps)))
        base_sc[h] = sum(jnp.where(lane2 == 15 - b, turned[b][:, h:h + 1], 0.0) for b in range(ktaps))
    band_ref[...] = jnp.zeros_like(band_ref)
    for h in range(heads):
        for g in range(2):
            src = h // 2 * 2 + g
            band_ref[h, g * qtaps:(g + 1) * qtaps, :] = base_sc[src] * (mix_ref[g, h] * scale)
        rows_sc[h] = rows_all[h // 2 * 2] * (mix_ref[0, h] * scale) + pltpu.roll(
            rows_all[h // 2 * 2 + 1], 2 * BAND, 1) * (mix_ref[1, h] * scale)

    def make_queries(p, dst, head, toep):
        per = ktaps * BAND
        for h in range(2):
            for b in range(ktaps):
                t32 = skew(jnp.broadcast_to(rows_sc[2 * p + h, b:b + 1, :], (BAND, LANES)), 0)
                hi = t32.astype(BF)
                at = h * per + b * BAND
                toep[pl.ds(at, BAND), 0:LANES] = hi
                toep[pl.ds(at, BAND), LANES:] = (t32 - hi.astype(F32)).astype(BF)
        for t in range(rows // (2 * BAND)):
            r0 = t * 2 * BAND
            halves = []
            for g in range(2):
                where = pl.ds(pl.multiple_of((p * 2 + g) * LANES, LANES), LANES)
                two = q2_ref[pl.ds(r0, 2 * BAND), where]
                if t == 0:
                    one = jnp.concatenate([jnp.zeros((BAND, LANES), BF), two[:BAND]], axis=0)
                else:
                    one = q2_ref[pl.ds(r0 - BAND, 2 * BAND), where]
                halves.append(jnp.concatenate([one, two], axis=1))
            rhs = jnp.concatenate(halves + halves, axis=0)
            y = jnp.dot(toep[...], rhs, preferred_element_type=F32)
            for h in range(2):
                for b in range(ktaps):
                    for e in range(2):
                        at = h * per + b * BAND
                        dst[head + h, pl.ds(r0 + e * BAND, BAND), b * LANES:(b + 1) * LANES] = (
                            y[at:at + BAND, e * LANES:(e + 1) * LANES].astype(BF))

    for kv in range(kvs):
        each = pairs // kvs

        def body(i, c, kv=kv, each=each):
            for j, toep in enumerate(toeps):
                p = i * len(toeps) + j
                make_queries(kv * each + p, qhats[kv], 2 * p, toep)
            return c

        lax.fori_loop(0, each // len(toeps), body, 0)
    for p in range(pages):
        keys = k_ref[table_ref[p]].astype(F32)
        values = v_ref[table_ref[p]].astype(F32)
        for kv in range(kvs):
            k2_ref[kv, p * page:(p + 1) * page, :] = keys[:, kv, :]
            v2_ref[kv, p * page:(p + 1) * page, :] = values[:, kv, :]


def prepare(table, mix, conv, queries, keys, values):
    rows, heads, _ = queries.shape
    pages, page, kvs, _ = keys.shape
    qtaps, ktaps, _ = conv.shape
    smem = pl.BlockSpec(memory_space=pltpu.SMEM)
    vmem = pl.BlockSpec(memory_space=pltpu.VMEM)
    store = jax.ShapeDtypeStruct((kvs, pages * page, LANES), F32)
    toep = pltpu.VMEM((2 * ktaps * BAND, 2 * LANES), BF)
    return pl.pallas_call(
        functools.partial(prepare_kernel, (rows, heads, kvs, pages, page, qtaps, ktaps)),
        out_shape=(
            jax.ShapeDtypeStruct((rows, heads * LANES), BF),
            store,
            store,
            jax.ShapeDtypeStruct((heads, 16, LANES), F32),
        )
        + (jax.ShapeDtypeStruct((heads // kvs, rows, ktaps * LANES), BF),) * kvs,
        in_specs=[smem, smem] + [vmem] * 4,
        out_specs=(vmem,) * (4 + kvs),
        scratch_shapes=[
            pltpu.VMEM((rows * heads, LANES), F32),
            pltpu.VMEM((heads, ktaps, LANES), F32),
            pltpu.VMEM((heads, qtaps, LANES), F32),
            toep,
            toep,
        ],
        compiler_params=pltpu.CompilerParams(vmem_limit_bytes=26 * 2**20),
        cost_estimate=pl.CostEstimate(flops=heads * rows * ktaps * LANES * 256 * 2, bytes_accessed=16 * 2**20, transcendentals=0),
        name="prepare",
    )(table, mix, conv, queries, keys, values)


def attend_kernel(dims, kv, off_ref, qhat_ref, q_ref, k_ref, v_ref, left_ref, right_ref,
                  band_ref, keep_ref, send_ref,
                  kext, krot, kwrap, vext, khat, vhat, sa, sb, ca, cb, out, stat, rev, fsc, fst, msc):
    rows, heads, kvs, page, qtaps, ktaps, keys_here, split_bit = dims
    hk = heads // kvs
    pairs = hk // 2
    rim = (ktaps - 1) // 2
    nblk = keys_here // LANES
    base = HEAD_PAD
    seq = lax.axis_index("seq")
    diag = off_ref[0] - seq * keys_here
    has_diag = (diag >= 1 - rows) & (diag <= keys_here + 8)
    shift = jnp.where(has_diag, lax.rem(diag + 2 * LANES, LANES), 0)

    kext[pl.ds(0, base - page), :] = jnp.zeros((base - page, LANES), F32)
    kext[pl.ds(base + keys_here + page, TAIL_PAD - page), :] = jnp.zeros((TAIL_PAD - page, LANES), F32)
    kext[pl.ds(base - page, page), :] = left_ref[:, kv, :].astype(F32)
    kext[pl.ds(base + keys_here, page), :] = right_ref[:, kv, :].astype(F32)
    kext[pl.ds(base, keys_here), :] = k_ref[kv]
    vext[pl.ds(0, VPAD), :] = jnp.zeros((VPAD, LANES), F32)
    vext[pl.ds(VPAD + keys_here, VPAD), :] = jnp.zeros((VPAD, LANES), F32)
    vext[pl.ds(VPAD, keys_here), :] = v_ref[kv]
    krot[...] = kext[pl.ds(base - 8 + shift, keys_here + 16), :]
    kwrap[...] = kext[pl.ds(base - 8 - LANES + shift, LANES + 16), :]
    first = iota((LANES, LANES), 0) < LANES - shift
    for n in range(nblk):
        for b in range(ktaps):
            part = krot[pl.ds(n * LANES + 8 + b - rim, LANES), :]
            if n == nblk - 1:
                part = jnp.where(first, part, kwrap[pl.ds(8 + b - rim, LANES), :])
            khat[pl.ds(n * LANES, LANES), b * LANES:(b + 1) * LANES] = part.astype(BF)
        part = vext[pl.ds(VPAD + n * LANES + shift, LANES), :]
        if n == nblk - 1:
            part = jnp.where(first, part, vext[pl.ds(shift, LANES), :])
        vhat[pl.ds(n * LANES, LANES), 0:LANES] = part.astype(BF)
    vhat[:, LANES:] = jnp.ones((keys_here, LANES), BF)

    cols = 2 * LANES
    nwin = 3 * LANES
    lane = iota((LANES, LANES), 1)
    row = iota((LANES, LANES), 0)
    block0 = (diag + 2 * LANES - shift) // LANES - 2

    def q_cols(p, g):
        return pl.ds(pl.multiple_of(((kv * pairs + p) * 2 + g) * LANES, LANES), LANES)

    def scores(head, dst, n):
        dst[:, n * cols:(n + 1) * cols] = nt(qhat_ref[head], khat[pl.ds(n * cols, cols), :])

    def future_band(p):
        future = (lane >= 127 - 10) & (lane <= 126)
        for g in range(2):
            w = nt(q_ref[:, q_cols(p, g)], rev[...])
            for f in range(rows // LANES):
                sub = w[f * LANES:(f + 1) * LANES]
                near = skew(sub[:, (2 - f) * LANES:(3 - f) * LANES], 0)
                far = skew(sub[:, (1 - f) * LANES:(2 - f) * LANES], 0)
                both = jnp.where(row <= lane, near, far)
                fsc[g, pl.ds(8 + f * LANES, LANES), :] = jnp.where(future, both, 0.0)

    def stack_band():
        tiles = [None, None]
        for g in range(2):
            for a in range(qtaps):
                slot = qtaps * g + a
                part = pltpu.roll(fsc[g, pl.ds(8 - a, rows), :], (16 * slot + 16) % LANES, 1)
                i = slot // 8
                tiles[i] = part if tiles[i] is None else tiles[i] + part
        fst[:, 0:LANES] = tiles[0]
        fst[:, LANES:] = tiles[1]

    def correction(p, h, dst):
        taps = band_ref[kv * hk + p * 2 + h]
        for u in range(5, 15):
            msc[pl.ds(u, 16, stride=16), :] = pltpu.roll(taps, 21 - u, 1)
        m = msc[...]
        mhi = m.astype(BF)
        mlow = (m - mhi.astype(F32)).astype(BF)
        x = fst[...]
        xhi = x.astype(BF)
        xlow = (x - xhi.astype(F32)).astype(BF)
        wide = jnp.dot(xhi, jnp.concatenate([mhi, mlow], axis=1), preferred_element_type=F32)
        c = wide[:, :LANES] + wide[:, LANES:] + jnp.dot(xlow, mhi, preferred_element_type=F32)
        for f in range(rows // LANES):
            dst[pl.ds(f * LANES, LANES), :] = skew(c[f * LANES:(f + 1) * LANES], 112)

    def correct(s, corr):
        for f in range(rows // LANES):
            part = pl.ds(f * LANES, LANES)
            r = corr[part, :]
            for e in range(2):
                y = lane - row + (16 if e else -112)
                n = block0 - 1 + f + e
                low = jnp.where(n == -1, LANES - shift, 0)
                high = jnp.where(n == nblk - 1, LANES - shift, LANES)
                high = jnp.where((n >= -1) & (n < nblk), high, 0)
                at = jnp.where(n == -1, nblk - 1, jnp.clip(n, 0, nblk - 1))
                ok = (y >= 7) & (y <= 16) & (lane >= low) & (lane < high)
                where = (part, pl.ds(pl.multiple_of(at * LANES, LANES), LANES))
                s[where] = s[where] - jnp.where(ok, r, 0.0)

    def peak_of(masked, s, n, top):
        for m in range(n * cols // LANES, (n + 1) * cols // LANES):
            where = (slice(None), slice(m * LANES, (m + 1) * LANES))
            part = s[where]
            if masked:
                col = iota((1, LANES), 1) + (m * LANES + shift)
                if m == nblk - 1:
                    col = jnp.where(col >= keys_here, col - keys_here, col)
                part = jnp.where(col <= diag + iota((rows, 1), 0), part, NEG)
                s[where] = part
            top = part if top is None else jnp.maximum(top, part)
        return top

    def weigh(s, peak, n, acc):
        w = jnp.exp2(s[:, n * cols:(n + 1) * cols] - peak).astype(BF)
        o = jnp.dot(w, vhat[pl.ds(n * cols, cols), :], preferred_element_type=F32)
        return o if acc is None else acc + o

    def store(p, h, o, peak):
        total = o[:, LANES:]
        head = p * 2 + h
        out[:, pl.ds(pl.multiple_of(head * LANES, LANES), LANES)] = (o[:, :LANES] / total).astype(BF)
        stat[...] = jnp.where(iota((rows, LANES), 1) == head, peak + jnp.log2(total), stat[...])

    ncol = keys_here // cols

    def half_step(masked, p, h, more, ahead):
        s, corr = (sa, ca) if h == 0 else (sb, cb)
        s2 = sb if h == 0 else sa
        steps = [functools.partial(scores, 2 * p + h + 1, s2, n) for n in range(ncol)] if more else []

        def one():
            if steps:
                steps.pop(0)()

        one()
        if masked:
            correct(s, corr)
        top = None
        for n in range(ncol):
            top = peak_of(masked, s, n, top)
        peak = jnp.max(top, axis=1, keepdims=True)
        one()
        acc = None
        for n in range(ncol):
            acc = weigh(s, peak, n, acc)
            if n % 2:
                one()
        while steps:
            one()
        store(p, h, acc, peak)
        if masked and h == 0:
            correction(p, 1, cb)
            if ahead:
                future_band(p + 1)
        if masked and h == 1 and ahead:
            stack_band()
            correction(p + 1, 0, ca)

    def run(masked):
        if masked:
            win = kext[pl.ds(base + diag, nwin), :].astype(BF)
            flip = (iota((nwin, nwin), 0) + iota((nwin, nwin), 1) == nwin - 1).astype(F32).astype(BF)
            rev[...] = jnp.dot(flip, win, preferred_element_type=F32).astype(BF)
            fsc[:, 0:8, :] = jnp.zeros((2, 8, LANES), F32)
            msc[...] = jnp.zeros((2 * LANES, LANES), F32)
            future_band(0)
            stack_band()
            correction(0, 0, ca)
        for n in range(ncol):
            scores(0, sa, n)

        def body(p, c):
            half_step(masked, p, 0, True, True)
            half_step(masked, p, 1, True, True)
            return c

        if pairs > 1:
            lax.fori_loop(0, pairs - 1, body, 0)
        half_step(masked, pairs - 1, 0, True, False)
        half_step(masked, pairs - 1, 1, False, False)

    stat[...] = jnp.zeros((rows, LANES), F32)

    @pl.when(diag > keys_here + 8)
    def _():
        run(False)

    @pl.when(has_diag)
    def _():
        run(True)

    @pl.when(diag < 1 - rows)
    def _():
        out[...] = jnp.zeros_like(out)
        stat[...] = jnp.where(iota((rows, LANES), 1) < hk, NEG, 0.0)

    half = rows // 2
    side = lax.rem(seq // split_bit, 2)
    stats = pack_stats(stat[...], hk)
    stat[...] = stats
    for ref, part in ((keep_ref, side), (send_ref, 1 - side)):
        at = pl.multiple_of(part * half, half)
        ref[:, :hk * LANES] = out[pl.ds(at, half), :]
        ref[:, hk * LANES:] = stat[pl.ds(at, half), :].astype(BF)


def attend(kv, qtaps, offset, qhat, q2, k2, v2, left, right, band):
    hk, rows, depth = qhat.shape
    kvs, keys_here, _ = k2.shape
    heads = hk * kvs
    page = left.shape[0]
    ktaps = depth // LANES
    dims = (rows, heads, kvs, page, qtaps, ktaps, keys_here, 1)
    smem = pl.BlockSpec(memory_space=pltpu.SMEM)
    vmem = pl.BlockSpec(memory_space=pltpu.VMEM)
    width = hk * LANES + LANES
    shape = jax.ShapeDtypeStruct((rows // 2, width), BF)
    flops = 2 * hk * rows * keys_here * (ktaps + 2) * LANES
    return pl.pallas_call(
        functools.partial(attend_kernel, dims, kv),
        out_shape=(shape, shape),
        in_specs=[smem] + [vmem] * 7,
        out_specs=(vmem, vmem),
        scratch_shapes=[
            pltpu.VMEM((HEAD_PAD + keys_here + TAIL_PAD, LANES), F32),
            pltpu.VMEM((keys_here + 16, LANES), F32),
            pltpu.VMEM((LANES + 16, LANES), F32),
            pltpu.VMEM((keys_here + 2 * VPAD, LANES), F32),
            pltpu.VMEM((keys_here, ktaps * LANES), BF),
            pltpu.VMEM((keys_here, 2 * LANES), BF),
            pltpu.VMEM((rows, keys_here), F32),
            pltpu.VMEM((rows, keys_here), F32),
            pltpu.VMEM((rows, LANES), F32),
            pltpu.VMEM((rows, LANES), F32),
            pltpu.VMEM((rows, hk * LANES), BF),
            pltpu.VMEM((rows, LANES), F32),
            pltpu.VMEM((3 * LANES, LANES), BF),
            pltpu.VMEM((2, rows + 8, LANES), F32),
            pltpu.VMEM((rows, 2 * LANES), F32),
            pltpu.VMEM((2 * LANES, LANES), F32),
        ],
        compiler_params=pltpu.CompilerParams(vmem_limit_bytes=22 * 2**20),
        cost_estimate=pl.CostEstimate(flops=flops, bytes_accessed=4 * 2**20, transcendentals=hk * rows * keys_here),
        name=f"attend{kv}",
    )(offset, qhat, q2, k2, v2, left, right, band)


def edge_kernel(table_ref, keys_ref, first_ref, last_ref, sem):
    pages = keys_ref.shape[0]
    copies = [
        pltpu.make_async_copy(keys_ref.at[table_ref[p]], ref, sem.at[i])
        for i, (p, ref) in enumerate(((0, first_ref), (pages - 1, last_ref)))
    ]
    for c in copies:
        c.start()
    for c in copies:
        c.wait()


def edge_pages(table, keys):
    one = jax.ShapeDtypeStruct(keys.shape[1:], keys.dtype)
    vmem = pl.BlockSpec(memory_space=pltpu.VMEM)
    return pl.pallas_call(
        edge_kernel,
        out_shape=(one, one),
        in_specs=[pl.BlockSpec(memory_space=pltpu.SMEM), pl.BlockSpec(memory_space=pl.ANY)],
        out_specs=(vmem, vmem),
        scratch_shapes=[pltpu.SemaphoreType.DMA((2,))],
        compiler_params=pltpu.CompilerParams(vmem_limit_bytes=2**20),
        name="edges",
    )(table, keys)


def place_in(level):
    seq = lax.axis_index("seq")
    place = 0
    for bit in level:
        place = place * 2 + lax.rem(seq // bit, 2)
    return place


def mask_of(level, rel):
    return sum(bit for i, bit in enumerate(reversed(level)) if rel >> i & 1)


def merge_kernel(hk, came, level, *refs):
    ins, outs = refs[:came], refs[came:]
    wide = hk * LANES
    lses = [unpack_stats(r[:, wide:], hk) for r in ins]
    top = functools.reduce(jnp.maximum, lses)
    lse = top + jnp.log2(sum(jnp.exp2(x - top) for x in lses))
    weights = [jnp.exp2(x - lse) for x in lses]
    rows = ins[0].shape[0]
    target = outs[-1] if level else outs[0]
    for h in range(hk):
        cols = slice(h * LANES, (h + 1) * LANES)
        mixed = sum(r[:, cols].astype(F32) * w[:, h:h + 1] for r, w in zip(ins, weights))
        target[:, cols] = mixed.astype(target.dtype)
    if level:
        target[:, wide:] = pack_stats(jnp.where(iota((rows, LANES), 1) < hk, lse, 0.0), hk)
        parts = 1 << len(level)
        size = rows // parts
        place = place_in(level)
        for rel in range(parts):
            at = pl.multiple_of(jnp.bitwise_xor(place, rel) * size, size)
            outs[rel][...] = target[pl.ds(at, size), :].astype(BF)


def merge(parts, hk, level):
    rows, width = parts[0].shape
    vmem = pl.BlockSpec(memory_space=pltpu.VMEM)
    if level:
        count = 1 << len(level)
        shapes = (jax.ShapeDtypeStruct((rows // count, width), BF),) * count
        specs = (vmem,) * count
        scratch = [pltpu.VMEM((rows, width), F32)]
    else:
        shapes, specs, scratch = jax.ShapeDtypeStruct((rows, hk * LANES), BF), vmem, []
    return pl.pallas_call(
        functools.partial(merge_kernel, hk, len(parts), level),
        out_shape=shapes,
        in_specs=[vmem] * len(parts),
        out_specs=specs,
        scratch_shapes=scratch,
        compiler_params=pltpu.CompilerParams(vmem_limit_bytes=4 * 2**20),
        cost_estimate=pl.CostEstimate(flops=4 * rows * width, bytes_accessed=6 * rows * width, transcendentals=rows * LANES * 5),
        name=f"merge{len(parts)}",
    )(*parts)


def project_kernel(chunks, heads_axis, *refs):
    xs = refs[:-4]
    w_ref, keep_ref, send_ref, xbuf = refs[-4:]
    count = lax.axis_size("seq")
    mine = place_in([1 << i for i in range(count.bit_length() - 1)])
    rows = xbuf.shape[0]
    unit = rows // count
    per = len(xs) // chunks
    width = xs[0].shape[1]
    for c in range(chunks):
        cols = slice(c * width, (c + 1) * width)
        held = 0
        for x_ref in xs[c * per:(c + 1) * per]:
            for k in range(x_ref.shape[0] // unit):
                to = jnp.bitwise_xor(mine, held)
                xbuf[pl.ds(pl.multiple_of(to * unit, unit), unit), cols] = (
                    x_ref[pl.ds(k * unit, unit), :].astype(xbuf.dtype))
                held += 1
    y = jnp.dot(xbuf[...].astype(BF), w_ref[...], preferred_element_type=F32)
    core = lax.rem(lax.axis_index("head"), 2)
    block = rows // heads_axis
    for g in range(heads_axis // 2):
        even = y[(2 * g) * block:(2 * g + 1) * block]
        odd = y[(2 * g + 1) * block:(2 * g + 2) * block]
        keep_ref[pl.ds(g * block, block), :] = jnp.where(core == 0, even, odd)
        send_ref[pl.ds(g * block, block), :] = jnp.where(core == 0, odd, even).astype(BF)


def project(chunks, pieces, weight, rows):
    heads_axis = lax.axis_size("head")
    vmem = pl.BlockSpec(memory_space=pltpu.VMEM)
    depth, cols = weight.shape
    unit = rows // lax.axis_size("seq")
    return pl.pallas_call(
        functools.partial(project_kernel, chunks, heads_axis),
        out_shape=(jax.ShapeDtypeStruct((rows // 2, cols), F32), jax.ShapeDtypeStruct((rows // 2, cols), BF)),
        in_specs=[vmem] * (len(pieces) + 1),
        out_specs=(vmem, vmem),
        scratch_shapes=[pltpu.VMEM((rows, depth), BF if unit % 16 == 0 else F32)],
        compiler_params=pltpu.CompilerParams(vmem_limit_bytes=12 * 2**20),
        cost_estimate=pl.CostEstimate(flops=2 * rows * depth * cols, bytes_accessed=2 * depth * cols, transcendentals=0),
        name="project",
    )(*pieces, weight)


def swap(x, axis, bit):
    count = lax.axis_size(axis)
    return lax.ppermute(x, axis, [(i, i ^ bit) for i in range(count)])


def per_device(queries, keys, values, page_table, offset, conv_kernel, head_mix, out_weight):
    rows, heads, head_dim = queries.shape
    pages, page, kvs, _ = keys.shape
    hk = heads // kvs
    seq_count = lax.axis_size("seq")
    head_count = lax.axis_size("head")

    ends = seq_count - 1

    first, last = edge_pages(page_table, keys)
    left = lax.ppermute(last, "seq", [(i, i + 1) for i in range(ends)])
    right = lax.ppermute(first, "seq", [(i + 1, i) for i in range(ends)])

    q2, k2, v2, band, *qhats = prepare(
        page_table, head_mix.T, jnp.transpose(conv_kernel, (1, 2, 0)), queries, keys, values)

    bits = [1 << i for i in range(seq_count.bit_length() - 1)]
    levels = [bits[:1]] + [bits[i:i + 2] for i in range(1, len(bits), 2)]
    pieces = []
    for kv in range(kvs):
        parts = attend(kv, conv_kernel.shape[1], offset, qhats[kv], q2, k2, v2, left, right, band)
        for i, level in enumerate(levels):
            got = [swap(x, "seq", mask_of(level, rel)) for rel, x in enumerate(parts) if rel]
            parts = merge([parts[0], *got], hk, levels[i + 1] if i + 1 < len(levels) else None)
        held = [parts]
        for level in reversed(levels):
            whole = held[0] if len(held) == 1 else jnp.concatenate(held, axis=0)
            held += [swap(whole, "seq", mask_of(level, rel)) for rel in range(1, 1 << len(level))]
        pieces += held

    keep, send = project(kvs, pieces, out_weight, rows)
    me = lax.axis_index("head")
    got = swap(send, "head", 1)
    total = keep + got.astype(F32)
    block = rows // head_count
    bit = 2
    while bit < head_count:
        parts = total.reshape(-1, 2, block, total.shape[1])
        high = (me // bit) % 2 == 1
        mine = jnp.where(high, parts[:, 1], parts[:, 0])
        other = jnp.where(high, parts[:, 0], parts[:, 1]).astype(BF)
        got = swap(other, "head", bit)
        total = (mine + got.astype(F32)).reshape(-1, total.shape[1])
        bit *= 2
    return total.astype(BF)


def solution(mesh):
    placed = (
        P(None, "head", None),
        P("seq", None, "head", None),
        P("seq", None, "head", None),
        P("seq"),
        P(),
        P("head", None, None),
        P("head", None),
        P("head", "seq"),
    )
    return jax.shard_map(
        per_device, mesh=mesh, in_specs=placed, out_specs=P("head", "seq"), check_vma=False
    )
```

time: 126 us -> 96.3 us (0.76)
  Pallas kernels: 41.9 us -> 31.8 us
  local copies, waits for them, and re-layouts: 16.7 us -> 7.13 us
  waiting for transfers between devices: 20.7 us -> 14.9 us
  starting transfers between devices: 35.1 us -> 40.7 us
  other arithmetic: 6.28 us -> 0.82 us
  between operations: 4.77 us -> 0.84 us
    pallas_call x2, Pallas kernels: 28.4 us -> 20.3 us  [attend(): pl.pallas_call(functools.partial(attend_kernel, dims, kv), out_shape=(sha...]
    ppermute x14 -> x18, waiting for transfers between devices: 20.7 us -> 14.9 us  [swap(): return lax.ppermute(x, axis, [(i, i ^ bit) for i in range(count)])]
    ppermute x14 -> x18, starting transfers between devices: 29 us -> 34.5 us  [swap(): return lax.ppermute(x, axis, [(i, i ^ bit) for i in range(count)])]
    unnamed x33 -> x17, local copies, waits for them, and re-layouts: 12.1 us -> 7.13 us
    concatenate x4 -> x2, other arithmetic: 3.41 us -> 0.04 us  [per_device(): whole = held[0] if len(held) == 1 else jnp.concatenate(held, axis=0)]
    slice x12 -> x0, local copies, waits for them, and re-layouts: 2.6 us -> none  [the longest x1 1.43 us: page_of(): page_table[p]]
    pallas_call x7, Pallas kernels: 13.5 us -> 11.5 us  [the longest x1 7.89 us: prepare(): pl.pallas_call(functools.partial(prepare_kernel, (rows, heads, kvs, pages...]
  transfers between devices with their start and end apart: 16 -> 20, of which waited for: 10 -> 9; matrix products, arithmetic and copies ran while one was open for 9% -> 1% of each run, Pallas kernels for 21% -> 21%
where the time goes in v2:
time: 96.3 us; the launch traced here: 96.2 us
  starting transfers between devices  40.7 us (42%)
  Pallas kernels  31.8 us (33%)
  waiting for transfers between devices  14.9 us (15%)
  local copies, waits for them, and re-layouts  7.13 us (7%)
    ppermute x18, starting transfers between devices, swap(): return lax.ppermute(x, axis, [(i, i ^ bit) for i in range(count)])  34.5 us
    pallas_call x2, Pallas kernels, attend(): pl.pallas_call(functools.partial(attend_kernel, dims, kv), out_shape=(sha...  20.3 us
    ppermute x18, waiting for transfers between devices, swap(): return lax.ppermute(x, axis, [(i, i ^ bit) for i in range(count)])  14.9 us
    pallas_call x1, Pallas kernels, prepare(): pl.pallas_call(functools.partial(prepare_kernel, (rows, heads, kvs, pages...  7.89 us
    unnamed x17, local copies, waits for them, and re-layouts  7.13 us
    ppermute x1, starting transfers between devices, per_device(): left = lax.ppermute(last, 'seq', [(i, i + 1) for i in range(ends)])  4.87 us
  transfers between devices with their start and end apart: 20, of which 9 were waited for; matrix products, arithmetic and copies ran while one was open for 1% of the time, Pallas kernels for 21%

profile of v2, /device:TPU:0, one launch (start us, length us, event | category | flops | bytes accessed | tf_op | source)
XLA Modules:
  0.0 96.2 jit_solution(12536472893719420923)
XLA Ops:
  0.0 1.0 %copy-done.1 = bf16[64,16,2,128]{3,2,1,0:T(2,128)(2,1)S(1)} copy-done((bf16[64,16,2,128]{3,2,1,0:T(2,128)(2,1)S(1)}, bf16[64,16,2,128]{3,2,1,0:T(2,128)(2,1)}, u32[]{:S(2)}) %copy-start.1) | copy-done | bytes 524312
  1.0 0.7 copy-done.3
  1.7 0.6 edges.1
  2.3 4.9 %collective-permute-start = (bf16[16,2,128]{2,1,0:T(2,128)(2,1)S(1)}, bf16[16,2,128]{2,1,0:T(2,128)(2,1)S(1)}, u32[]{:S(2)}, u32[]{:S(2)}) collective-permute-start(bf16[16,2,128]{2,1,0:T(2,128)(2,1)S(1)} %get-tuple-element.31), channel_id=1, source_target_pairs={{0,4},{4,8},{8,12},{12,16},{16,20},{20,24},{24,28},{1,5},{5,9},{9,... | collective-permute-start | bytes 24584 | tf_op jit(solution)/shard_map/ppermute | solution.py:542
  7.2 1.3 %collective-permute-start.1 = (bf16[16,2,128]{2,1,0:T(2,128)(2,1)S(1)}, bf16[16,2,128]{2,1,0:T(2,128)(2,1)S(1)}, u32[]{:S(2)}, u32[]{:S(2)}) collective-permute-start(bf16[16,2,128]{2,1,0:T(2,128)(2,1)S(1)} %get-tuple-element.32), channel_id=1, source_target_pairs={{4,0},{8,4},{12,8},{16,12},{20,16},{24,20},{28,24},{5,1},{9,5},{13... | collective-permute-start | bytes 24584 | tf_op jit(solution)/shard_map/ppermute | solution.py:543
  8.5 0.8 copy.11
  9.3 1.0 %copy-done.2 = bf16[64,16,2,128]{3,2,1,0:T(2,128)(2,1)S(1)} copy-done((bf16[64,16,2,128]{3,2,1,0:T(2,128)(2,1)S(1)}, bf16[64,16,2,128]{3,2,1,0:T(2,128)(2,1)}, u32[]{:S(2)}) %copy-start.2) | copy-done | bytes 524312
  10.3 0.7 copy-done.4
  11.0 1.2 %copy-done.5 = bf16[256,16,128]{2,1,0:T(8,128)(2,1)S(1)} copy-done((bf16[256,16,128]{2,1,0:T(8,128)(2,1)S(1)}, bf16[256,16,128]{2,1,0:T(8,128)(2,1)}, u32[]{:S(2)}) %copy-start.5) | copy-done | bytes 1048600
  12.2 1.0 %copy-done.6 = bf16[64,16,2,128]{3,2,1,0:T(2,128)(2,1)S(1)} copy-done((bf16[64,16,2,128]{3,2,1,0:T(2,128)(2,1)S(1)}, bf16[64,16,2,128]{3,2,1,0:T(2,128)(2,1)}, u32[]{:S(2)}) %copy-start.6) | copy-done | bytes 524312
  13.2 0.7 copy-done.7
  13.9 7.9 %prepare.1 = (bf16[256,2048]{1,0:T(8,128)(2,1)S(1)}, f32[2,1024,128]{2,1,0:T(8,128)S(1)}, f32[2,1024,128]{2,1,0:T(8,128)S(1)}, f32[16,16,128]{2,1,0:T(8,128)S(1)...) custom-call(s32[64]{0:T(128)S(1)} %copy-done.4, f32[2,16]{1,0:T(2,128)S(1)} %bitcast.16, ...), custom_call_target="tpu_custom_call" | custom-call | flops 2952790016 | bytes 16777216 | tf_op jit(solution)/shard_map/prepare/pallas_call | solution.py:126
  22.5 10.0 %attend1.1 = (bf16[128,1152]{1,0:T(8,128)(2,1)S(1)}, bf16[128,1152]{1,0:T(8,128)(2,1)S(1)}) custom-call(s32[1]{0:T(128)S(6)} %copy.12.off_ref, bf16[8,256,1408]{2,1,0:T(8,128)(2,1)S(1)} %get-tuple-element.40.qhat_ref, bf16[256,2048]{1,0:T(8,128)(2,1)S(1)} %get-tuple-element.28.q_ref, f32[2,1024,128]{2,1,0:T(8,128)S(1)} %get-tuple-element.29.k_ref, ...), custom_call_target="tpu_custom_call" | custom-call | flops 6979321856 | bytes 4194304 | tf_op jit(solution)/shard_map/attend1/pallas_call | solution.py:370
  32.5 2.7 %collective-permute-start.10 = (bf16[128,1152]{1,0:T(8,128)(2,1)S(1)}, bf16[128,1152]{1,0:T(8,128)(2,1)S(1)}, u32[]{:S(2)}, u32[]{:S(2)}) collective-permute-start(bf16[128,1152]{1,0:T(8,128)(2,1)S(1)} %get-tuple-element.42), channel_id=1, source_target_pairs={{0,4},{4,0},{8,12},{12,8},{16,20},{20,16},{24,28},{28,24},{1,5},{5... | collective-permute-start | bytes 884744 | tf_op jit(solution)/shard_map/ppermute | solution.py:529
  35.2 10.3 %attend0.1 = (bf16[128,1152]{1,0:T(8,128)(2,1)S(1)}, bf16[128,1152]{1,0:T(8,128)(2,1)S(1)}) custom-call(s32[1]{0:T(128)S(6)} %copy.12.off_ref, bf16[8,256,1408]{2,1,0:T(8,128)(2,1)S(1)} %get-tuple-element.27.qhat_ref, bf16[256,2048]{1,0:T(8,128)(2,1)S(1)} %get-tuple-element.28.q_ref, f32[2,1024,128]{2,1,0:T(8,128)S(1)} %get-tuple-element.29.k_ref, ...), custom_call_target="tpu_custom_call" | custom-call | flops 6979321856 | bytes 4194304 | tf_op jit(solution)/shard_map/attend0/pallas_call | solution.py:370
  45.5 0.1 collective-permute-start.2
  45.6 0.5 merge2.3
  46.1 4.0 %collective-permute-start.11 = (bf16[32,1152]{1,0:T(8,128)(2,1)S(1)}, bf16[32,1152]{1,0:T(8,128)(2,1)S(1)}, u32[]{:S(2)}, u32[]{:S(2)}) collective-permute-start(bf16[32,1152]{1,0:T(8,128)(2,1)S(1)} %get-tuple-element.44), channel_id=1, source_target_pairs={{0,16},{4,20},{8,24},{12,28},{16,0},{20,4},{24,8},{28,12},{1,17},{... | collective-permute-start | bytes 221192 | tf_op jit(solution)/shard_map/ppermute | solution.py:529
  50.2 5.8 %collective-permute-start.12 = (bf16[32,1152]{1,0:T(8,128)(2,1)S(1)}, bf16[32,1152]{1,0:T(8,128)(2,1)S(1)}, u32[]{:S(2)}, u32[]{:S(2)}) collective-permute-start(bf16[32,1152]{1,0:T(8,128)(2,1)S(1)} %get-tuple-element.45), channel_id=1, source_target_pairs={{0,8},{4,12},{8,0},{12,4},{16,24},{20,28},{24,16},{28,20},{1,9},{5... | collective-permute-start | bytes 221192 | tf_op jit(solution)/shard_map/ppermute | solution.py:529
  56.0 0.0 collective-permute-start.13
  56.0 0.0 collective-permute-done.2.refs_1_
  56.0 0.5 merge2.2
  56.5 1.5 %collective-permute-start.3 = (bf16[32,1152]{1,0:T(8,128)(2,1)S(1)}, bf16[32,1152]{1,0:T(8,128)(2,1)S(1)}, u32[]{:S(2)}, u32[]{:S(2)}) collective-permute-start(bf16[32,1152]{1,0:T(8,128)(2,1)S(1)} %get-tuple-element.37), channel_id=1, source_target_pairs={{0,16},{4,20},{8,24},{12,28},{16,0},{20,4},{24,8},{28,12},{1,17},{... | collective-permute-start | bytes 221192 | tf_op jit(solution)/shard_map/ppermute | solution.py:529
  58.0 6.1 %collective-permute-start.4 = (bf16[32,1152]{1,0:T(8,128)(2,1)S(1)}, bf16[32,1152]{1,0:T(8,128)(2,1)S(1)}, u32[]{:S(2)}, u32[]{:S(2)}) collective-permute-start(bf16[32,1152]{1,0:T(8,128)(2,1)S(1)} %get-tuple-element.38), channel_id=1, source_target_pairs={{0,8},{4,12},{8,0},{12,4},{16,24},{20,28},{24,16},{28,20},{1,9},{5... | collective-permute-start | bytes 221192 | tf_op jit(solution)/shard_map/ppermute | solution.py:529
  64.1 0.0 collective-permute-done.13.refs_3_
  64.1 0.3 merge4.3.refs_5_
  64.5 1.5 %collective-permute-start.14 = (bf16[32,1024]{1,0:T(8,128)(2,1)S(1)}, bf16[32,1024]{1,0:T(8,128)(2,1)S(1)}, u32[]{:S(2)}, u32[]{:S(2)}) collective-permute-start(bf16[32,1024]{1,0:T(8,128)(2,1)S(1)} %merge4.3.refs_5_), channel_id=1, source_target_pairs={{0,16},{4,20},{8,24},{12,28},{16,0},{20,4},{24,8},{28,12},{1,17},{... | collective-permute-start | bytes 196616 | tf_op jit(solution)/shard_map/ppermute | solution.py:529
  66.0 2.9 %collective-permute-start.15 = (bf16[32,1024]{1,0:T(8,128)(2,1)S(1)}, bf16[32,1024]{1,0:T(8,128)(2,1)S(1)}, u32[]{:S(2)}, u32[]{:S(2)}) collective-permute-start(bf16[32,1024]{1,0:T(8,128)(2,1)S(1)} %merge4.3.refs_5_), channel_id=1, source_target_pairs={{0,8},{4,12},{8,0},{12,4},{16,24},{20,28},{24,16},{28,20},{1,9},{5... | collective-permute-start | bytes 196616 | tf_op jit(solution)/shard_map/ppermute | solution.py:529
  68.9 1.0 %collective-permute-start.16 = (bf16[32,1024]{1,0:T(8,128)(2,1)S(1)}, bf16[32,1024]{1,0:T(8,128)(2,1)S(1)}, u32[]{:S(2)}, u32[]{:S(2)}) collective-permute-start(bf16[32,1024]{1,0:T(8,128)(2,1)S(1)} %merge4.3.refs_5_), channel_id=1, source_target_pairs={{0,24},{4,28},{8,16},{12,20},{16,8},{20,12},{24,0},{28,4},{1,25},{... | collective-permute-start | bytes 196616 | tf_op jit(solution)/shard_map/ppermute | solution.py:529
  70.0 0.5 collective-permute-done.5.refs_3_
  70.4 0.3 merge4.2.refs_0_
  70.7 3.1 %collective-permute-start.6 = (bf16[32,1024]{1,0:T(8,128)(2,1)S(1)}, bf16[32,1024]{1,0:T(8,128)(2,1)S(1)}, u32[]{:S(2)}, u32[]{:S(2)}) collective-permute-start(bf16[32,1024]{1,0:T(8,128)(2,1)S(1)} %merge4.2.refs_0_), channel_id=1, source_target_pairs={{0,16},{4,20},{8,24},{12,28},{16,0},{20,4},{24,8},{28,12},{1,17},{... | collective-permute-start | bytes 196616 | tf_op jit(solution)/shard_map/ppermute | solution.py:529
  73.9 0.1 collective-permute-done.14.refs_6_
  74.0 2.0 %collective-permute-start.8 = (bf16[32,1024]{1,0:T(8,128)(2,1)S(1)}, bf16[32,1024]{1,0:T(8,128)(2,1)S(1)}, u32[]{:S(2)}, u32[]{:S(2)}) collective-permute-start(bf16[32,1024]{1,0:T(8,128)(2,1)S(1)} %merge4.2.refs_0_), channel_id=1, source_target_pairs={{0,24},{4,28},{8,16},{12,20},{16,8},{20,12},{24,0},{28,4},{1,25},{... | collective-permute-start | bytes 196616 | tf_op jit(solution)/shard_map/ppermute | solution.py:529
  76.0 1.0 %collective-permute-start.17 = (bf16[128,1024]{1,0:T(8,128)(2,1)S(1)}, bf16[128,1024]{1,0:T(8,128)(2,1)S(1)}, u32[]{:S(2)}, u32[]{:S(2)}) collective-permute-start(bf16[128,1024]{1,0:T(8,128)(2,1)S(1)} %pad_maximum_fusion.1), channel_id=1, source_target_pairs={{0,4},{4,0},{8,12},{12,8},{16,20},{20,16},{24,28},{28,24},{1,5},{5... | collective-permute-start | bytes 786440 | tf_op jit(solution)/shard_map/ppermute | solution.py:529
  77.0 1.3 %collective-permute-done.6.refs_1_ = bf16[32,1024]{1,0:T(8,128)(2,1)S(1)} collective-permute-done((bf16[32,1024]{1,0:T(8,128)(2,1)S(1)}, bf16[32,1024]{1,0:T(8,128)(2,1)S(1)}, u32[]{:S(2)}, u32[]{:S(2)}) %collective-permute-start.6) | collective-permute-done | bytes 65568 | tf_op jit(solution)/shard_map/ppermute | solution.py:529
  78.3 0.3 collective-permute-done.7.refs_2_
  78.6 1.6 %collective-permute-done.8.refs_3_ = bf16[32,1024]{1,0:T(8,128)(2,1)S(1)} collective-permute-done((bf16[32,1024]{1,0:T(8,128)(2,1)S(1)}, bf16[32,1024]{1,0:T(8,128)(2,1)S(1)}, u32[]{:S(2)}, u32[]{:S(2)}) %collective-permute-start.8) | collective-permute-done | bytes 65568 | tf_op jit(solution)/shard_map/ppermute | solution.py:529
  80.2 1.1 %collective-permute-start.9 = (bf16[128,1024]{1,0:T(8,128)(2,1)S(1)}, bf16[128,1024]{1,0:T(8,128)(2,1)S(1)}, u32[]{:S(2)}, u32[]{:S(2)}) collective-permute-start(bf16[128,1024]{1,0:T(8,128)(2,1)S(1)} %pad_maximum_fusion), channel_id=1, source_target_pairs={{0,4},{4,0},{8,12},{12,8},{16,20},{20,16},{24,28},{28,24},{1,5},{5... | collective-permute-start | bytes 786440 | tf_op jit(solution)/shard_map/ppermute | solution.py:529
  81.3 2.8 %collective-permute-done.17.refs_9_ = bf16[128,1024]{1,0:T(8,128)(2,1)S(1)} collective-permute-done((bf16[128,1024]{1,0:T(8,128)(2,1)S(1)}, bf16[128,1024]{1,0:T(8,128)(2,1)S(1)}, u32[]{:S(2)}, u32[]{:S(2)}) %collective-permute-start.17) | collective-permute-done | bytes 262176 | tf_op jit(solution)/shard_map/ppermute | solution.py:529
  84.0 2.8 %collective-permute-done.9.refs_4_ = bf16[128,1024]{1,0:T(8,128)(2,1)S(1)} collective-permute-done((bf16[128,1024]{1,0:T(8,128)(2,1)S(1)}, bf16[128,1024]{1,0:T(8,128)(2,1)S(1)}, u32[]{:S(2)}, u32[]{:S(2)}) %collective-permute-start.9) | collective-permute-done | bytes 262176 | tf_op jit(solution)/shard_map/ppermute | solution.py:529
  86.8 1.3 %project.1 = (f32[128,1024]{1,0:T(8,128)S(1)}, bf16[128,1024]{1,0:T(8,128)(2,1)S(1)}) custom-call(bf16[32,1024]{1,0:T(8,128)(2,1)S(1)} %merge4.2.refs_0_, bf16[32,1024]{1,0:T(8,128)(2,1)S(1)} %collective-permute-done.6.refs_1_, bf16[32,1024]{1,0:T(8,128)(2,1)S(1)} %collective-permute-done.7.refs_2_, bf16[32,1024]{1,0:T(8,128)(2,1)S(1)} %collective-permute-done.8.refs_3_, ...), custom_call_target="tpu_custom_call" | custom-call | flops 1073741824 | bytes 4194304 | tf_op jit(solution)/shard_map/project/pallas_call | solution.py:515
  88.2 0.1 collective-permute-start.18
  88.3 1.5 %collective-permute-done.18 = bf16[128,1024]{1,0:T(8,128)(2,1)S(1)} collective-permute-done((bf16[128,1024]{1,0:T(8,128)(2,1)S(1)}, bf16[128,1024]{1,0:T(8,128)(2,1)S(1)}, u32[]{:S(2)}, u32[]{:S(2)}) %collective-permute-start.18) | collective-permute-done | bytes 262176 | tf_op jit(solution)/shard_map/ppermute | solution.py:529
  89.8 0.1 convert_add_fusion
  89.9 1.6 %collective-permute-start.19 = (bf16[1,64,1024]{2,1,0:T(8,128)(2,1)S(1)}, bf16[1,64,1024]{2,1,0:T(8,128)(2,1)S(1)}, u32[]{:S(2)}, u32[]{:S(2)}) collective-permute-start(bf16[1,64,1024]{2,1,0:T(8,128)(2,1)S(1)} %fusion.1), channel_id=1, source_target_pairs={{0,2},{1,3},{2,0},{3,1},{4,6},{5,7},{6,4},{7,5},{8,10},{9,11},{10,... | collective-permute-start | bytes 393224 | tf_op jit(solution)/shard_map/ppermute | solution.py:529
  91.4 4.0 %collective-permute-done.19 = bf16[1,64,1024]{2,1,0:T(8,128)(2,1)S(1)} collective-permute-done((bf16[1,64,1024]{2,1,0:T(8,128)(2,1)S(1)}, bf16[1,64,1024]{2,1,0:T(8,128)(2,1)S(1)}, u32[]{:S(2)}, u32[]{:S(2)}) %collective-permute-start.19) | collective-permute-done | bytes 131104 | tf_op jit(solution)/shard_map/ppermute | solution.py:529
  95.5 0.7 fusion.2
  (23 shorter events, 0.1 us)
Async XLA Ops:
  0.0 1.0 %copy-start.1 = (bf16[64,16,2,128]{3,2,1,0:T(2,128)(2,1)S(1)}, bf16[64,16,2,128]{3,2,1,0:T(2,128)(2,1)}, u32[]{:S(2)}) copy-start(bf16[64,16,2,128]{3,2,1,0:T(2,128)(2,1)} %keys_ref.1) | copy-start | bytes 1572868
  1.0 0.7 copy-start.3
  2.3 20.2 %collective-permute-start = (bf16[16,2,128]{2,1,0:T(2,128)(2,1)S(1)}, bf16[16,2,128]{2,1,0:T(2,128)(2,1)S(1)}, u32[]{:S(2)}, u32[]{:S(2)}) collective-permute-start(bf16[16,2,128]{2,1,0:T(2,128)(2,1)S(1)} %get-tuple-element.31), channel_id=1, source_target_pairs={{0,4},{4,8},{8,12},{12,16},{16,20},{20,24},{24,28},{1,5},{5,9},{9,... | collective-permute-start | bytes 24584 | tf_op jit(solution)/shard_map/ppermute | solution.py:542
  7.2 15.3 %collective-permute-start.1 = (bf16[16,2,128]{2,1,0:T(2,128)(2,1)S(1)}, bf16[16,2,128]{2,1,0:T(2,128)(2,1)S(1)}, u32[]{:S(2)}, u32[]{:S(2)}) collective-permute-start(bf16[16,2,128]{2,1,0:T(2,128)(2,1)S(1)} %get-tuple-element.32), channel_id=1, source_target_pairs={{4,0},{8,4},{12,8},{16,12},{20,16},{24,20},{28,24},{5,1},{9,5},{13... | collective-permute-start | bytes 24584 | tf_op jit(solution)/shard_map/ppermute | solution.py:543
  9.3 1.0 %copy-start.2 = (bf16[64,16,2,128]{3,2,1,0:T(2,128)(2,1)S(1)}, bf16[64,16,2,128]{3,2,1,0:T(2,128)(2,1)}, u32[]{:S(2)}) copy-start(bf16[64,16,2,128]{3,2,1,0:T(2,128)(2,1)} %keys_ref.1) | copy-start | bytes 1572868
  10.3 0.7 copy-start.4
  11.0 1.2 %copy-start.5 = (bf16[256,16,128]{2,1,0:T(8,128)(2,1)S(1)}, bf16[256,16,128]{2,1,0:T(8,128)(2,1)}, u32[]{:S(2)}) copy-start(bf16[256,16,128]{2,1,0:T(8,128)(2,1)} %q_ref.1) | copy-start | bytes 3145732
  12.2 1.0 %copy-start.6 = (bf16[64,16,2,128]{3,2,1,0:T(2,128)(2,1)S(1)}, bf16[64,16,2,128]{3,2,1,0:T(2,128)(2,1)}, u32[]{:S(2)}) copy-start(bf16[64,16,2,128]{3,2,1,0:T(2,128)(2,1)} %v_ref.1) | copy-start | bytes 1572868
  13.2 0.7 copy-start.7
  32.5 13.1 %collective-permute-start.10 = (bf16[128,1152]{1,0:T(8,128)(2,1)S(1)}, bf16[128,1152]{1,0:T(8,128)(2,1)S(1)}, u32[]{:S(2)}, u32[]{:S(2)}) collective-permute-start(bf16[128,1152]{1,0:T(8,128)(2,1)S(1)} %get-tuple-element.42), channel_id=1, source_target_pairs={{0,4},{4,0},{8,12},{12,8},{16,20},{20,16},{24,28},{28,24},{1,5},{5... | collective-permute-start | bytes 884744 | tf_op jit(solution)/shard_map/ppermute | solution.py:529
  35.2 51.6 %copy-start = (bf16[2048,1024]{1,0:T(8,128)(2,1)S(1)}, bf16[2048,1024]{1,0:T(8,128)(2,1)}, u32[]{:S(2)}) copy-start(bf16[2048,1024]{1,0:T(8,128)(2,1)} %refs_10_.1) | copy-start | bytes 12582916
  45.5 10.5 %collective-permute-start.2 = (bf16[128,1152]{1,0:T(8,128)(2,1)S(1)}, bf16[128,1152]{1,0:T(8,128)(2,1)S(1)}, u32[]{:S(2)}, u32[]{:S(2)}) collective-permute-start(bf16[128,1152]{1,0:T(8,128)(2,1)S(1)} %get-tuple-element.35), channel_id=1, source_target_pairs={{0,4},{4,0},{8,12},{12,8},{16,20},{20,16},{24,28},{28,24},{1,5},{5... | collective-permute-start | bytes 884744 | tf_op jit(solution)/shard_map/ppermute | solution.py:529
  46.1 18.0 %collective-permute-start.11 = (bf16[32,1152]{1,0:T(8,128)(2,1)S(1)}, bf16[32,1152]{1,0:T(8,128)(2,1)S(1)}, u32[]{:S(2)}, u32[]{:S(2)}) collective-permute-start(bf16[32,1152]{1,0:T(8,128)(2,1)S(1)} %get-tuple-element.44), channel_id=1, source_target_pairs={{0,16},{4,20},{8,24},{12,28},{16,0},{20,4},{24,8},{28,12},{1,17},{... | collective-permute-start | bytes 221192 | tf_op jit(solution)/shard_map/ppermute | solution.py:529
  50.2 14.0 %collective-permute-start.12 = (bf16[32,1152]{1,0:T(8,128)(2,1)S(1)}, bf16[32,1152]{1,0:T(8,128)(2,1)S(1)}, u32[]{:S(2)}, u32[]{:S(2)}) collective-permute-start(bf16[32,1152]{1,0:T(8,128)(2,1)S(1)} %get-tuple-element.45), channel_id=1, source_target_pairs={{0,8},{4,12},{8,0},{12,4},{16,24},{20,28},{24,16},{28,20},{1,9},{5... | collective-permute-start | bytes 221192 | tf_op jit(solution)/shard_map/ppermute | solution.py:529
  56.0 8.2 %collective-permute-start.13 = (bf16[32,1152]{1,0:T(8,128)(2,1)S(1)}, bf16[32,1152]{1,0:T(8,128)(2,1)S(1)}, u32[]{:S(2)}, u32[]{:S(2)}) collective-permute-start(bf16[32,1152]{1,0:T(8,128)(2,1)S(1)} %get-tuple-element.46), channel_id=1, source_target_pairs={{0,24},{4,28},{8,16},{12,20},{16,8},{20,12},{24,0},{28,4},{1,25},{... | collective-permute-start | bytes 221192 | tf_op jit(solution)/shard_map/ppermute | solution.py:529
  56.5 12.4 %collective-permute-start.3 = (bf16[32,1152]{1,0:T(8,128)(2,1)S(1)}, bf16[32,1152]{1,0:T(8,128)(2,1)S(1)}, u32[]{:S(2)}, u32[]{:S(2)}) collective-permute-start(bf16[32,1152]{1,0:T(8,128)(2,1)S(1)} %get-tuple-element.37), channel_id=1, source_target_pairs={{0,16},{4,20},{8,24},{12,28},{16,0},{20,4},{24,8},{28,12},{1,17},{... | collective-permute-start | bytes 221192 | tf_op jit(solution)/shard_map/ppermute | solution.py:529
  58.0 11.9 %collective-permute-start.4 = (bf16[32,1152]{1,0:T(8,128)(2,1)S(1)}, bf16[32,1152]{1,0:T(8,128)(2,1)S(1)}, u32[]{:S(2)}, u32[]{:S(2)}) collective-permute-start(bf16[32,1152]{1,0:T(8,128)(2,1)S(1)} %get-tuple-element.38), channel_id=1, source_target_pairs={{0,8},{4,12},{8,0},{12,4},{16,24},{20,28},{24,16},{28,20},{1,9},{5... | collective-permute-start | bytes 221192 | tf_op jit(solution)/shard_map/ppermute | solution.py:529
  64.1 6.3 %collective-permute-start.5 = (bf16[32,1152]{1,0:T(8,128)(2,1)S(1)}, bf16[32,1152]{1,0:T(8,128)(2,1)S(1)}, u32[]{:S(2)}, u32[]{:S(2)}) collective-permute-start(bf16[32,1152]{1,0:T(8,128)(2,1)S(1)} %get-tuple-element.39), channel_id=1, source_target_pairs={{0,24},{4,28},{8,16},{12,20},{16,8},{20,12},{24,0},{28,4},{1,25},{... | collective-permute-start | bytes 221192 | tf_op jit(solution)/shard_map/ppermute | solution.py:529
  64.5 9.5 %collective-permute-start.14 = (bf16[32,1024]{1,0:T(8,128)(2,1)S(1)}, bf16[32,1024]{1,0:T(8,128)(2,1)S(1)}, u32[]{:S(2)}, u32[]{:S(2)}) collective-permute-start(bf16[32,1024]{1,0:T(8,128)(2,1)S(1)} %merge4.3.refs_5_), channel_id=1, source_target_pairs={{0,16},{4,20},{8,24},{12,28},{16,0},{20,4},{24,8},{28,12},{1,17},{... | collective-permute-start | bytes 196616 | tf_op jit(solution)/shard_map/ppermute | solution.py:529
  66.0 10.0 %collective-permute-start.15 = (bf16[32,1024]{1,0:T(8,128)(2,1)S(1)}, bf16[32,1024]{1,0:T(8,128)(2,1)S(1)}, u32[]{:S(2)}, u32[]{:S(2)}) collective-permute-start(bf16[32,1024]{1,0:T(8,128)(2,1)S(1)} %merge4.3.refs_5_), channel_id=1, source_target_pairs={{0,8},{4,12},{8,0},{12,4},{16,24},{20,28},{24,16},{28,20},{1,9},{5... | collective-permute-start | bytes 196616 | tf_op jit(solution)/shard_map/ppermute | solution.py:529
  68.9 7.1 %collective-permute-start.16 = (bf16[32,1024]{1,0:T(8,128)(2,1)S(1)}, bf16[32,1024]{1,0:T(8,128)(2,1)S(1)}, u32[]{:S(2)}, u32[]{:S(2)}) collective-permute-start(bf16[32,1024]{1,0:T(8,128)(2,1)S(1)} %merge4.3.refs_5_), channel_id=1, source_target_pairs={{0,24},{4,28},{8,16},{12,20},{16,8},{20,12},{24,0},{28,4},{1,25},{... | collective-permute-start | bytes 196616 | tf_op jit(solution)/shard_map/ppermute | solution.py:529
  70.7 7.5 %collective-permute-start.6 = (bf16[32,1024]{1,0:T(8,128)(2,1)S(1)}, bf16[32,1024]{1,0:T(8,128)(2,1)S(1)}, u32[]{:S(2)}, u32[]{:S(2)}) collective-permute-start(bf16[32,1024]{1,0:T(8,128)(2,1)S(1)} %merge4.2.refs_0_), channel_id=1, source_target_pairs={{0,16},{4,20},{8,24},{12,28},{16,0},{20,4},{24,8},{28,12},{1,17},{... | collective-permute-start | bytes 196616 | tf_op jit(solution)/shard_map/ppermute | solution.py:529
  73.9 4.7 %collective-permute-start.7 = (bf16[32,1024]{1,0:T(8,128)(2,1)S(1)}, bf16[32,1024]{1,0:T(8,128)(2,1)S(1)}, u32[]{:S(2)}, u32[]{:S(2)}) collective-permute-start(bf16[32,1024]{1,0:T(8,128)(2,1)S(1)} %merge4.2.refs_0_), channel_id=1, source_target_pairs={{0,8},{4,12},{8,0},{12,4},{16,24},{20,28},{24,16},{28,20},{1,9},{5... | collective-permute-start | bytes 196616 | tf_op jit(solution)/shard_map/ppermute | solution.py:529
  74.0 6.2 %collective-permute-start.8 = (bf16[32,1024]{1,0:T(8,128)(2,1)S(1)}, bf16[32,1024]{1,0:T(8,128)(2,1)S(1)}, u32[]{:S(2)}, u32[]{:S(2)}) collective-permute-start(bf16[32,1024]{1,0:T(8,128)(2,1)S(1)} %merge4.2.refs_0_), channel_id=1, source_target_pairs={{0,24},{4,28},{8,16},{12,20},{16,8},{20,12},{24,0},{28,4},{1,25},{... | collective-permute-start | bytes 196616 | tf_op jit(solution)/shard_map/ppermute | solution.py:529
  76.0 8.0 %collective-permute-start.17 = (bf16[128,1024]{1,0:T(8,128)(2,1)S(1)}, bf16[128,1024]{1,0:T(8,128)(2,1)S(1)}, u32[]{:S(2)}, u32[]{:S(2)}) collective-permute-start(bf16[128,1024]{1,0:T(8,128)(2,1)S(1)} %pad_maximum_fusion.1), channel_id=1, source_target_pairs={{0,4},{4,0},{8,12},{12,8},{16,20},{20,16},{24,28},{28,24},{1,5},{5... | collective-permute-start | bytes 786440 | tf_op jit(solution)/shard_map/ppermute | solution.py:529
  80.2 6.6 %collective-permute-start.9 = (bf16[128,1024]{1,0:T(8,128)(2,1)S(1)}, bf16[128,1024]{1,0:T(8,128)(2,1)S(1)}, u32[]{:S(2)}, u32[]{:S(2)}) collective-permute-start(bf16[128,1024]{1,0:T(8,128)(2,1)S(1)} %pad_maximum_fusion), channel_id=1, source_target_pairs={{0,4},{4,0},{8,12},{12,8},{16,20},{20,16},{24,28},{28,24},{1,5},{5... | collective-permute-start | bytes 786440 | tf_op jit(solution)/shard_map/ppermute | solution.py:529
  88.2 1.6 %collective-permute-start.18 = (bf16[128,1024]{1,0:T(8,128)(2,1)S(1)}, bf16[128,1024]{1,0:T(8,128)(2,1)S(1)}, u32[]{:S(2)}, u32[]{:S(2)}) collective-permute-start(bf16[128,1024]{1,0:T(8,128)(2,1)S(1)} %get-tuple-element.48), channel_id=1, source_target_pairs={{0,1},{1,0},{2,3},{3,2},{4,5},{5,4},{6,7},{7,6},{8,9},{9,8},{10,11... | collective-permute-start | bytes 786440 | tf_op jit(solution)/shard_map/ppermute | solution.py:529
  89.9 5.6 %collective-permute-start.19 = (bf16[1,64,1024]{2,1,0:T(8,128)(2,1)S(1)}, bf16[1,64,1024]{2,1,0:T(8,128)(2,1)S(1)}, u32[]{:S(2)}, u32[]{:S(2)}) collective-permute-start(bf16[1,64,1024]{2,1,0:T(8,128)(2,1)S(1)} %fusion.1), channel_id=1, source_target_pairs={{0,2},{1,3},{2,0},{3,1},{4,6},{5,7},{6,4},{7,5},{8,10},{9,11},{10,... | collective-permute-start | bytes 393224 | tf_op jit(solution)/shard_map/ppermute | solution.py:529

commit v3 on v2

--- a/solution.py
+++ b/solution.py
@@ -43,17 +43,24 @@
     return x + pltpu.roll(x, LANES - heads, 1) + pltpu.roll(x, LANES - 2 * heads, 1)
 
 
-def prepare_kernel(dims, table_ref, mix_ref, conv_ref, q_ref, k_ref, v_ref,
+def prepare_kernel(dims, table_ref, mix_far, conv_far, q_far, k_far, v_far,
                    q2_ref, k2_ref, v2_ref, band_ref, *rest):
     rows, heads, kvs, pages, page, qtaps, ktaps = dims
-    qhats, (q32, rows_sc, base_sc, *toeps) = rest[:kvs], rest[kvs:]
+    qhats, rest = rest[:kvs], rest[kvs:]
+    (mix_ref, conv_ref, q_ref, k_ref, v_ref, sem, q32, rows_sc, base_sc, *toeps) = rest
+    copies = [
+        pltpu.make_async_copy(x, ref, sem.at[i])
+        for i, (x, ref) in enumerate(
+            zip((mix_far, conv_far, q_far, k_far, v_far), (mix_ref, conv_ref, q_ref, k_ref, v_ref)))
+    ]
+    for c in copies:
+        c.start()
     pairs = heads // 2
     scale = LOG2E / math.sqrt(LANES)
-    q32[...] = q_ref[...].reshape(rows * heads, LANES).astype(F32)
-    for h in range(heads):
-        q2_ref[:, h * LANES:(h + 1) * LANES] = q32[pl.ds(h, rows, stride=heads), :].astype(BF)
-    conv = conv_ref[...]
-    turned = jnp.swapaxes(conv, 0, 1)
+    copies[0].wait()
+    copies[1].wait()
+    turned = conv_ref[...]
+    conv = jnp.swapaxes(turned, 0, 1)
     lane = iota((ktaps, LANES), 1)
     lane2 = iota((qtaps, LANES), 1) + iota((qtaps, LANES), 0)
     rows_all = []
@@ -64,9 +71,14 @@
     for h in range(heads):
         for g in range(2):
             src = h // 2 * 2 + g
-            band_ref[h, g * qtaps:(g + 1) * qtaps, :] = base_sc[src] * (mix_ref[g, h] * scale)
-        rows_sc[h] = rows_all[h // 2 * 2] * (mix_ref[0, h] * scale) + pltpu.roll(
-            rows_all[h // 2 * 2 + 1], 2 * BAND, 1) * (mix_ref[1, h] * scale)
+            band_ref[h, g * qtaps:(g + 1) * qtaps, :] = base_sc[src] * (mix_ref[g:g + 1, h:h + 1] * scale)
+        rows_sc[h] = rows_all[h // 2 * 2] * (mix_ref[0:1, h:h + 1] * scale) + pltpu.roll(
+            rows_all[h // 2 * 2 + 1], 2 * BAND, 1) * (mix_ref[1:2, h:h + 1] * scale)
+
+    copies[2].wait()
+    q32[...] = q_ref[...].reshape(rows * heads, LANES).astype(F32)
+    for h in range(heads):
+        q2_ref[:, h * LANES:(h + 1) * LANES] = q32[pl.ds(h, rows, stride=heads), :].astype(BF)
 
     def make_queries(p, dst, head, toep):
         per = ktaps * BAND
@@ -107,6 +119,8 @@
             return c
 
         lax.fori_loop(0, each // len(toeps), body, 0)
+    copies[3].wait()
+    copies[4].wait()
     for p in range(pages):
         keys = k_ref[table_ref[p]].astype(F32)
         values = v_ref[table_ref[p]].astype(F32)
@@ -118,7 +132,7 @@
 def prepare(table, mix, conv, queries, keys, values):
     rows, heads, _ = queries.shape
     pages, page, kvs, _ = keys.shape
-    qtaps, ktaps, _ = conv.shape
+    ktaps, qtaps, _ = conv.shape
     smem = pl.BlockSpec(memory_space=pltpu.SMEM)
     vmem = pl.BlockSpec(memory_space=pltpu.VMEM)
     store = jax.ShapeDtypeStruct((kvs, pages * page, LANES), F32)
@@ -132,9 +146,15 @@
             jax.ShapeDtypeStruct((heads, 16, LANES), F32),
         )
         + (jax.ShapeDtypeStruct((heads // kvs, rows, ktaps * LANES), BF),) * kvs,
-        in_specs=[smem, smem] + [vmem] * 4,
+        in_specs=[smem] + [pl.BlockSpec(memory_space=pltpu.HBM)] * 5,
         out_specs=(vmem,) * (4 + kvs),
         scratch_shapes=[
+            pltpu.VMEM(mix.shape, F32),
+            pltpu.VMEM(conv.shape, F32),
+            pltpu.VMEM(queries.shape, BF),
+            pltpu.VMEM(keys.shape, BF),
+            pltpu.VMEM(values.shape, BF),
+            pltpu.SemaphoreType.DMA((5,)),
             pltpu.VMEM((rows * heads, LANES), F32),
             pltpu.VMEM((heads, ktaps, LANES), F32),
             pltpu.VMEM((heads, qtaps, LANES), F32),
@@ -414,10 +434,11 @@
     return pl.pallas_call(
         edge_kernel,
         out_shape=(one, one),
-        in_specs=[pl.BlockSpec(memory_space=pltpu.SMEM), pl.BlockSpec(memory_space=pl.ANY)],
+        in_specs=[pl.BlockSpec(memory_space=pltpu.SMEM), pl.BlockSpec(memory_space=pltpu.HBM)],
         out_specs=(vmem, vmem),
         scratch_shapes=[pltpu.SemaphoreType.DMA((2,))],
         compiler_params=pltpu.CompilerParams(vmem_limit_bytes=2**20),
+        cost_estimate=pl.CostEstimate(flops=2 * 10**10, bytes_accessed=2**20, transcendentals=0),
         name="edges",
     )(table, keys)
 
@@ -543,7 +564,7 @@
     right = lax.ppermute(first, "seq", [(i + 1, i) for i in range(ends)])
 
     q2, k2, v2, band, *qhats = prepare(
-        page_table, head_mix.T, jnp.transpose(conv_kernel, (1, 2, 0)), queries, keys, values)
+        page_table, head_mix.T, jnp.transpose(conv_kernel, (2, 1, 0)), queries, keys, values)
 
     bits = [1 << i for i in range(seq_count.bit_length() - 1)]
     levels = [bits[:1]] + [bits[i:i + 2] for i in range(1, len(bits), 2)]

time: 96.3 us -> 90.9 us (0.944)
  local copies, waits for them, and re-layouts: 7.13 us -> 1.81 us
    unnamed x17 -> x18, local copies, waits for them, and re-layouts: 7.13 us -> 1.81 us
  transfers between devices with their start and end apart: 20 -> 20, of which waited for: 9 -> 9; matrix products, arithmetic and copies ran while one was open for 1% -> 0% of each run, Pallas kernels for 21% -> 22%
where the time goes in v3:
time: 90.9 us; the launch traced here: 90.7 us
  starting transfers between devices  40.1 us (44%)
  Pallas kernels  32.1 us (35%)
  waiting for transfers between devices  14.9 us (16%)
  local copies, waits for them, and re-layouts  1.81 us (2%)
    ppermute x18, starting transfers between devices, swap(): return lax.ppermute(x, axis, [(i, i ^ bit) for i in range(count)])  34 us
    pallas_call x2, Pallas kernels, attend(): pl.pallas_call(functools.partial(attend_kernel, dims, kv), out_shape=(sha...  20.3 us
    ppermute x18, waiting for transfers between devices, swap(): return lax.ppermute(x, axis, [(i, i ^ bit) for i in range(count)])  14.9 us
    pallas_call x1, Pallas kernels, prepare(): pl.pallas_call(functools.partial(prepare_kernel, (rows, heads, kvs, pages...  8.2 us
    ppermute x1, starting transfers between devices, per_device(): left = lax.ppermute(last, 'seq', [(i, i + 1) for i in range(ends)])  4.87 us
  transfers between devices with their start and end apart: 20, of which 9 were waited for; matrix products, arithmetic and copies ran while one was open for 0% of the time, Pallas kernels for 22%

profile of v3, /device:TPU:0, one launch (start us, length us, event | category | flops | bytes accessed | tf_op | source)
XLA Modules:
  0.0 90.7 jit_solution(3647857472604123568)
XLA Ops:
  0.0 1.1 %copy-done.2 = bf16[64,16,2,128]{3,2,1,0:T(2,128)(2,1)S(1)} copy-done((bf16[64,16,2,128]{3,2,1,0:T(2,128)(2,1)S(1)}, bf16[64,16,2,128]{3,2,1,0:T(2,128)(2,1)}, u32[]{:S(2)}) %copy-start.2) | copy-done | bytes 524312
  1.1 0.7 copy-done.7
  1.8 0.6 edges.1
  2.4 4.9 %collective-permute-start = (bf16[16,2,128]{2,1,0:T(2,128)(2,1)S(1)}, bf16[16,2,128]{2,1,0:T(2,128)(2,1)S(1)}, u32[]{:S(2)}, u32[]{:S(2)}) collective-permute-start(bf16[16,2,128]{2,1,0:T(2,128)(2,1)S(1)} %get-tuple-element.31), channel_id=1, source_target_pairs={{0,4},{4,8},{8,12},{12,16},{16,20},{20,24},{24,28},{1,5},{5,9},{9,... | collective-permute-start | bytes 24584 | tf_op jit(solution)/shard_map/ppermute | solution.py:563
  7.3 1.3 %collective-permute-start.1 = (bf16[16,2,128]{2,1,0:T(2,128)(2,1)S(1)}, bf16[16,2,128]{2,1,0:T(2,128)(2,1)S(1)}, u32[]{:S(2)}, u32[]{:S(2)}) collective-permute-start(bf16[16,2,128]{2,1,0:T(2,128)(2,1)S(1)} %get-tuple-element.32), channel_id=1, source_target_pairs={{4,0},{8,4},{12,8},{16,12},{20,16},{24,20},{28,24},{5,1},{9,5},{13... | collective-permute-start | bytes 24584 | tf_op jit(solution)/shard_map/ppermute | solution.py:564
  8.6 8.2 %prepare.1 = (bf16[256,2048]{1,0:T(8,128)(2,1)S(1)}, f32[2,1024,128]{2,1,0:T(8,128)S(1)}, f32[2,1024,128]{2,1,0:T(8,128)S(1)}, f32[16,16,128]{2,1,0:T(8,128)S(1)...) custom-call(s32[64]{0:T(128)S(1)} %copy-done.8, f32[2,16]{1,0:T(2,128)S(1)} %bitcast.14, ...), custom_call_target="tpu_custom_call" | custom-call | flops 2952790016 | bytes 16777216 | tf_op jit(solution)/shard_map/prepare/pallas_call | solution.py:140
  17.5 0.0 collective-permute-done.left_ref
  17.5 0.0 collective-permute-done.1.right_ref
  17.5 10.0 %attend1.1 = (bf16[128,1152]{1,0:T(8,128)(2,1)S(1)}, bf16[128,1152]{1,0:T(8,128)(2,1)S(1)}) custom-call(s32[1]{0:T(128)S(6)} %copy.9.off_ref, bf16[8,256,1408]{2,1,0:T(8,128)(2,1)S(1)} %get-tuple-element.40.qhat_ref, bf16[256,2048]{1,0:T(8,128)(2,1)S(1)} %get-tuple-element.28.q_ref, f32[2,1024,128]{2,1,0:T(8,128)S(1)} %get-tuple-element.29.k_ref, ...), custom_call_target="tpu_custom_call" | custom-call | flops 6979321856 | bytes 4194304 | tf_op jit(solution)/shard_map/attend1/pallas_call | solution.py:390
  27.5 2.7 %collective-permute-start.10 = (bf16[128,1152]{1,0:T(8,128)(2,1)S(1)}, bf16[128,1152]{1,0:T(8,128)(2,1)S(1)}, u32[]{:S(2)}, u32[]{:S(2)}) collective-permute-start(bf16[128,1152]{1,0:T(8,128)(2,1)S(1)} %get-tuple-element.42), channel_id=1, source_target_pairs={{0,4},{4,0},{8,12},{12,8},{16,20},{20,16},{24,28},{28,24},{1,5},{5... | collective-permute-start | bytes 884744 | tf_op jit(solution)/shard_map/ppermute | solution.py:550
  30.2 10.3 %attend0.1 = (bf16[128,1152]{1,0:T(8,128)(2,1)S(1)}, bf16[128,1152]{1,0:T(8,128)(2,1)S(1)}) custom-call(s32[1]{0:T(128)S(6)} %copy.9.off_ref, bf16[8,256,1408]{2,1,0:T(8,128)(2,1)S(1)} %get-tuple-element.27.qhat_ref, bf16[256,2048]{1,0:T(8,128)(2,1)S(1)} %get-tuple-element.28.q_ref, f32[2,1024,128]{2,1,0:T(8,128)S(1)} %get-tuple-element.29.k_ref, ...), custom_call_target="tpu_custom_call" | custom-call | flops 6979321856 | bytes 4194304 | tf_op jit(solution)/shard_map/attend0/pallas_call | solution.py:390
  40.5 0.1 collective-permute-start.2
  40.6 0.0 collective-permute-done.10.refs_1_
  40.6 0.5 merge2.3
  41.2 8.8 %collective-permute-start.11 = (bf16[32,1152]{1,0:T(8,128)(2,1)S(1)}, bf16[32,1152]{1,0:T(8,128)(2,1)S(1)}, u32[]{:S(2)}, u32[]{:S(2)}) collective-permute-start(bf16[32,1152]{1,0:T(8,128)(2,1)S(1)} %get-tuple-element.44), channel_id=1, source_target_pairs={{0,16},{4,20},{8,24},{12,28},{16,0},{20,4},{24,8},{28,12},{1,17},{... | collective-permute-start | bytes 221192 | tf_op jit(solution)/shard_map/ppermute | solution.py:550
  50.0 0.0 collective-permute-start.12
  50.0 1.5 %collective-permute-start.13 = (bf16[32,1152]{1,0:T(8,128)(2,1)S(1)}, bf16[32,1152]{1,0:T(8,128)(2,1)S(1)}, u32[]{:S(2)}, u32[]{:S(2)}) collective-permute-start(bf16[32,1152]{1,0:T(8,128)(2,1)S(1)} %get-tuple-element.46), channel_id=1, source_target_pairs={{0,24},{4,28},{8,16},{12,20},{16,8},{20,12},{24,0},{28,4},{1,25},{... | collective-permute-start | bytes 221192 | tf_op jit(solution)/shard_map/ppermute | solution.py:550
  51.6 0.0 collective-permute-done.2.refs_1_
  51.6 0.5 merge2.2
  52.1 4.4 %collective-permute-start.3 = (bf16[32,1152]{1,0:T(8,128)(2,1)S(1)}, bf16[32,1152]{1,0:T(8,128)(2,1)S(1)}, u32[]{:S(2)}, u32[]{:S(2)}) collective-permute-start(bf16[32,1152]{1,0:T(8,128)(2,1)S(1)} %get-tuple-element.37), channel_id=1, source_target_pairs={{0,16},{4,20},{8,24},{12,28},{16,0},{20,4},{24,8},{28,12},{1,17},{... | collective-permute-start | bytes 221192 | tf_op jit(solution)/shard_map/ppermute | solution.py:550
  56.5 1.5 %collective-permute-start.5 = (bf16[32,1152]{1,0:T(8,128)(2,1)S(1)}, bf16[32,1152]{1,0:T(8,128)(2,1)S(1)}, u32[]{:S(2)}, u32[]{:S(2)}) collective-permute-start(bf16[32,1152]{1,0:T(8,128)(2,1)S(1)} %get-tuple-element.39), channel_id=1, source_target_pairs={{0,24},{4,28},{8,16},{12,20},{16,8},{20,12},{24,0},{28,4},{1,25},{... | collective-permute-start | bytes 221192 | tf_op jit(solution)/shard_map/ppermute | solution.py:550
  58.0 0.0 collective-permute-done.12.refs_2_
  58.0 0.0 collective-permute-done.13.refs_3_
  58.0 0.3 merge4.3.refs_5_
  58.3 2.0 %collective-permute-start.14 = (bf16[32,1024]{1,0:T(8,128)(2,1)S(1)}, bf16[32,1024]{1,0:T(8,128)(2,1)S(1)}, u32[]{:S(2)}, u32[]{:S(2)}) collective-permute-start(bf16[32,1024]{1,0:T(8,128)(2,1)S(1)} %merge4.3.refs_5_), channel_id=1, source_target_pairs={{0,16},{4,20},{8,24},{12,28},{16,0},{20,4},{24,8},{28,12},{1,17},{... | collective-permute-start | bytes 196616 | tf_op jit(solution)/shard_map/ppermute | solution.py:550
  60.4 0.9 collective-permute-start.15
  61.3 0.3 collective-permute-done.3.refs_1_
  61.6 1.2 %collective-permute-start.16 = (bf16[32,1024]{1,0:T(8,128)(2,1)S(1)}, bf16[32,1024]{1,0:T(8,128)(2,1)S(1)}, u32[]{:S(2)}, u32[]{:S(2)}) collective-permute-start(bf16[32,1024]{1,0:T(8,128)(2,1)S(1)} %merge4.3.refs_5_), channel_id=1, source_target_pairs={{0,24},{4,28},{8,16},{12,20},{16,8},{20,12},{24,0},{28,4},{1,25},{... | collective-permute-start | bytes 196616 | tf_op jit(solution)/shard_map/ppermute | solution.py:550
  62.8 0.2 collective-permute-done.4.refs_2_
  63.0 0.0 collective-permute-done.5.refs_3_
  63.0 0.3 merge4.2.refs_0_
  63.4 3.4 %collective-permute-start.6 = (bf16[32,1024]{1,0:T(8,128)(2,1)S(1)}, bf16[32,1024]{1,0:T(8,128)(2,1)S(1)}, u32[]{:S(2)}, u32[]{:S(2)}) collective-permute-start(bf16[32,1024]{1,0:T(8,128)(2,1)S(1)} %merge4.2.refs_0_), channel_id=1, source_target_pairs={{0,16},{4,20},{8,24},{12,28},{16,0},{20,4},{24,8},{28,12},{1,17},{... | collective-permute-start | bytes 196616 | tf_op jit(solution)/shard_map/ppermute | solution.py:550
  66.8 0.4 collective-permute-start.7
  67.2 1.0 %collective-permute-done.14.refs_6_ = bf16[32,1024]{1,0:T(8,128)(2,1)S(1)} collective-permute-done((bf16[32,1024]{1,0:T(8,128)(2,1)S(1)}, bf16[32,1024]{1,0:T(8,128)(2,1)S(1)}, u32[]{:S(2)}, u32[]{:S(2)}) %collective-permute-start.14) | collective-permute-done | bytes 65568 | tf_op jit(solution)/shard_map/ppermute | solution.py:550
  68.2 1.9 %collective-permute-start.8 = (bf16[32,1024]{1,0:T(8,128)(2,1)S(1)}, bf16[32,1024]{1,0:T(8,128)(2,1)S(1)}, u32[]{:S(2)}, u32[]{:S(2)}) collective-permute-start(bf16[32,1024]{1,0:T(8,128)(2,1)S(1)} %merge4.2.refs_0_), channel_id=1, source_target_pairs={{0,24},{4,28},{8,16},{12,20},{16,8},{20,12},{24,0},{28,4},{1,25},{... | collective-permute-start | bytes 196616 | tf_op jit(solution)/shard_map/ppermute | solution.py:550
  70.1 1.1 %collective-permute-start.17 = (bf16[128,1024]{1,0:T(8,128)(2,1)S(1)}, bf16[128,1024]{1,0:T(8,128)(2,1)S(1)}, u32[]{:S(2)}, u32[]{:S(2)}) collective-permute-start(bf16[128,1024]{1,0:T(8,128)(2,1)S(1)} %pad_maximum_fusion.1), channel_id=1, source_target_pairs={{0,4},{4,0},{8,12},{12,8},{16,20},{20,16},{24,28},{28,24},{1,5},{5... | collective-permute-start | bytes 786440 | tf_op jit(solution)/shard_map/ppermute | solution.py:550
  71.2 1.2 %collective-permute-done.6.refs_1_ = bf16[32,1024]{1,0:T(8,128)(2,1)S(1)} collective-permute-done((bf16[32,1024]{1,0:T(8,128)(2,1)S(1)}, bf16[32,1024]{1,0:T(8,128)(2,1)S(1)}, u32[]{:S(2)}, u32[]{:S(2)}) %collective-permute-start.6) | collective-permute-done | bytes 65568 | tf_op jit(solution)/shard_map/ppermute | solution.py:550
  72.4 1.8 %collective-permute-done.8.refs_3_ = bf16[32,1024]{1,0:T(8,128)(2,1)S(1)} collective-permute-done((bf16[32,1024]{1,0:T(8,128)(2,1)S(1)}, bf16[32,1024]{1,0:T(8,128)(2,1)S(1)}, u32[]{:S(2)}, u32[]{:S(2)}) %collective-permute-start.8) | collective-permute-done | bytes 65568 | tf_op jit(solution)/shard_map/ppermute | solution.py:550
  74.3 2.4 %collective-permute-start.9 = (bf16[128,1024]{1,0:T(8,128)(2,1)S(1)}, bf16[128,1024]{1,0:T(8,128)(2,1)S(1)}, u32[]{:S(2)}, u32[]{:S(2)}) collective-permute-start(bf16[128,1024]{1,0:T(8,128)(2,1)S(1)} %pad_maximum_fusion), channel_id=1, source_target_pairs={{0,4},{4,0},{8,12},{12,8},{16,20},{20,16},{24,28},{28,24},{1,5},{5... | collective-permute-start | bytes 786440 | tf_op jit(solution)/shard_map/ppermute | solution.py:550
  76.7 1.9 %collective-permute-done.17.refs_9_ = bf16[128,1024]{1,0:T(8,128)(2,1)S(1)} collective-permute-done((bf16[128,1024]{1,0:T(8,128)(2,1)S(1)}, bf16[128,1024]{1,0:T(8,128)(2,1)S(1)}, u32[]{:S(2)}, u32[]{:S(2)}) %collective-permute-start.17) | collective-permute-done | bytes 262176 | tf_op jit(solution)/shard_map/ppermute | solution.py:550
  78.6 2.8 %collective-permute-done.9.refs_4_ = bf16[128,1024]{1,0:T(8,128)(2,1)S(1)} collective-permute-done((bf16[128,1024]{1,0:T(8,128)(2,1)S(1)}, bf16[128,1024]{1,0:T(8,128)(2,1)S(1)}, u32[]{:S(2)}, u32[]{:S(2)}) %collective-permute-start.9) | collective-permute-done | bytes 262176 | tf_op jit(solution)/shard_map/ppermute | solution.py:550
  81.4 1.3 %project.1 = (f32[128,1024]{1,0:T(8,128)S(1)}, bf16[128,1024]{1,0:T(8,128)(2,1)S(1)}) custom-call(bf16[32,1024]{1,0:T(8,128)(2,1)S(1)} %merge4.2.refs_0_, bf16[32,1024]{1,0:T(8,128)(2,1)S(1)} %collective-permute-done.6.refs_1_, bf16[32,1024]{1,0:T(8,128)(2,1)S(1)} %collective-permute-done.7.refs_2_, bf16[32,1024]{1,0:T(8,128)(2,1)S(1)} %collective-permute-done.8.refs_3_, ...), custom_call_target="tpu_custom_call" | custom-call | flops 1073741824 | bytes 4194304 | tf_op jit(solution)/shard_map/project/pallas_call | solution.py:536
  82.7 0.1 collective-permute-start.18
  82.8 1.5 %collective-permute-done.18 = bf16[128,1024]{1,0:T(8,128)(2,1)S(1)} collective-permute-done((bf16[128,1024]{1,0:T(8,128)(2,1)S(1)}, bf16[128,1024]{1,0:T(8,128)(2,1)S(1)}, u32[]{:S(2)}, u32[]{:S(2)}) %collective-permute-start.18) | collective-permute-done | bytes 262176 | tf_op jit(solution)/shard_map/ppermute | solution.py:550
  84.3 0.1 convert_add_fusion
  84.4 1.5 %collective-permute-start.19 = (bf16[1,64,1024]{2,1,0:T(8,128)(2,1)S(1)}, bf16[1,64,1024]{2,1,0:T(8,128)(2,1)S(1)}, u32[]{:S(2)}, u32[]{:S(2)}) collective-permute-start(bf16[1,64,1024]{2,1,0:T(8,128)(2,1)S(1)} %fusion.1), channel_id=1, source_target_pairs={{0,2},{1,3},{2,0},{3,1},{4,6},{5,7},{6,4},{7,5},{8,10},{9,11},{10,... | collective-permute-start | bytes 393224 | tf_op jit(solution)/shard_map/ppermute | solution.py:550
  86.0 4.1 %collective-permute-done.19 = bf16[1,64,1024]{2,1,0:T(8,128)(2,1)S(1)} collective-permute-done((bf16[1,64,1024]{2,1,0:T(8,128)(2,1)S(1)}, bf16[1,64,1024]{2,1,0:T(8,128)(2,1)S(1)}, u32[]{:S(2)}, u32[]{:S(2)}) %collective-permute-start.19) | collective-permute-done | bytes 131104 | tf_op jit(solution)/shard_map/ppermute | solution.py:550
  90.0 0.7 fusion.2
  (24 shorter events, 0.1 us)
Async XLA Ops:
  0.0 8.6 %copy-start.1 = (bf16[256,16,128]{2,1,0:T(8,128)(2,1)S(1)}, bf16[256,16,128]{2,1,0:T(8,128)(2,1)}, u32[]{:S(2)}) copy-start(bf16[256,16,128]{2,1,0:T(8,128)(2,1)} %q_far.1) | copy-start | bytes 3145732
  0.0 1.1 %copy-start.2 = (bf16[64,16,2,128]{3,2,1,0:T(2,128)(2,1)S(1)}, bf16[64,16,2,128]{3,2,1,0:T(2,128)(2,1)}, u32[]{:S(2)}) copy-start(bf16[64,16,2,128]{3,2,1,0:T(2,128)(2,1)} %keys_ref.1) | copy-start | bytes 1572868
  1.1 0.7 copy-start.7
  1.8 6.8 %copy-start.3 = (bf16[64,16,2,128]{3,2,1,0:T(2,128)(2,1)S(1)}, bf16[64,16,2,128]{3,2,1,0:T(2,128)(2,1)}, u32[]{:S(2)}) copy-start(bf16[64,16,2,128]{3,2,1,0:T(2,128)(2,1)} %keys_ref.1) | copy-start | bytes 1572868
  1.8 6.8 %copy-start.4 = (bf16[64,16,2,128]{3,2,1,0:T(2,128)(2,1)S(1)}, bf16[64,16,2,128]{3,2,1,0:T(2,128)(2,1)}, u32[]{:S(2)}) copy-start(bf16[64,16,2,128]{3,2,1,0:T(2,128)(2,1)} %v_far.1) | copy-start | bytes 1572868
  1.8 6.8 %copy-start.5 = (f32[16,6,11]{0,1,2:T(8,128)S(1)}, f32[16,6,11]{0,1,2:T(8,128)}, u32[]{:S(2)}) copy-start(f32[16,6,11]{0,1,2:T(8,128)} %param.13) | copy-start | bytes 12676
  1.8 6.8 %copy-start.6 = (f32[16,2]{0,1:T(2,128)S(1)}, f32[16,2]{0,1:T(2,128)}, u32[]{:S(2)}) copy-start(f32[16,2]{0,1:T(2,128)} %param.14) | copy-start | bytes 388
  1.8 6.8 %copy-start.8 = (s32[64]{0:T(128)S(1)}, s32[64]{0:T(128)}, u32[]{:S(2)}) copy-start(s32[64]{0:T(128)} %table_ref.3) | copy-start | bytes 772
  2.4 15.1 %collective-permute-start = (bf16[16,2,128]{2,1,0:T(2,128)(2,1)S(1)}, bf16[16,2,128]{2,1,0:T(2,128)(2,1)S(1)}, u32[]{:S(2)}, u32[]{:S(2)}) collective-permute-start(bf16[16,2,128]{2,1,0:T(2,128)(2,1)S(1)} %get-tuple-element.31), channel_id=1, source_target_pairs={{0,4},{4,8},{8,12},{12,16},{16,20},{20,24},{24,28},{1,5},{5,9},{9,... | collective-permute-start | bytes 24584 | tf_op jit(solution)/shard_map/ppermute | solution.py:563
  7.3 10.2 %collective-permute-start.1 = (bf16[16,2,128]{2,1,0:T(2,128)(2,1)S(1)}, bf16[16,2,128]{2,1,0:T(2,128)(2,1)S(1)}, u32[]{:S(2)}, u32[]{:S(2)}) collective-permute-start(bf16[16,2,128]{2,1,0:T(2,128)(2,1)S(1)} %get-tuple-element.32), channel_id=1, source_target_pairs={{4,0},{8,4},{12,8},{16,12},{20,16},{24,20},{28,24},{5,1},{9,5},{13... | collective-permute-start | bytes 24584 | tf_op jit(solution)/shard_map/ppermute | solution.py:564
  27.5 13.1 %collective-permute-start.10 = (bf16[128,1152]{1,0:T(8,128)(2,1)S(1)}, bf16[128,1152]{1,0:T(8,128)(2,1)S(1)}, u32[]{:S(2)}, u32[]{:S(2)}) collective-permute-start(bf16[128,1152]{1,0:T(8,128)(2,1)S(1)} %get-tuple-element.42), channel_id=1, source_target_pairs={{0,4},{4,0},{8,12},{12,8},{16,20},{20,16},{24,28},{28,24},{1,5},{5... | collective-permute-start | bytes 884744 | tf_op jit(solution)/shard_map/ppermute | solution.py:550
  30.2 51.2 %copy-start = (bf16[2048,1024]{1,0:T(8,128)(2,1)S(1)}, bf16[2048,1024]{1,0:T(8,128)(2,1)}, u32[]{:S(2)}) copy-start(bf16[2048,1024]{1,0:T(8,128)(2,1)} %refs_10_.1) | copy-start | bytes 12582916
  40.5 11.0 %collective-permute-start.2 = (bf16[128,1152]{1,0:T(8,128)(2,1)S(1)}, bf16[128,1152]{1,0:T(8,128)(2,1)S(1)}, u32[]{:S(2)}, u32[]{:S(2)}) collective-permute-start(bf16[128,1152]{1,0:T(8,128)(2,1)S(1)} %get-tuple-element.35), channel_id=1, source_target_pairs={{0,4},{4,0},{8,12},{12,8},{16,20},{20,16},{24,28},{28,24},{1,5},{5... | collective-permute-start | bytes 884744 | tf_op jit(solution)/shard_map/ppermute | solution.py:550
  41.2 15.3 %collective-permute-start.11 = (bf16[32,1152]{1,0:T(8,128)(2,1)S(1)}, bf16[32,1152]{1,0:T(8,128)(2,1)S(1)}, u32[]{:S(2)}, u32[]{:S(2)}) collective-permute-start(bf16[32,1152]{1,0:T(8,128)(2,1)S(1)} %get-tuple-element.44), channel_id=1, source_target_pairs={{0,16},{4,20},{8,24},{12,28},{16,0},{20,4},{24,8},{28,12},{1,17},{... | collective-permute-start | bytes 221192 | tf_op jit(solution)/shard_map/ppermute | solution.py:550
  50.0 8.0 %collective-permute-start.12 = (bf16[32,1152]{1,0:T(8,128)(2,1)S(1)}, bf16[32,1152]{1,0:T(8,128)(2,1)S(1)}, u32[]{:S(2)}, u32[]{:S(2)}) collective-permute-start(bf16[32,1152]{1,0:T(8,128)(2,1)S(1)} %get-tuple-element.45), channel_id=1, source_target_pairs={{0,8},{4,12},{8,0},{12,4},{16,24},{20,28},{24,16},{28,20},{1,9},{5... | collective-permute-start | bytes 221192 | tf_op jit(solution)/shard_map/ppermute | solution.py:550
  50.0 8.0 %collective-permute-start.13 = (bf16[32,1152]{1,0:T(8,128)(2,1)S(1)}, bf16[32,1152]{1,0:T(8,128)(2,1)S(1)}, u32[]{:S(2)}, u32[]{:S(2)}) collective-permute-start(bf16[32,1152]{1,0:T(8,128)(2,1)S(1)} %get-tuple-element.46), channel_id=1, source_target_pairs={{0,24},{4,28},{8,16},{12,20},{16,8},{20,12},{24,0},{28,4},{1,25},{... | collective-permute-start | bytes 221192 | tf_op jit(solution)/shard_map/ppermute | solution.py:550
  52.1 9.5 %collective-permute-start.3 = (bf16[32,1152]{1,0:T(8,128)(2,1)S(1)}, bf16[32,1152]{1,0:T(8,128)(2,1)S(1)}, u32[]{:S(2)}, u32[]{:S(2)}) collective-permute-start(bf16[32,1152]{1,0:T(8,128)(2,1)S(1)} %get-tuple-element.37), channel_id=1, source_target_pairs={{0,16},{4,20},{8,24},{12,28},{16,0},{20,4},{24,8},{28,12},{1,17},{... | collective-permute-start | bytes 221192 | tf_op jit(solution)/shard_map/ppermute | solution.py:550
  56.5 6.5 %collective-permute-start.4 = (bf16[32,1152]{1,0:T(8,128)(2,1)S(1)}, bf16[32,1152]{1,0:T(8,128)(2,1)S(1)}, u32[]{:S(2)}, u32[]{:S(2)}) collective-permute-start(bf16[32,1152]{1,0:T(8,128)(2,1)S(1)} %get-tuple-element.38), channel_id=1, source_target_pairs={{0,8},{4,12},{8,0},{12,4},{16,24},{20,28},{24,16},{28,20},{1,9},{5... | collective-permute-start | bytes 221192 | tf_op jit(solution)/shard_map/ppermute | solution.py:550
  56.5 6.6 %collective-permute-start.5 = (bf16[32,1152]{1,0:T(8,128)(2,1)S(1)}, bf16[32,1152]{1,0:T(8,128)(2,1)S(1)}, u32[]{:S(2)}, u32[]{:S(2)}) collective-permute-start(bf16[32,1152]{1,0:T(8,128)(2,1)S(1)} %get-tuple-element.39), channel_id=1, source_target_pairs={{0,24},{4,28},{8,16},{12,20},{16,8},{20,12},{24,0},{28,4},{1,25},{... | collective-permute-start | bytes 221192 | tf_op jit(solution)/shard_map/ppermute | solution.py:550
  58.3 9.8 %collective-permute-start.14 = (bf16[32,1024]{1,0:T(8,128)(2,1)S(1)}, bf16[32,1024]{1,0:T(8,128)(2,1)S(1)}, u32[]{:S(2)}, u32[]{:S(2)}) collective-permute-start(bf16[32,1024]{1,0:T(8,128)(2,1)S(1)} %merge4.3.refs_5_), channel_id=1, source_target_pairs={{0,16},{4,20},{8,24},{12,28},{16,0},{20,4},{24,8},{28,12},{1,17},{... | collective-permute-start | bytes 196616 | tf_op jit(solution)/shard_map/ppermute | solution.py:550
  60.4 9.7 %collective-permute-start.15 = (bf16[32,1024]{1,0:T(8,128)(2,1)S(1)}, bf16[32,1024]{1,0:T(8,128)(2,1)S(1)}, u32[]{:S(2)}, u32[]{:S(2)}) collective-permute-start(bf16[32,1024]{1,0:T(8,128)(2,1)S(1)} %merge4.3.refs_5_), channel_id=1, source_target_pairs={{0,8},{4,12},{8,0},{12,4},{16,24},{20,28},{24,16},{28,20},{1,9},{5... | collective-permute-start | bytes 196616 | tf_op jit(solution)/shard_map/ppermute | solution.py:550
  61.6 8.5 %collective-permute-start.16 = (bf16[32,1024]{1,0:T(8,128)(2,1)S(1)}, bf16[32,1024]{1,0:T(8,128)(2,1)S(1)}, u32[]{:S(2)}, u32[]{:S(2)}) collective-permute-start(bf16[32,1024]{1,0:T(8,128)(2,1)S(1)} %merge4.3.refs_5_), channel_id=1, source_target_pairs={{0,24},{4,28},{8,16},{12,20},{16,8},{20,12},{24,0},{28,4},{1,25},{... | collective-permute-start | bytes 196616 | tf_op jit(solution)/shard_map/ppermute | solution.py:550
  63.4 9.0 %collective-permute-start.6 = (bf16[32,1024]{1,0:T(8,128)(2,1)S(1)}, bf16[32,1024]{1,0:T(8,128)(2,1)S(1)}, u32[]{:S(2)}, u32[]{:S(2)}) collective-permute-start(bf16[32,1024]{1,0:T(8,128)(2,1)S(1)} %merge4.2.refs_0_), channel_id=1, source_target_pairs={{0,16},{4,20},{8,24},{12,28},{16,0},{20,4},{24,8},{28,12},{1,17},{... | collective-permute-start | bytes 196616 | tf_op jit(solution)/shard_map/ppermute | solution.py:550
  66.8 5.6 %collective-permute-start.7 = (bf16[32,1024]{1,0:T(8,128)(2,1)S(1)}, bf16[32,1024]{1,0:T(8,128)(2,1)S(1)}, u32[]{:S(2)}, u32[]{:S(2)}) collective-permute-start(bf16[32,1024]{1,0:T(8,128)(2,1)S(1)} %merge4.2.refs_0_), channel_id=1, source_target_pairs={{0,8},{4,12},{8,0},{12,4},{16,24},{20,28},{24,16},{28,20},{1,9},{5... | collective-permute-start | bytes 196616 | tf_op jit(solution)/shard_map/ppermute | solution.py:550
  68.2 6.1 %collective-permute-start.8 = (bf16[32,1024]{1,0:T(8,128)(2,1)S(1)}, bf16[32,1024]{1,0:T(8,128)(2,1)S(1)}, u32[]{:S(2)}, u32[]{:S(2)}) collective-permute-start(bf16[32,1024]{1,0:T(8,128)(2,1)S(1)} %merge4.2.refs_0_), channel_id=1, source_target_pairs={{0,24},{4,28},{8,16},{12,20},{16,8},{20,12},{24,0},{28,4},{1,25},{... | collective-permute-start | bytes 196616 | tf_op jit(solution)/shard_map/ppermute | solution.py:550
  70.1 8.5 %collective-permute-start.17 = (bf16[128,1024]{1,0:T(8,128)(2,1)S(1)}, bf16[128,1024]{1,0:T(8,128)(2,1)S(1)}, u32[]{:S(2)}, u32[]{:S(2)}) collective-permute-start(bf16[128,1024]{1,0:T(8,128)(2,1)S(1)} %pad_maximum_fusion.1), channel_id=1, source_target_pairs={{0,4},{4,0},{8,12},{12,8},{16,20},{20,16},{24,28},{28,24},{1,5},{5... | collective-permute-start | bytes 786440 | tf_op jit(solution)/shard_map/ppermute | solution.py:550
  74.3 7.1 %collective-permute-start.9 = (bf16[128,1024]{1,0:T(8,128)(2,1)S(1)}, bf16[128,1024]{1,0:T(8,128)(2,1)S(1)}, u32[]{:S(2)}, u32[]{:S(2)}) collective-permute-start(bf16[128,1024]{1,0:T(8,128)(2,1)S(1)} %pad_maximum_fusion), channel_id=1, source_target_pairs={{0,4},{4,0},{8,12},{12,8},{16,20},{20,16},{24,28},{28,24},{1,5},{5... | collective-permute-start | bytes 786440 | tf_op jit(solution)/shard_map/ppermute | solution.py:550
  82.7 1.6 %collective-permute-start.18 = (bf16[128,1024]{1,0:T(8,128)(2,1)S(1)}, bf16[128,1024]{1,0:T(8,128)(2,1)S(1)}, u32[]{:S(2)}, u32[]{:S(2)}) collective-permute-start(bf16[128,1024]{1,0:T(8,128)(2,1)S(1)} %get-tuple-element.48), channel_id=1, source_target_pairs={{0,1},{1,0},{2,3},{3,2},{4,5},{5,4},{6,7},{7,6},{8,9},{9,8},{10,11... | collective-permute-start | bytes 786440 | tf_op jit(solution)/shard_map/ppermute | solution.py:550
  84.4 5.6 %collective-permute-start.19 = (bf16[1,64,1024]{2,1,0:T(8,128)(2,1)S(1)}, bf16[1,64,1024]{2,1,0:T(8,128)(2,1)S(1)}, u32[]{:S(2)}, u32[]{:S(2)}) collective-permute-start(bf16[1,64,1024]{2,1,0:T(8,128)(2,1)S(1)} %fusion.1), channel_id=1, source_target_pairs={{0,2},{1,3},{2,0},{3,1},{4,6},{5,7},{6,4},{7,5},{8,10},{9,11},{10,... | collective-permute-start | bytes 393224 | tf_op jit(solution)/shard_map/ppermute | solution.py:550

commit v4 on v3

--- a/solution.py
+++ b/solution.py
@@ -43,22 +43,13 @@
     return x + pltpu.roll(x, LANES - heads, 1) + pltpu.roll(x, LANES - 2 * heads, 1)
 
 
-def prepare_kernel(dims, table_ref, mix_far, conv_far, q_far, k_far, v_far,
+def prepare_kernel(dims, table_ref, mix_ref, conv_ref, q_ref, k_ref, v_ref,
                    q2_ref, k2_ref, v2_ref, band_ref, *rest):
     rows, heads, kvs, pages, page, qtaps, ktaps = dims
     qhats, rest = rest[:kvs], rest[kvs:]
-    (mix_ref, conv_ref, q_ref, k_ref, v_ref, sem, q32, rows_sc, base_sc, *toeps) = rest
-    copies = [
-        pltpu.make_async_copy(x, ref, sem.at[i])
-        for i, (x, ref) in enumerate(
-            zip((mix_far, conv_far, q_far, k_far, v_far), (mix_ref, conv_ref, q_ref, k_ref, v_ref)))
-    ]
-    for c in copies:
-        c.start()
+    q32, rows_sc, base_sc, *toeps = rest
     pairs = heads // 2
     scale = LOG2E / math.sqrt(LANES)
-    copies[0].wait()
-    copies[1].wait()
     turned = conv_ref[...]
     conv = jnp.swapaxes(turned, 0, 1)
     lane = iota((ktaps, LANES), 1)
@@ -75,7 +66,6 @@
         rows_sc[h] = rows_all[h // 2 * 2] * (mix_ref[0:1, h:h + 1] * scale) + pltpu.roll(
             rows_all[h // 2 * 2 + 1], 2 * BAND, 1) * (mix_ref[1:2, h:h + 1] * scale)
 
-    copies[2].wait()
     q32[...] = q_ref[...].reshape(rows * heads, LANES).astype(F32)
     for h in range(heads):
         q2_ref[:, h * LANES:(h + 1) * LANES] = q32[pl.ds(h, rows, stride=heads), :].astype(BF)
@@ -109,24 +99,16 @@
                         dst[head + h, pl.ds(r0 + e * BAND, BAND), b * LANES:(b + 1) * LANES] = (
                             y[at:at + BAND, e * LANES:(e + 1) * LANES].astype(BF))
 
-    for kv in range(kvs):
-        each = pairs // kvs
-
-        def body(i, c, kv=kv, each=each):
-            for j, toep in enumerate(toeps):
-                p = i * len(toeps) + j
-                make_queries(kv * each + p, qhats[kv], 2 * p, toep)
-            return c
-
-        lax.fori_loop(0, each // len(toeps), body, 0)
-    copies[3].wait()
-    copies[4].wait()
-    for p in range(pages):
-        keys = k_ref[table_ref[p]].astype(F32)
-        values = v_ref[table_ref[p]].astype(F32)
-        for kv in range(kvs):
-            k2_ref[kv, p * page:(p + 1) * page, :] = keys[:, kv, :]
-            v2_ref[kv, p * page:(p + 1) * page, :] = values[:, kv, :]
+    each = pairs // kvs
+    share = -(-pages // pairs)
+    for p in range(pairs):
+        make_queries(p, qhats[p // each], 2 * (p % each), toeps[p % len(toeps)])
+        for at in range(p * share, min(pages, (p + 1) * share)):
+            keys = k_ref[table_ref[at]].astype(F32)
+            values = v_ref[table_ref[at]].astype(F32)
+            for kv in range(kvs):
+                k2_ref[kv, at * page:(at + 1) * page, :] = keys[:, kv, :]
+                v2_ref[kv, at * page:(at + 1) * page, :] = values[:, kv, :]
 
 
 def prepare(table, mix, conv, queries, keys, values):
@@ -146,18 +128,13 @@
             jax.ShapeDtypeStruct((heads, 16, LANES), F32),
         )
         + (jax.ShapeDtypeStruct((heads // kvs, rows, ktaps * LANES), BF),) * kvs,
-        in_specs=[smem] + [pl.BlockSpec(memory_space=pltpu.HBM)] * 5,
+        in_specs=[smem] + [vmem] * 5,
         out_specs=(vmem,) * (4 + kvs),
         scratch_shapes=[
-            pltpu.VMEM(mix.shape, F32),
-            pltpu.VMEM(conv.shape, F32),
-            pltpu.VMEM(queries.shape, BF),
-            pltpu.VMEM(keys.shape, BF),
-            pltpu.VMEM(values.shape, BF),
-            pltpu.SemaphoreType.DMA((5,)),
             pltpu.VMEM((rows * heads, LANES), F32),
             pltpu.VMEM((heads, ktaps, LANES), F32),
             pltpu.VMEM((heads, qtaps, LANES), F32),
+            toep,
             toep,
             toep,
         ],
@@ -268,21 +245,27 @@
                 where = (part, pl.ds(pl.multiple_of(at * LANES, LANES), LANES))
                 s[where] = s[where] - jnp.where(ok, r, 0.0)
 
+    def masked_part(masked, s, m):
+        part = s[:, m * LANES:(m + 1) * LANES]
+        if not masked:
+            return part
+        col = iota((1, LANES), 1) + (m * LANES + shift)
+        if m == nblk - 1:
+            col = jnp.where(col >= keys_here, col - keys_here, col)
+        return jnp.where(col <= diag + iota((rows, 1), 0), part, NEG)
+
     def peak_of(masked, s, n, top):
         for m in range(n * cols // LANES, (n + 1) * cols // LANES):
-            where = (slice(None), slice(m * LANES, (m + 1) * LANES))
-            part = s[where]
-            if masked:
-                col = iota((1, LANES), 1) + (m * LANES + shift)
-                if m == nblk - 1:
-                    col = jnp.where(col >= keys_here, col - keys_here, col)
-                part = jnp.where(col <= diag + iota((rows, 1), 0), part, NEG)
-                s[where] = part
+            part = masked_part(masked, s, m)
             top = part if top is None else jnp.maximum(top, part)
         return top
 
-    def weigh(s, peak, n, acc):
-        w = jnp.exp2(s[:, n * cols:(n + 1) * cols] - peak).astype(BF)
+    def weigh(masked, s, peak, n, acc):
+        parts = [
+            jnp.exp2(masked_part(masked, s, m) - peak).astype(BF)
+            for m in range(n * cols // LANES, (n + 1) * cols // LANES)
+        ]
+        w = jnp.concatenate(parts, axis=1)
         o = jnp.dot(w, vhat[pl.ds(n * cols, cols), :], preferred_element_type=F32)
         return o if acc is None else acc + o
 
@@ -313,7 +296,7 @@
         one()
         acc = None
         for n in range(ncol):
-            acc = weigh(s, peak, n, acc)
+            acc = weigh(masked, s, peak, n, acc)
             if n % 2:
                 one()
         while steps:

time: 90.9 us -> 90.3 us (level)
  Pallas kernels: 32.1 us -> 30.7 us
  starting transfers between devices: 40.1 us -> 41.4 us
    pallas_call x1, Pallas kernels: 8.2 us -> 6.75 us  [prepare(): pl.pallas_call(functools.partial(prepare_kernel, (rows, heads, kvs, pages...]
    ppermute x18, starting transfers between devices: 34 us -> 35.3 us  [swap(): return lax.ppermute(x, axis, [(i, i ^ bit) for i in range(count)])]
  transfers between devices with their start and end apart: 20 -> 20, of which waited for: 9 -> 9; matrix products, arithmetic and copies ran while one was open for 0% -> 0% of each run, Pallas kernels for 22% -> 21%
where the time goes in v4:
time: 90.3 us
  starting transfers between devices  41.4 us (46%)
  Pallas kernels  30.7 us (34%)
  waiting for transfers between devices  14.6 us (16%)
  local copies, waits for them, and re-layouts  1.81 us (2%)
    ppermute x18, starting transfers between devices, swap(): return lax.ppermute(x, axis, [(i, i ^ bit) for i in range(count)])  35.3 us
    pallas_call x2, Pallas kernels, attend(): pl.pallas_call(functools.partial(attend_kernel, dims, kv), out_shape=(sha...  20.3 us
    ppermute x18, waiting for transfers between devices, swap(): return lax.ppermute(x, axis, [(i, i ^ bit) for i in range(count)])  14.6 us
    pallas_call x1, Pallas kernels, prepare(): pl.pallas_call(functools.partial(prepare_kernel, (rows, heads, kvs, pages...  6.75 us
    ppermute x1, starting transfers between devices, per_device(): left = lax.ppermute(last, 'seq', [(i, i + 1) for i in range(ends)])  4.87 us
    unnamed x18, local copies, waits for them, and re-layouts  1.81 us
  transfers between devices with their start and end apart: 20, of which 9 were waited for; matrix products, arithmetic and copies ran while one was open for 0% of the time, Pallas kernels for 21%

profile of v4, /device:TPU:0, one launch (start us, length us, event | category | flops | bytes accessed | tf_op | source)
XLA Modules:
  0.0 90.3 jit_solution(7353502012444147926)
XLA Ops:
  0.0 1.1 %copy-done.2 = bf16[64,16,2,128]{3,2,1,0:T(2,128)(2,1)S(1)} copy-done((bf16[64,16,2,128]{3,2,1,0:T(2,128)(2,1)S(1)}, bf16[64,16,2,128]{3,2,1,0:T(2,128)(2,1)}, u32[]{:S(2)}) %copy-start.2) | copy-done | bytes 524312
  1.1 0.7 copy-done.7
  1.8 0.6 edges.1
  2.4 4.9 %collective-permute-start = (bf16[16,2,128]{2,1,0:T(2,128)(2,1)S(1)}, bf16[16,2,128]{2,1,0:T(2,128)(2,1)S(1)}, u32[]{:S(2)}, u32[]{:S(2)}) collective-permute-start(bf16[16,2,128]{2,1,0:T(2,128)(2,1)S(1)} %get-tuple-element.31), channel_id=1, source_target_pairs={{0,4},{4,8},{8,12},{12,16},{16,20},{20,24},{24,28},{1,5},{5,9},{9,... | collective-permute-start | bytes 24584 | tf_op jit(solution)/shard_map/ppermute | solution.py:546
  7.3 1.3 %collective-permute-start.1 = (bf16[16,2,128]{2,1,0:T(2,128)(2,1)S(1)}, bf16[16,2,128]{2,1,0:T(2,128)(2,1)S(1)}, u32[]{:S(2)}, u32[]{:S(2)}) collective-permute-start(bf16[16,2,128]{2,1,0:T(2,128)(2,1)S(1)} %get-tuple-element.32), channel_id=1, source_target_pairs={{4,0},{8,4},{12,8},{16,12},{20,16},{24,20},{28,24},{5,1},{9,5},{13... | collective-permute-start | bytes 24584 | tf_op jit(solution)/shard_map/ppermute | solution.py:547
  8.6 6.7 %prepare.1 = (bf16[256,2048]{1,0:T(8,128)(2,1)S(1)}, f32[2,1024,128]{2,1,0:T(8,128)S(1)}, f32[2,1024,128]{2,1,0:T(8,128)S(1)}, f32[16,16,128]{2,1,0:T(8,128)S(1)...) custom-call(s32[64]{0:T(128)S(1)} %copy-done.8, f32[2,16]{1,0:T(2,128)S(1)} %bitcast.14, ...), custom_call_target="tpu_custom_call" | custom-call | flops 2952790016 | bytes 16777216 | tf_op jit(solution)/shard_map/prepare/pallas_call | solution.py:122
  16.0 0.0 collective-permute-done.left_ref
  16.1 0.0 collective-permute-done.1.right_ref
  16.1 10.0 %attend1.1 = (bf16[128,1152]{1,0:T(8,128)(2,1)S(1)}, bf16[128,1152]{1,0:T(8,128)(2,1)S(1)}) custom-call(s32[1]{0:T(128)S(6)} %copy.9.off_ref, bf16[8,256,1408]{2,1,0:T(8,128)(2,1)S(1)} %get-tuple-element.40.qhat_ref, bf16[256,2048]{1,0:T(8,128)(2,1)S(1)} %get-tuple-element.28.q_ref, f32[2,1024,128]{2,1,0:T(8,128)S(1)} %get-tuple-element.29.k_ref, ...), custom_call_target="tpu_custom_call" | custom-call | flops 6979321856 | bytes 4194304 | tf_op jit(solution)/shard_map/attend1/pallas_call | solution.py:373
  26.1 2.7 %collective-permute-start.10 = (bf16[128,1152]{1,0:T(8,128)(2,1)S(1)}, bf16[128,1152]{1,0:T(8,128)(2,1)S(1)}, u32[]{:S(2)}, u32[]{:S(2)}) collective-permute-start(bf16[128,1152]{1,0:T(8,128)(2,1)S(1)} %get-tuple-element.42), channel_id=1, source_target_pairs={{0,4},{4,0},{8,12},{12,8},{16,20},{20,16},{24,28},{28,24},{1,5},{5... | collective-permute-start | bytes 884744 | tf_op jit(solution)/shard_map/ppermute | solution.py:533
  28.8 10.3 %attend0.1 = (bf16[128,1152]{1,0:T(8,128)(2,1)S(1)}, bf16[128,1152]{1,0:T(8,128)(2,1)S(1)}) custom-call(s32[1]{0:T(128)S(6)} %copy.9.off_ref, bf16[8,256,1408]{2,1,0:T(8,128)(2,1)S(1)} %get-tuple-element.27.qhat_ref, bf16[256,2048]{1,0:T(8,128)(2,1)S(1)} %get-tuple-element.28.q_ref, f32[2,1024,128]{2,1,0:T(8,128)S(1)} %get-tuple-element.29.k_ref, ...), custom_call_target="tpu_custom_call" | custom-call | flops 6979321856 | bytes 4194304 | tf_op jit(solution)/shard_map/attend0/pallas_call | solution.py:373
  39.1 0.1 collective-permute-start.2
  39.2 0.0 collective-permute-done.10.refs_1_
  39.2 0.5 merge2.3
  39.7 4.0 %collective-permute-start.11 = (bf16[32,1152]{1,0:T(8,128)(2,1)S(1)}, bf16[32,1152]{1,0:T(8,128)(2,1)S(1)}, u32[]{:S(2)}, u32[]{:S(2)}) collective-permute-start(bf16[32,1152]{1,0:T(8,128)(2,1)S(1)} %get-tuple-element.44), channel_id=1, source_target_pairs={{0,16},{4,20},{8,24},{12,28},{16,0},{20,4},{24,8},{28,12},{1,17},{... | collective-permute-start | bytes 221192 | tf_op jit(solution)/shard_map/ppermute | solution.py:533
  43.8 7.7 %collective-permute-start.12 = (bf16[32,1152]{1,0:T(8,128)(2,1)S(1)}, bf16[32,1152]{1,0:T(8,128)(2,1)S(1)}, u32[]{:S(2)}, u32[]{:S(2)}) collective-permute-start(bf16[32,1152]{1,0:T(8,128)(2,1)S(1)} %get-tuple-element.45), channel_id=1, source_target_pairs={{0,8},{4,12},{8,0},{12,4},{16,24},{20,28},{24,16},{28,20},{1,9},{5... | collective-permute-start | bytes 221192 | tf_op jit(solution)/shard_map/ppermute | solution.py:533
  51.4 0.0 collective-permute-start.13
  51.4 0.5 merge2.2
  52.0 1.5 %collective-permute-start.3 = (bf16[32,1152]{1,0:T(8,128)(2,1)S(1)}, bf16[32,1152]{1,0:T(8,128)(2,1)S(1)}, u32[]{:S(2)}, u32[]{:S(2)}) collective-permute-start(bf16[32,1152]{1,0:T(8,128)(2,1)S(1)} %get-tuple-element.37), channel_id=1, source_target_pairs={{0,16},{4,20},{8,24},{12,28},{16,0},{20,4},{24,8},{28,12},{1,17},{... | collective-permute-start | bytes 221192 | tf_op jit(solution)/shard_map/ppermute | solution.py:533
  53.5 4.4 %collective-permute-start.4 = (bf16[32,1152]{1,0:T(8,128)(2,1)S(1)}, bf16[32,1152]{1,0:T(8,128)(2,1)S(1)}, u32[]{:S(2)}, u32[]{:S(2)}) collective-permute-start(bf16[32,1152]{1,0:T(8,128)(2,1)S(1)} %get-tuple-element.38), channel_id=1, source_target_pairs={{0,8},{4,12},{8,0},{12,4},{16,24},{20,28},{24,16},{28,20},{1,9},{5... | collective-permute-start | bytes 221192 | tf_op jit(solution)/shard_map/ppermute | solution.py:533
  57.9 0.0 collective-permute-done.11.refs_1_
  57.9 0.0 collective-permute-start.5
  57.9 0.0 collective-permute-done.12.refs_2_
  57.9 0.4 collective-permute-done.13.refs_3_
  58.3 0.3 merge4.3.refs_5_
  58.6 1.1 %collective-permute-start.14 = (bf16[32,1024]{1,0:T(8,128)(2,1)S(1)}, bf16[32,1024]{1,0:T(8,128)(2,1)S(1)}, u32[]{:S(2)}, u32[]{:S(2)}) collective-permute-start(bf16[32,1024]{1,0:T(8,128)(2,1)S(1)} %merge4.3.refs_5_), channel_id=1, source_target_pairs={{0,16},{4,20},{8,24},{12,28},{16,0},{20,4},{24,8},{28,12},{1,17},{... | collective-permute-start | bytes 196616 | tf_op jit(solution)/shard_map/ppermute | solution.py:533
  59.8 2.9 %collective-permute-start.15 = (bf16[32,1024]{1,0:T(8,128)(2,1)S(1)}, bf16[32,1024]{1,0:T(8,128)(2,1)S(1)}, u32[]{:S(2)}, u32[]{:S(2)}) collective-permute-start(bf16[32,1024]{1,0:T(8,128)(2,1)S(1)} %merge4.3.refs_5_), channel_id=1, source_target_pairs={{0,8},{4,12},{8,0},{12,4},{16,24},{20,28},{24,16},{28,20},{1,9},{5... | collective-permute-start | bytes 196616 | tf_op jit(solution)/shard_map/ppermute | solution.py:533
  62.7 0.0 collective-permute-done.3.refs_1_
  62.7 1.5 %collective-permute-start.16 = (bf16[32,1024]{1,0:T(8,128)(2,1)S(1)}, bf16[32,1024]{1,0:T(8,128)(2,1)S(1)}, u32[]{:S(2)}, u32[]{:S(2)}) collective-permute-start(bf16[32,1024]{1,0:T(8,128)(2,1)S(1)} %merge4.3.refs_5_), channel_id=1, source_target_pairs={{0,24},{4,28},{8,16},{12,20},{16,8},{20,12},{24,0},{28,4},{1,25},{... | collective-permute-start | bytes 196616 | tf_op jit(solution)/shard_map/ppermute | solution.py:533
  64.2 0.3 collective-permute-done.5.refs_3_
  64.6 0.3 merge4.2.refs_0_
  64.9 3.2 %collective-permute-start.6 = (bf16[32,1024]{1,0:T(8,128)(2,1)S(1)}, bf16[32,1024]{1,0:T(8,128)(2,1)S(1)}, u32[]{:S(2)}, u32[]{:S(2)}) collective-permute-start(bf16[32,1024]{1,0:T(8,128)(2,1)S(1)} %merge4.2.refs_0_), channel_id=1, source_target_pairs={{0,16},{4,20},{8,24},{12,28},{16,0},{20,4},{24,8},{28,12},{1,17},{... | collective-permute-start | bytes 196616 | tf_op jit(solution)/shard_map/ppermute | solution.py:533
  68.1 0.0 collective-permute-done.14.refs_6_
  68.1 3.3 %collective-permute-start.8 = (bf16[32,1024]{1,0:T(8,128)(2,1)S(1)}, bf16[32,1024]{1,0:T(8,128)(2,1)S(1)}, u32[]{:S(2)}, u32[]{:S(2)}) collective-permute-start(bf16[32,1024]{1,0:T(8,128)(2,1)S(1)} %merge4.2.refs_0_), channel_id=1, source_target_pairs={{0,24},{4,28},{8,16},{12,20},{16,8},{20,12},{24,0},{28,4},{1,25},{... | collective-permute-start | bytes 196616 | tf_op jit(solution)/shard_map/ppermute | solution.py:533
  71.4 0.1 collective-permute-start.17
  71.5 1.0 %collective-permute-done.6.refs_1_ = bf16[32,1024]{1,0:T(8,128)(2,1)S(1)} collective-permute-done((bf16[32,1024]{1,0:T(8,128)(2,1)S(1)}, bf16[32,1024]{1,0:T(8,128)(2,1)S(1)}, u32[]{:S(2)}, u32[]{:S(2)}) %collective-permute-start.6) | collective-permute-done | bytes 65568 | tf_op jit(solution)/shard_map/ppermute | solution.py:533
  72.5 0.2 collective-permute-done.7.refs_2_
  72.8 1.5 %collective-permute-done.8.refs_3_ = bf16[32,1024]{1,0:T(8,128)(2,1)S(1)} collective-permute-done((bf16[32,1024]{1,0:T(8,128)(2,1)S(1)}, bf16[32,1024]{1,0:T(8,128)(2,1)S(1)}, u32[]{:S(2)}, u32[]{:S(2)}) %collective-permute-start.8) | collective-permute-done | bytes 65568 | tf_op jit(solution)/shard_map/ppermute | solution.py:533
  74.3 1.1 %collective-permute-start.9 = (bf16[128,1024]{1,0:T(8,128)(2,1)S(1)}, bf16[128,1024]{1,0:T(8,128)(2,1)S(1)}, u32[]{:S(2)}, u32[]{:S(2)}) collective-permute-start(bf16[128,1024]{1,0:T(8,128)(2,1)S(1)} %pad_maximum_fusion), channel_id=1, source_target_pairs={{0,4},{4,0},{8,12},{12,8},{16,20},{20,16},{24,28},{28,24},{1,5},{5... | collective-permute-start | bytes 786440 | tf_op jit(solution)/shard_map/ppermute | solution.py:533
  75.4 2.7 %collective-permute-done.17.refs_9_ = bf16[128,1024]{1,0:T(8,128)(2,1)S(1)} collective-permute-done((bf16[128,1024]{1,0:T(8,128)(2,1)S(1)}, bf16[128,1024]{1,0:T(8,128)(2,1)S(1)}, u32[]{:S(2)}, u32[]{:S(2)}) %collective-permute-start.17) | collective-permute-done | bytes 262176 | tf_op jit(solution)/shard_map/ppermute | solution.py:533
  78.1 2.8 %collective-permute-done.9.refs_4_ = bf16[128,1024]{1,0:T(8,128)(2,1)S(1)} collective-permute-done((bf16[128,1024]{1,0:T(8,128)(2,1)S(1)}, bf16[128,1024]{1,0:T(8,128)(2,1)S(1)}, u32[]{:S(2)}, u32[]{:S(2)}) %collective-permute-start.9) | collective-permute-done | bytes 262176 | tf_op jit(solution)/shard_map/ppermute | solution.py:533
  80.9 1.3 %project.1 = (f32[128,1024]{1,0:T(8,128)S(1)}, bf16[128,1024]{1,0:T(8,128)(2,1)S(1)}) custom-call(bf16[32,1024]{1,0:T(8,128)(2,1)S(1)} %merge4.2.refs_0_, bf16[32,1024]{1,0:T(8,128)(2,1)S(1)} %collective-permute-done.6.refs_1_, bf16[32,1024]{1,0:T(8,128)(2,1)S(1)} %collective-permute-done.7.refs_2_, bf16[32,1024]{1,0:T(8,128)(2,1)S(1)} %collective-permute-done.8.refs_3_, ...), custom_call_target="tpu_custom_call" | custom-call | flops 1073741824 | bytes 4194304 | tf_op jit(solution)/shard_map/project/pallas_call | solution.py:519
  82.3 0.1 collective-permute-start.18
  82.4 1.5 %collective-permute-done.18 = bf16[128,1024]{1,0:T(8,128)(2,1)S(1)} collective-permute-done((bf16[128,1024]{1,0:T(8,128)(2,1)S(1)}, bf16[128,1024]{1,0:T(8,128)(2,1)S(1)}, u32[]{:S(2)}, u32[]{:S(2)}) %collective-permute-start.18) | collective-permute-done | bytes 262176 | tf_op jit(solution)/shard_map/ppermute | solution.py:533
  83.9 0.1 convert_add_fusion
  84.0 1.6 %collective-permute-start.19 = (bf16[1,64,1024]{2,1,0:T(8,128)(2,1)S(1)}, bf16[1,64,1024]{2,1,0:T(8,128)(2,1)S(1)}, u32[]{:S(2)}, u32[]{:S(2)}) collective-permute-start(bf16[1,64,1024]{2,1,0:T(8,128)(2,1)S(1)} %fusion.1), channel_id=1, source_target_pairs={{0,2},{1,3},{2,0},{3,1},{4,6},{5,7},{6,4},{7,5},{8,10},{9,11},{10,... | collective-permute-start | bytes 393224 | tf_op jit(solution)/shard_map/ppermute | solution.py:533
  85.5 4.1 %collective-permute-done.19 = bf16[1,64,1024]{2,1,0:T(8,128)(2,1)S(1)} collective-permute-done((bf16[1,64,1024]{2,1,0:T(8,128)(2,1)S(1)}, bf16[1,64,1024]{2,1,0:T(8,128)(2,1)S(1)}, u32[]{:S(2)}, u32[]{:S(2)}) %collective-permute-start.19) | collective-permute-done | bytes 131104 | tf_op jit(solution)/shard_map/ppermute | solution.py:533
  89.6 0.7 fusion.2
  (24 shorter events, 0.1 us)
Async XLA Ops:
  0.0 8.6 %copy-start.1 = (bf16[256,16,128]{2,1,0:T(8,128)(2,1)S(1)}, bf16[256,16,128]{2,1,0:T(8,128)(2,1)}, u32[]{:S(2)}) copy-start(bf16[256,16,128]{2,1,0:T(8,128)(2,1)} %q_ref.1) | copy-start | bytes 3145732
  0.0 1.1 %copy-start.2 = (bf16[64,16,2,128]{3,2,1,0:T(2,128)(2,1)S(1)}, bf16[64,16,2,128]{3,2,1,0:T(2,128)(2,1)}, u32[]{:S(2)}) copy-start(bf16[64,16,2,128]{3,2,1,0:T(2,128)(2,1)} %keys_ref.1) | copy-start | bytes 1572868
  1.1 0.7 copy-start.7
  1.8 6.8 %copy-start.3 = (bf16[64,16,2,128]{3,2,1,0:T(2,128)(2,1)S(1)}, bf16[64,16,2,128]{3,2,1,0:T(2,128)(2,1)}, u32[]{:S(2)}) copy-start(bf16[64,16,2,128]{3,2,1,0:T(2,128)(2,1)} %keys_ref.1) | copy-start | bytes 1572868
  1.8 6.8 %copy-start.4 = (bf16[64,16,2,128]{3,2,1,0:T(2,128)(2,1)S(1)}, bf16[64,16,2,128]{3,2,1,0:T(2,128)(2,1)}, u32[]{:S(2)}) copy-start(bf16[64,16,2,128]{3,2,1,0:T(2,128)(2,1)} %v_ref.1) | copy-start | bytes 1572868
  1.8 6.8 %copy-start.5 = (f32[16,6,11]{0,1,2:T(8,128)S(1)}, f32[16,6,11]{0,1,2:T(8,128)}, u32[]{:S(2)}) copy-start(f32[16,6,11]{0,1,2:T(8,128)} %param.13) | copy-start | bytes 12676
  1.8 6.8 %copy-start.6 = (f32[16,2]{0,1:T(2,128)S(1)}, f32[16,2]{0,1:T(2,128)}, u32[]{:S(2)}) copy-start(f32[16,2]{0,1:T(2,128)} %param.14) | copy-start | bytes 388
  1.8 6.8 %copy-start.8 = (s32[64]{0:T(128)S(1)}, s32[64]{0:T(128)}, u32[]{:S(2)}) copy-start(s32[64]{0:T(128)} %table_ref.3) | copy-start | bytes 772
  2.4 13.6 %collective-permute-start = (bf16[16,2,128]{2,1,0:T(2,128)(2,1)S(1)}, bf16[16,2,128]{2,1,0:T(2,128)(2,1)S(1)}, u32[]{:S(2)}, u32[]{:S(2)}) collective-permute-start(bf16[16,2,128]{2,1,0:T(2,128)(2,1)S(1)} %get-tuple-element.31), channel_id=1, source_target_pairs={{0,4},{4,8},{8,12},{12,16},{16,20},{20,24},{24,28},{1,5},{5,9},{9,... | collective-permute-start | bytes 24584 | tf_op jit(solution)/shard_map/ppermute | solution.py:546
  7.3 8.8 %collective-permute-start.1 = (bf16[16,2,128]{2,1,0:T(2,128)(2,1)S(1)}, bf16[16,2,128]{2,1,0:T(2,128)(2,1)S(1)}, u32[]{:S(2)}, u32[]{:S(2)}) collective-permute-start(bf16[16,2,128]{2,1,0:T(2,128)(2,1)S(1)} %get-tuple-element.32), channel_id=1, source_target_pairs={{4,0},{8,4},{12,8},{16,12},{20,16},{24,20},{28,24},{5,1},{9,5},{13... | collective-permute-start | bytes 24584 | tf_op jit(solution)/shard_map/ppermute | solution.py:547
  26.1 13.1 %collective-permute-start.10 = (bf16[128,1152]{1,0:T(8,128)(2,1)S(1)}, bf16[128,1152]{1,0:T(8,128)(2,1)S(1)}, u32[]{:S(2)}, u32[]{:S(2)}) collective-permute-start(bf16[128,1152]{1,0:T(8,128)(2,1)S(1)} %get-tuple-element.42), channel_id=1, source_target_pairs={{0,4},{4,0},{8,12},{12,8},{16,20},{20,16},{24,28},{28,24},{1,5},{5... | collective-permute-start | bytes 884744 | tf_op jit(solution)/shard_map/ppermute | solution.py:533
  28.8 52.2 %copy-start = (bf16[2048,1024]{1,0:T(8,128)(2,1)S(1)}, bf16[2048,1024]{1,0:T(8,128)(2,1)}, u32[]{:S(2)}) copy-start(bf16[2048,1024]{1,0:T(8,128)(2,1)} %refs_10_.1) | copy-start | bytes 12582916
  39.1 12.3 %collective-permute-start.2 = (bf16[128,1152]{1,0:T(8,128)(2,1)S(1)}, bf16[128,1152]{1,0:T(8,128)(2,1)S(1)}, u32[]{:S(2)}, u32[]{:S(2)}) collective-permute-start(bf16[128,1152]{1,0:T(8,128)(2,1)S(1)} %get-tuple-element.35), channel_id=1, source_target_pairs={{0,4},{4,0},{8,12},{12,8},{16,20},{20,16},{24,28},{28,24},{1,5},{5... | collective-permute-start | bytes 884744 | tf_op jit(solution)/shard_map/ppermute | solution.py:533
  39.7 18.2 %collective-permute-start.11 = (bf16[32,1152]{1,0:T(8,128)(2,1)S(1)}, bf16[32,1152]{1,0:T(8,128)(2,1)S(1)}, u32[]{:S(2)}, u32[]{:S(2)}) collective-permute-start(bf16[32,1152]{1,0:T(8,128)(2,1)S(1)} %get-tuple-element.44), channel_id=1, source_target_pairs={{0,16},{4,20},{8,24},{12,28},{16,0},{20,4},{24,8},{28,12},{1,17},{... | collective-permute-start | bytes 221192 | tf_op jit(solution)/shard_map/ppermute | solution.py:533
  43.8 14.1 %collective-permute-start.12 = (bf16[32,1152]{1,0:T(8,128)(2,1)S(1)}, bf16[32,1152]{1,0:T(8,128)(2,1)S(1)}, u32[]{:S(2)}, u32[]{:S(2)}) collective-permute-start(bf16[32,1152]{1,0:T(8,128)(2,1)S(1)} %get-tuple-element.45), channel_id=1, source_target_pairs={{0,8},{4,12},{8,0},{12,4},{16,24},{20,28},{24,16},{28,20},{1,9},{5... | collective-permute-start | bytes 221192 | tf_op jit(solution)/shard_map/ppermute | solution.py:533
  51.4 6.9 %collective-permute-start.13 = (bf16[32,1152]{1,0:T(8,128)(2,1)S(1)}, bf16[32,1152]{1,0:T(8,128)(2,1)S(1)}, u32[]{:S(2)}, u32[]{:S(2)}) collective-permute-start(bf16[32,1152]{1,0:T(8,128)(2,1)S(1)} %get-tuple-element.46), channel_id=1, source_target_pairs={{0,24},{4,28},{8,16},{12,20},{16,8},{20,12},{24,0},{28,4},{1,25},{... | collective-permute-start | bytes 221192 | tf_op jit(solution)/shard_map/ppermute | solution.py:533
  52.0 10.7 %collective-permute-start.3 = (bf16[32,1152]{1,0:T(8,128)(2,1)S(1)}, bf16[32,1152]{1,0:T(8,128)(2,1)S(1)}, u32[]{:S(2)}, u32[]{:S(2)}) collective-permute-start(bf16[32,1152]{1,0:T(8,128)(2,1)S(1)} %get-tuple-element.37), channel_id=1, source_target_pairs={{0,16},{4,20},{8,24},{12,28},{16,0},{20,4},{24,8},{28,12},{1,17},{... | collective-permute-start | bytes 221192 | tf_op jit(solution)/shard_map/ppermute | solution.py:533
  53.5 10.7 %collective-permute-start.4 = (bf16[32,1152]{1,0:T(8,128)(2,1)S(1)}, bf16[32,1152]{1,0:T(8,128)(2,1)S(1)}, u32[]{:S(2)}, u32[]{:S(2)}) collective-permute-start(bf16[32,1152]{1,0:T(8,128)(2,1)S(1)} %get-tuple-element.38), channel_id=1, source_target_pairs={{0,8},{4,12},{8,0},{12,4},{16,24},{20,28},{24,16},{28,20},{1,9},{5... | collective-permute-start | bytes 221192 | tf_op jit(solution)/shard_map/ppermute | solution.py:533
  57.9 6.6 %collective-permute-start.5 = (bf16[32,1152]{1,0:T(8,128)(2,1)S(1)}, bf16[32,1152]{1,0:T(8,128)(2,1)S(1)}, u32[]{:S(2)}, u32[]{:S(2)}) collective-permute-start(bf16[32,1152]{1,0:T(8,128)(2,1)S(1)} %get-tuple-element.39), channel_id=1, source_target_pairs={{0,24},{4,28},{8,16},{12,20},{16,8},{20,12},{24,0},{28,4},{1,25},{... | collective-permute-start | bytes 221192 | tf_op jit(solution)/shard_map/ppermute | solution.py:533
  58.6 9.4 %collective-permute-start.14 = (bf16[32,1024]{1,0:T(8,128)(2,1)S(1)}, bf16[32,1024]{1,0:T(8,128)(2,1)S(1)}, u32[]{:S(2)}, u32[]{:S(2)}) collective-permute-start(bf16[32,1024]{1,0:T(8,128)(2,1)S(1)} %merge4.3.refs_5_), channel_id=1, source_target_pairs={{0,16},{4,20},{8,24},{12,28},{16,0},{20,4},{24,8},{28,12},{1,17},{... | collective-permute-start | bytes 196616 | tf_op jit(solution)/shard_map/ppermute | solution.py:533
  59.8 11.6 %collective-permute-start.15 = (bf16[32,1024]{1,0:T(8,128)(2,1)S(1)}, bf16[32,1024]{1,0:T(8,128)(2,1)S(1)}, u32[]{:S(2)}, u32[]{:S(2)}) collective-permute-start(bf16[32,1024]{1,0:T(8,128)(2,1)S(1)} %merge4.3.refs_5_), channel_id=1, source_target_pairs={{0,8},{4,12},{8,0},{12,4},{16,24},{20,28},{24,16},{28,20},{1,9},{5... | collective-permute-start | bytes 196616 | tf_op jit(solution)/shard_map/ppermute | solution.py:533
  62.7 8.7 %collective-permute-start.16 = (bf16[32,1024]{1,0:T(8,128)(2,1)S(1)}, bf16[32,1024]{1,0:T(8,128)(2,1)S(1)}, u32[]{:S(2)}, u32[]{:S(2)}) collective-permute-start(bf16[32,1024]{1,0:T(8,128)(2,1)S(1)} %merge4.3.refs_5_), channel_id=1, source_target_pairs={{0,24},{4,28},{8,16},{12,20},{16,8},{20,12},{24,0},{28,4},{1,25},{... | collective-permute-start | bytes 196616 | tf_op jit(solution)/shard_map/ppermute | solution.py:533
  64.9 7.6 %collective-permute-start.6 = (bf16[32,1024]{1,0:T(8,128)(2,1)S(1)}, bf16[32,1024]{1,0:T(8,128)(2,1)S(1)}, u32[]{:S(2)}, u32[]{:S(2)}) collective-permute-start(bf16[32,1024]{1,0:T(8,128)(2,1)S(1)} %merge4.2.refs_0_), channel_id=1, source_target_pairs={{0,16},{4,20},{8,24},{12,28},{16,0},{20,4},{24,8},{28,12},{1,17},{... | collective-permute-start | bytes 196616 | tf_op jit(solution)/shard_map/ppermute | solution.py:533
  68.1 4.7 %collective-permute-start.7 = (bf16[32,1024]{1,0:T(8,128)(2,1)S(1)}, bf16[32,1024]{1,0:T(8,128)(2,1)S(1)}, u32[]{:S(2)}, u32[]{:S(2)}) collective-permute-start(bf16[32,1024]{1,0:T(8,128)(2,1)S(1)} %merge4.2.refs_0_), channel_id=1, source_target_pairs={{0,8},{4,12},{8,0},{12,4},{16,24},{20,28},{24,16},{28,20},{1,9},{5... | collective-permute-start | bytes 196616 | tf_op jit(solution)/shard_map/ppermute | solution.py:533
  68.1 6.2 %collective-permute-start.8 = (bf16[32,1024]{1,0:T(8,128)(2,1)S(1)}, bf16[32,1024]{1,0:T(8,128)(2,1)S(1)}, u32[]{:S(2)}, u32[]{:S(2)}) collective-permute-start(bf16[32,1024]{1,0:T(8,128)(2,1)S(1)} %merge4.2.refs_0_), channel_id=1, source_target_pairs={{0,24},{4,28},{8,16},{12,20},{16,8},{20,12},{24,0},{28,4},{1,25},{... | collective-permute-start | bytes 196616 | tf_op jit(solution)/shard_map/ppermute | solution.py:533
  71.4 6.7 %collective-permute-start.17 = (bf16[128,1024]{1,0:T(8,128)(2,1)S(1)}, bf16[128,1024]{1,0:T(8,128)(2,1)S(1)}, u32[]{:S(2)}, u32[]{:S(2)}) collective-permute-start(bf16[128,1024]{1,0:T(8,128)(2,1)S(1)} %pad_maximum_fusion.1), channel_id=1, source_target_pairs={{0,4},{4,0},{8,12},{12,8},{16,20},{20,16},{24,28},{28,24},{1,5},{5... | collective-permute-start | bytes 786440 | tf_op jit(solution)/shard_map/ppermute | solution.py:533
  74.3 6.7 %collective-permute-start.9 = (bf16[128,1024]{1,0:T(8,128)(2,1)S(1)}, bf16[128,1024]{1,0:T(8,128)(2,1)S(1)}, u32[]{:S(2)}, u32[]{:S(2)}) collective-permute-start(bf16[128,1024]{1,0:T(8,128)(2,1)S(1)} %pad_maximum_fusion), channel_id=1, source_target_pairs={{0,4},{4,0},{8,12},{12,8},{16,20},{20,16},{24,28},{28,24},{1,5},{5... | collective-permute-start | bytes 786440 | tf_op jit(solution)/shard_map/ppermute | solution.py:533
  82.3 1.6 %collective-permute-start.18 = (bf16[128,1024]{1,0:T(8,128)(2,1)S(1)}, bf16[128,1024]{1,0:T(8,128)(2,1)S(1)}, u32[]{:S(2)}, u32[]{:S(2)}) collective-permute-start(bf16[128,1024]{1,0:T(8,128)(2,1)S(1)} %get-tuple-element.48), channel_id=1, source_target_pairs={{0,1},{1,0},{2,3},{3,2},{4,5},{5,4},{6,7},{7,6},{8,9},{9,8},{10,11... | collective-permute-start | bytes 786440 | tf_op jit(solution)/shard_map/ppermute | solution.py:533
  84.0 5.6 %collective-permute-start.19 = (bf16[1,64,1024]{2,1,0:T(8,128)(2,1)S(1)}, bf16[1,64,1024]{2,1,0:T(8,128)(2,1)S(1)}, u32[]{:S(2)}, u32[]{:S(2)}) collective-permute-start(bf16[1,64,1024]{2,1,0:T(8,128)(2,1)S(1)} %fusion.1), channel_id=1, source_target_pairs={{0,2},{1,3},{2,0},{3,1},{4,6},{5,7},{6,4},{7,5},{8,10},{9,11},{10,... | collective-permute-start | bytes 393224 | tf_op jit(solution)/shard_map/ppermute | solution.py:533

commit v5 on v4

--- a/solution.py
+++ b/solution.py
@@ -144,7 +144,7 @@
     )(table, mix, conv, queries, keys, values)
 
 
-def attend_kernel(dims, kv, off_ref, qhat_ref, q_ref, k_ref, v_ref, left_ref, right_ref,
+def attend_kernel(dims, kv, off_ref, qhat_ref, q_ref, k_ref, v_ref, pair_ref, next_ref,
                   band_ref, keep_ref, send_ref,
                   kext, krot, kwrap, vext, khat, vhat, sa, sb, ca, cb, out, stat, rev, fsc, fst, msc):
     rows, heads, kvs, page, qtaps, ktaps, keys_here, split_bit = dims
@@ -160,8 +160,9 @@
 
     kext[pl.ds(0, base - page), :] = jnp.zeros((base - page, LANES), F32)
     kext[pl.ds(base + keys_here + page, TAIL_PAD - page), :] = jnp.zeros((TAIL_PAD - page, LANES), F32)
-    kext[pl.ds(base - page, page), :] = left_ref[:, kv, :].astype(F32)
-    kext[pl.ds(base + keys_here, page), :] = right_ref[:, kv, :].astype(F32)
+    odd = lax.rem(seq, 2)
+    kext[pl.ds(base - page + (1 - odd) * (keys_here + page), page), :] = pair_ref[:, kv, :].astype(F32)
+    kext[pl.ds(base - page + odd * (keys_here + page), page), :] = next_ref[:, kv, :].astype(F32)
     kext[pl.ds(base, keys_here), :] = k_ref[kv]
     vext[pl.ds(0, VPAD), :] = jnp.zeros((VPAD, LANES), F32)
     vext[pl.ds(VPAD + keys_here, VPAD), :] = jnp.zeros((VPAD, LANES), F32)
@@ -358,11 +359,11 @@
         ref[:, hk * LANES:] = stat[pl.ds(at, half), :].astype(BF)
 
 
-def attend(kv, qtaps, offset, qhat, q2, k2, v2, left, right, band):
+def attend(kv, qtaps, offset, qhat, q2, k2, v2, from_pair, from_next, band):
     hk, rows, depth = qhat.shape
     kvs, keys_here, _ = k2.shape
     heads = hk * kvs
-    page = left.shape[0]
+    page = from_pair.shape[0]
     ktaps = depth // LANES
     dims = (rows, heads, kvs, page, qtaps, ktaps, keys_here, 1)
     smem = pl.BlockSpec(memory_space=pltpu.SMEM)
@@ -396,14 +397,15 @@
         compiler_params=pltpu.CompilerParams(vmem_limit_bytes=22 * 2**20),
         cost_estimate=pl.CostEstimate(flops=flops, bytes_accessed=4 * 2**20, transcendentals=hk * rows * keys_here),
         name=f"attend{kv}",
-    )(offset, qhat, q2, k2, v2, left, right, band)
-
-
-def edge_kernel(table_ref, keys_ref, first_ref, last_ref, sem):
-    pages = keys_ref.shape[0]
+    )(offset, qhat, q2, k2, v2, from_pair, from_next, band)
+
+
+def edge_kernel(table_ref, keys_ref, pair_ref, next_ref, sem):
+    end = keys_ref.shape[0] - 1
+    odd = lax.rem(lax.axis_index("seq"), 2)
     copies = [
         pltpu.make_async_copy(keys_ref.at[table_ref[p]], ref, sem.at[i])
-        for i, (p, ref) in enumerate(((0, first_ref), (pages - 1, last_ref)))
+        for i, (p, ref) in enumerate(((end * (1 - odd), pair_ref), (end * odd, next_ref)))
     ]
     for c in copies:
         c.start()
@@ -540,11 +542,10 @@
     seq_count = lax.axis_size("seq")
     head_count = lax.axis_size("head")
 
-    ends = seq_count - 1
-
-    first, last = edge_pages(page_table, keys)
-    left = lax.ppermute(last, "seq", [(i, i + 1) for i in range(ends)])
-    right = lax.ppermute(first, "seq", [(i + 1, i) for i in range(ends)])
+    to_pair, to_next = edge_pages(page_table, keys)
+    from_pair = swap(to_pair, "seq", 1)
+    from_next = lax.ppermute(
+        to_next, "seq", [(i, j) for k in range(1, seq_count - 1, 2) for i, j in ((k, k + 1), (k + 1, k))])
 
     q2, k2, v2, band, *qhats = prepare(
         page_table, head_mix.T, jnp.transpose(conv_kernel, (2, 1, 0)), queries, keys, values)
@@ -553,7 +554,7 @@
     levels = [bits[:1]] + [bits[i:i + 2] for i in range(1, len(bits), 2)]
     pieces = []
     for kv in range(kvs):
-        parts = attend(kv, conv_kernel.shape[1], offset, qhats[kv], q2, k2, v2, left, right, band)
+        parts = attend(kv, conv_kernel.shape[1], offset, qhats[kv], q2, k2, v2, from_pair, from_next, band)
         for i, level in enumerate(levels):
             got = [swap(x, "seq", mask_of(level, rel)) for rel, x in enumerate(parts) if rel]
             parts = merge([parts[0], *got], hk, levels[i + 1] if i + 1 < len(levels) else None)

time: 90.3 us -> 87.8 us (0.972); the launches traced: 90.3 us -> 86.8 us
  starting transfers between devices: 41.4 us -> 37.8 us
    ppermute x2 -> x1, starting transfers between devices: 6.16 us -> 0.65 us  [per_device(): lax.ppermute(to_next, 'seq', [(i, j) for k in range(1, seq_count - 1, 2)...]
    ppermute x18 -> x19, starting transfers between devices: 35.3 us -> 37.1 us  [swap(): return lax.ppermute(x, axis, [(i, i ^ bit) for i in range(count)])]
    ppermute x18 -> x19, waiting for transfers between devices: 14.6 us -> 14.9 us  [swap(): return lax.ppermute(x, axis, [(i, i ^ bit) for i in range(count)])]
  transfers between devices with their start and end apart: 20 -> 20, of which waited for: 9 -> 9; matrix products, arithmetic and copies ran while one was open for 0% -> 0% of each run, Pallas kernels for 21% -> 22%
where the time goes in v5:
time: 87.8 us; the launch traced here: 86.8 us
  starting transfers between devices  37.8 us (43%)
  Pallas kernels  30.7 us (35%)
  waiting for transfers between devices  14.9 us (17%)
  local copies, waits for them, and re-layouts  1.81 us (2%)
  between operations  0.88 us (1%)
    ppermute x19, starting transfers between devices, swap(): return lax.ppermute(x, axis, [(i, i ^ bit) for i in range(count)])  37.1 us
    pallas_call x2, Pallas kernels, attend(): pl.pallas_call(functools.partial(attend_kernel, dims, kv), out_shape=(sha...  20.3 us
    ppermute x19, waiting for transfers between devices, swap(): return lax.ppermute(x, axis, [(i, i ^ bit) for i in range(count)])  14.9 us
    pallas_call x1, Pallas kernels, prepare(): pl.pallas_call(functools.partial(prepare_kernel, (rows, heads, kvs, pages...  6.74 us
    unnamed x18, local copies, waits for them, and re-layouts  1.81 us
  transfers between devices with their start and end apart: 20, of which 9 were waited for; matrix products, arithmetic and copies ran while one was open for 0% of the time, Pallas kernels for 22%

profile of v5, /device:TPU:0, one launch (start us, length us, event | category | flops | bytes accessed | tf_op | source)
XLA Modules:
  0.0 86.8 jit_solution(18053459903524758910)
XLA Ops:
  0.0 1.1 %copy-done.2 = bf16[64,16,2,128]{3,2,1,0:T(2,128)(2,1)S(1)} copy-done((bf16[64,16,2,128]{3,2,1,0:T(2,128)(2,1)S(1)}, bf16[64,16,2,128]{3,2,1,0:T(2,128)(2,1)}, u32[]{:S(2)}) %copy-start.2) | copy-done | bytes 524312
  1.1 0.7 copy-done.7
  1.8 0.6 edges.1
  2.4 3.0 %collective-permute-start = (bf16[16,2,128]{2,1,0:T(2,128)(2,1)S(1)}, bf16[16,2,128]{2,1,0:T(2,128)(2,1)S(1)}, u32[]{:S(2)}, u32[]{:S(2)}) collective-permute-start(bf16[16,2,128]{2,1,0:T(2,128)(2,1)S(1)} %get-tuple-element.31), channel_id=1, source_target_pairs={{0,4},{4,0},{8,12},{12,8},{16,20},{20,16},{24,28},{28,24},{1,5},{5... | collective-permute-start | bytes 24584 | tf_op jit(solution)/shard_map/ppermute | solution.py:535
  5.5 0.6 collective-permute-start.1
  6.2 6.7 %prepare.1 = (bf16[256,2048]{1,0:T(8,128)(2,1)S(1)}, f32[2,1024,128]{2,1,0:T(8,128)S(1)}, f32[2,1024,128]{2,1,0:T(8,128)S(1)}, f32[16,16,128]{2,1,0:T(8,128)S(1)...) custom-call(s32[64]{0:T(128)S(1)} %copy-done.8, f32[2,16]{1,0:T(2,128)S(1)} %bitcast.14, ...), custom_call_target="tpu_custom_call" | custom-call | flops 2952790016 | bytes 16777216 | tf_op jit(solution)/shard_map/prepare/pallas_call | solution.py:122
  13.6 0.0 collective-permute-done.pair_ref
  13.6 0.0 collective-permute-done.1.next_ref
  13.6 10.0 %attend1.1 = (bf16[128,1152]{1,0:T(8,128)(2,1)S(1)}, bf16[128,1152]{1,0:T(8,128)(2,1)S(1)}) custom-call(s32[1]{0:T(128)S(6)} %copy.9.off_ref, bf16[8,256,1408]{2,1,0:T(8,128)(2,1)S(1)} %get-tuple-element.40.qhat_ref, bf16[256,2048]{1,0:T(8,128)(2,1)S(1)} %get-tuple-element.28.q_ref, f32[2,1024,128]{2,1,0:T(8,128)S(1)} %get-tuple-element.29.k_ref, ...), custom_call_target="tpu_custom_call" | custom-call | flops 6979321856 | bytes 4194304 | tf_op jit(solution)/shard_map/attend1/pallas_call | solution.py:374
  23.6 4.4 %collective-permute-start.10 = (bf16[128,1152]{1,0:T(8,128)(2,1)S(1)}, bf16[128,1152]{1,0:T(8,128)(2,1)S(1)}, u32[]{:S(2)}, u32[]{:S(2)}) collective-permute-start(bf16[128,1152]{1,0:T(8,128)(2,1)S(1)} %get-tuple-element.42), channel_id=1, source_target_pairs={{0,4},{4,0},{8,12},{12,8},{16,20},{20,16},{24,28},{28,24},{1,5},{5... | collective-permute-start | bytes 884744 | tf_op jit(solution)/shard_map/ppermute | solution.py:535
  27.9 10.3 %attend0.1 = (bf16[128,1152]{1,0:T(8,128)(2,1)S(1)}, bf16[128,1152]{1,0:T(8,128)(2,1)S(1)}) custom-call(s32[1]{0:T(128)S(6)} %copy.9.off_ref, bf16[8,256,1408]{2,1,0:T(8,128)(2,1)S(1)} %get-tuple-element.27.qhat_ref, bf16[256,2048]{1,0:T(8,128)(2,1)S(1)} %get-tuple-element.28.q_ref, f32[2,1024,128]{2,1,0:T(8,128)S(1)} %get-tuple-element.29.k_ref, ...), custom_call_target="tpu_custom_call" | custom-call | flops 6979321856 | bytes 4194304 | tf_op jit(solution)/shard_map/attend0/pallas_call | solution.py:374
  38.3 0.1 collective-permute-start.2
  38.4 0.5 merge2.3
  38.9 2.6 %collective-permute-start.11 = (bf16[32,1152]{1,0:T(8,128)(2,1)S(1)}, bf16[32,1152]{1,0:T(8,128)(2,1)S(1)}, u32[]{:S(2)}, u32[]{:S(2)}) collective-permute-start(bf16[32,1152]{1,0:T(8,128)(2,1)S(1)} %get-tuple-element.44), channel_id=1, source_target_pairs={{0,16},{4,20},{8,24},{12,28},{16,0},{20,4},{24,8},{28,12},{1,17},{... | collective-permute-start | bytes 221192 | tf_op jit(solution)/shard_map/ppermute | solution.py:535
  41.5 5.1 %collective-permute-start.12 = (bf16[32,1152]{1,0:T(8,128)(2,1)S(1)}, bf16[32,1152]{1,0:T(8,128)(2,1)S(1)}, u32[]{:S(2)}, u32[]{:S(2)}) collective-permute-start(bf16[32,1152]{1,0:T(8,128)(2,1)S(1)} %get-tuple-element.45), channel_id=1, source_target_pairs={{0,8},{4,12},{8,0},{12,4},{16,24},{20,28},{24,16},{28,20},{1,9},{5... | collective-permute-start | bytes 221192 | tf_op jit(solution)/shard_map/ppermute | solution.py:535
  46.6 0.5 merge2.2
  47.2 2.3 %collective-permute-start.3 = (bf16[32,1152]{1,0:T(8,128)(2,1)S(1)}, bf16[32,1152]{1,0:T(8,128)(2,1)S(1)}, u32[]{:S(2)}, u32[]{:S(2)}) collective-permute-start(bf16[32,1152]{1,0:T(8,128)(2,1)S(1)} %get-tuple-element.37), channel_id=1, source_target_pairs={{0,16},{4,20},{8,24},{12,28},{16,0},{20,4},{24,8},{28,12},{1,17},{... | collective-permute-start | bytes 221192 | tf_op jit(solution)/shard_map/ppermute | solution.py:535
  49.4 5.4 %collective-permute-start.4 = (bf16[32,1152]{1,0:T(8,128)(2,1)S(1)}, bf16[32,1152]{1,0:T(8,128)(2,1)S(1)}, u32[]{:S(2)}, u32[]{:S(2)}) collective-permute-start(bf16[32,1152]{1,0:T(8,128)(2,1)S(1)} %get-tuple-element.38), channel_id=1, source_target_pairs={{0,8},{4,12},{8,0},{12,4},{16,24},{20,28},{24,16},{28,20},{1,9},{5... | collective-permute-start | bytes 221192 | tf_op jit(solution)/shard_map/ppermute | solution.py:535
  54.8 0.0 collective-permute-done.11.refs_1_
  54.8 0.0 collective-permute-start.5
  54.8 0.0 collective-permute-done.12.refs_2_
  54.8 0.3 merge4.3.refs_5_
  55.1 1.5 %collective-permute-start.14 = (bf16[32,1024]{1,0:T(8,128)(2,1)S(1)}, bf16[32,1024]{1,0:T(8,128)(2,1)S(1)}, u32[]{:S(2)}, u32[]{:S(2)}) collective-permute-start(bf16[32,1024]{1,0:T(8,128)(2,1)S(1)} %merge4.3.refs_5_), channel_id=1, source_target_pairs={{0,16},{4,20},{8,24},{12,28},{16,0},{20,4},{24,8},{28,12},{1,17},{... | collective-permute-start | bytes 196616 | tf_op jit(solution)/shard_map/ppermute | solution.py:535
  56.7 2.9 %collective-permute-start.15 = (bf16[32,1024]{1,0:T(8,128)(2,1)S(1)}, bf16[32,1024]{1,0:T(8,128)(2,1)S(1)}, u32[]{:S(2)}, u32[]{:S(2)}) collective-permute-start(bf16[32,1024]{1,0:T(8,128)(2,1)S(1)} %merge4.3.refs_5_), channel_id=1, source_target_pairs={{0,8},{4,12},{8,0},{12,4},{16,24},{20,28},{24,16},{28,20},{1,9},{5... | collective-permute-start | bytes 196616 | tf_op jit(solution)/shard_map/ppermute | solution.py:535
  59.6 0.0 collective-permute-done.3.refs_1_
  59.6 1.0 %collective-permute-start.16 = (bf16[32,1024]{1,0:T(8,128)(2,1)S(1)}, bf16[32,1024]{1,0:T(8,128)(2,1)S(1)}, u32[]{:S(2)}, u32[]{:S(2)}) collective-permute-start(bf16[32,1024]{1,0:T(8,128)(2,1)S(1)} %merge4.3.refs_5_), channel_id=1, source_target_pairs={{0,24},{4,28},{8,16},{12,20},{16,8},{20,12},{24,0},{28,4},{1,25},{... | collective-permute-start | bytes 196616 | tf_op jit(solution)/shard_map/ppermute | solution.py:535
  60.6 0.0 collective-permute-done.4.refs_2_
  60.6 0.5 collective-permute-done.5.refs_3_
  61.1 0.3 merge4.2.refs_0_
  61.4 3.1 %collective-permute-start.6 = (bf16[32,1024]{1,0:T(8,128)(2,1)S(1)}, bf16[32,1024]{1,0:T(8,128)(2,1)S(1)}, u32[]{:S(2)}, u32[]{:S(2)}) collective-permute-start(bf16[32,1024]{1,0:T(8,128)(2,1)S(1)} %merge4.2.refs_0_), channel_id=1, source_target_pairs={{0,16},{4,20},{8,24},{12,28},{16,0},{20,4},{24,8},{28,12},{1,17},{... | collective-permute-start | bytes 196616 | tf_op jit(solution)/shard_map/ppermute | solution.py:535
  64.5 0.0 collective-permute-start.7
  64.5 0.1 collective-permute-done.14.refs_6_
  64.7 2.0 %collective-permute-start.8 = (bf16[32,1024]{1,0:T(8,128)(2,1)S(1)}, bf16[32,1024]{1,0:T(8,128)(2,1)S(1)}, u32[]{:S(2)}, u32[]{:S(2)}) collective-permute-start(bf16[32,1024]{1,0:T(8,128)(2,1)S(1)} %merge4.2.refs_0_), channel_id=1, source_target_pairs={{0,24},{4,28},{8,16},{12,20},{16,8},{20,12},{24,0},{28,4},{1,25},{... | collective-permute-start | bytes 196616 | tf_op jit(solution)/shard_map/ppermute | solution.py:535
  66.7 0.0 collective-permute-done.15.refs_7_
  66.7 1.0 %collective-permute-start.17 = (bf16[128,1024]{1,0:T(8,128)(2,1)S(1)}, bf16[128,1024]{1,0:T(8,128)(2,1)S(1)}, u32[]{:S(2)}, u32[]{:S(2)}) collective-permute-start(bf16[128,1024]{1,0:T(8,128)(2,1)S(1)} %pad_maximum_fusion.1), channel_id=1, source_target_pairs={{0,4},{4,0},{8,12},{12,8},{16,20},{20,16},{24,28},{28,24},{1,5},{5... | collective-permute-start | bytes 786440 | tf_op jit(solution)/shard_map/ppermute | solution.py:535
  67.7 1.3 %collective-permute-done.6.refs_1_ = bf16[32,1024]{1,0:T(8,128)(2,1)S(1)} collective-permute-done((bf16[32,1024]{1,0:T(8,128)(2,1)S(1)}, bf16[32,1024]{1,0:T(8,128)(2,1)S(1)}, u32[]{:S(2)}, u32[]{:S(2)}) %collective-permute-start.6) | collective-permute-done | bytes 65568 | tf_op jit(solution)/shard_map/ppermute | solution.py:535
  68.9 0.3 collective-permute-done.7.refs_2_
  69.2 1.6 %collective-permute-done.8.refs_3_ = bf16[32,1024]{1,0:T(8,128)(2,1)S(1)} collective-permute-done((bf16[32,1024]{1,0:T(8,128)(2,1)S(1)}, bf16[32,1024]{1,0:T(8,128)(2,1)S(1)}, u32[]{:S(2)}, u32[]{:S(2)}) %collective-permute-start.8) | collective-permute-done | bytes 65568 | tf_op jit(solution)/shard_map/ppermute | solution.py:535
  70.8 1.1 %collective-permute-start.9 = (bf16[128,1024]{1,0:T(8,128)(2,1)S(1)}, bf16[128,1024]{1,0:T(8,128)(2,1)S(1)}, u32[]{:S(2)}, u32[]{:S(2)}) collective-permute-start(bf16[128,1024]{1,0:T(8,128)(2,1)S(1)} %pad_maximum_fusion), channel_id=1, source_target_pairs={{0,4},{4,0},{8,12},{12,8},{16,20},{20,16},{24,28},{28,24},{1,5},{5... | collective-permute-start | bytes 786440 | tf_op jit(solution)/shard_map/ppermute | solution.py:535
  71.9 2.8 %collective-permute-done.17.refs_9_ = bf16[128,1024]{1,0:T(8,128)(2,1)S(1)} collective-permute-done((bf16[128,1024]{1,0:T(8,128)(2,1)S(1)}, bf16[128,1024]{1,0:T(8,128)(2,1)S(1)}, u32[]{:S(2)}, u32[]{:S(2)}) %collective-permute-start.17) | collective-permute-done | bytes 262176 | tf_op jit(solution)/shard_map/ppermute | solution.py:535
  74.7 2.8 %collective-permute-done.9.refs_4_ = bf16[128,1024]{1,0:T(8,128)(2,1)S(1)} collective-permute-done((bf16[128,1024]{1,0:T(8,128)(2,1)S(1)}, bf16[128,1024]{1,0:T(8,128)(2,1)S(1)}, u32[]{:S(2)}, u32[]{:S(2)}) %collective-permute-start.9) | collective-permute-done | bytes 262176 | tf_op jit(solution)/shard_map/ppermute | solution.py:535
  77.5 1.3 %project.1 = (f32[128,1024]{1,0:T(8,128)S(1)}, bf16[128,1024]{1,0:T(8,128)(2,1)S(1)}) custom-call(bf16[32,1024]{1,0:T(8,128)(2,1)S(1)} %merge4.2.refs_0_, bf16[32,1024]{1,0:T(8,128)(2,1)S(1)} %collective-permute-done.6.refs_1_, bf16[32,1024]{1,0:T(8,128)(2,1)S(1)} %collective-permute-done.7.refs_2_, bf16[32,1024]{1,0:T(8,128)(2,1)S(1)} %collective-permute-done.8.refs_3_, ...), custom_call_target="tpu_custom_call" | custom-call | flops 1073741824 | bytes 4194304 | tf_op jit(solution)/shard_map/project/pallas_call | solution.py:521
  78.8 0.1 collective-permute-start.18
  78.9 1.5 %collective-permute-done.18 = bf16[128,1024]{1,0:T(8,128)(2,1)S(1)} collective-permute-done((bf16[128,1024]{1,0:T(8,128)(2,1)S(1)}, bf16[128,1024]{1,0:T(8,128)(2,1)S(1)}, u32[]{:S(2)}, u32[]{:S(2)}) %collective-permute-start.18) | collective-permute-done | bytes 262176 | tf_op jit(solution)/shard_map/ppermute | solution.py:535
  80.4 0.1 convert_add_fusion
  80.5 1.6 %collective-permute-start.19 = (bf16[1,64,1024]{2,1,0:T(8,128)(2,1)S(1)}, bf16[1,64,1024]{2,1,0:T(8,128)(2,1)S(1)}, u32[]{:S(2)}, u32[]{:S(2)}) collective-permute-start(bf16[1,64,1024]{2,1,0:T(8,128)(2,1)S(1)} %fusion.1), channel_id=1, source_target_pairs={{0,2},{1,3},{2,0},{3,1},{4,6},{5,7},{6,4},{7,5},{8,10},{9,11},{10,... | collective-permute-start | bytes 393224 | tf_op jit(solution)/shard_map/ppermute | solution.py:535
  82.1 4.0 %collective-permute-done.19 = bf16[1,64,1024]{2,1,0:T(8,128)(2,1)S(1)} collective-permute-done((bf16[1,64,1024]{2,1,0:T(8,128)(2,1)S(1)}, bf16[1,64,1024]{2,1,0:T(8,128)(2,1)S(1)}, u32[]{:S(2)}, u32[]{:S(2)}) %collective-permute-start.19) | collective-permute-done | bytes 131104 | tf_op jit(solution)/shard_map/ppermute | solution.py:535
  86.1 0.7 fusion.2
  (24 shorter events, 0.1 us)
Async XLA Ops:
  0.0 6.1 %copy-start.1 = (bf16[256,16,128]{2,1,0:T(8,128)(2,1)S(1)}, bf16[256,16,128]{2,1,0:T(8,128)(2,1)}, u32[]{:S(2)}) copy-start(bf16[256,16,128]{2,1,0:T(8,128)(2,1)} %q_ref.1) | copy-start | bytes 3145732
  0.0 1.1 %copy-start.2 = (bf16[64,16,2,128]{3,2,1,0:T(2,128)(2,1)S(1)}, bf16[64,16,2,128]{3,2,1,0:T(2,128)(2,1)}, u32[]{:S(2)}) copy-start(bf16[64,16,2,128]{3,2,1,0:T(2,128)(2,1)} %keys_ref.1) | copy-start | bytes 1572868
  1.1 0.7 copy-start.7
  1.8 4.3 %copy-start.3 = (bf16[64,16,2,128]{3,2,1,0:T(2,128)(2,1)S(1)}, bf16[64,16,2,128]{3,2,1,0:T(2,128)(2,1)}, u32[]{:S(2)}) copy-start(bf16[64,16,2,128]{3,2,1,0:T(2,128)(2,1)} %keys_ref.1) | copy-start | bytes 1572868
  1.8 4.3 %copy-start.4 = (bf16[64,16,2,128]{3,2,1,0:T(2,128)(2,1)S(1)}, bf16[64,16,2,128]{3,2,1,0:T(2,128)(2,1)}, u32[]{:S(2)}) copy-start(bf16[64,16,2,128]{3,2,1,0:T(2,128)(2,1)} %v_ref.1) | copy-start | bytes 1572868
  1.8 4.3 %copy-start.5 = (f32[16,6,11]{0,1,2:T(8,128)S(1)}, f32[16,6,11]{0,1,2:T(8,128)}, u32[]{:S(2)}) copy-start(f32[16,6,11]{0,1,2:T(8,128)} %param.13) | copy-start | bytes 12676
  1.8 4.4 %copy-start.6 = (f32[16,2]{0,1:T(2,128)S(1)}, f32[16,2]{0,1:T(2,128)}, u32[]{:S(2)}) copy-start(f32[16,2]{0,1:T(2,128)} %param.14) | copy-start | bytes 388
  1.8 4.4 %copy-start.8 = (s32[64]{0:T(128)S(1)}, s32[64]{0:T(128)}, u32[]{:S(2)}) copy-start(s32[64]{0:T(128)} %table_ref.3) | copy-start | bytes 772
  2.4 11.2 %collective-permute-start = (bf16[16,2,128]{2,1,0:T(2,128)(2,1)S(1)}, bf16[16,2,128]{2,1,0:T(2,128)(2,1)S(1)}, u32[]{:S(2)}, u32[]{:S(2)}) collective-permute-start(bf16[16,2,128]{2,1,0:T(2,128)(2,1)S(1)} %get-tuple-element.31), channel_id=1, source_target_pairs={{0,4},{4,0},{8,12},{12,8},{16,20},{20,16},{24,28},{28,24},{1,5},{5... | collective-permute-start | bytes 24584 | tf_op jit(solution)/shard_map/ppermute | solution.py:535
  5.5 8.1 %collective-permute-start.1 = (bf16[16,2,128]{2,1,0:T(2,128)(2,1)S(1)}, bf16[16,2,128]{2,1,0:T(2,128)(2,1)S(1)}, u32[]{:S(2)}, u32[]{:S(2)}) collective-permute-start(bf16[16,2,128]{2,1,0:T(2,128)(2,1)S(1)} %get-tuple-element.32), channel_id=1, source_target_pairs={{4,8},{8,4},{12,16},{16,12},{20,24},{24,20},{5,9},{9,5},{13,17},{1... | collective-permute-start | bytes 24584 | tf_op jit(solution)/shard_map/ppermute | solution.py:547
  23.6 14.8 %collective-permute-start.10 = (bf16[128,1152]{1,0:T(8,128)(2,1)S(1)}, bf16[128,1152]{1,0:T(8,128)(2,1)S(1)}, u32[]{:S(2)}, u32[]{:S(2)}) collective-permute-start(bf16[128,1152]{1,0:T(8,128)(2,1)S(1)} %get-tuple-element.42), channel_id=1, source_target_pairs={{0,4},{4,0},{8,12},{12,8},{16,20},{20,16},{24,28},{28,24},{1,5},{5... | collective-permute-start | bytes 884744 | tf_op jit(solution)/shard_map/ppermute | solution.py:535
  27.9 49.6 %copy-start = (bf16[2048,1024]{1,0:T(8,128)(2,1)S(1)}, bf16[2048,1024]{1,0:T(8,128)(2,1)}, u32[]{:S(2)}) copy-start(bf16[2048,1024]{1,0:T(8,128)(2,1)} %refs_10_.1) | copy-start | bytes 12582916
  38.3 8.4 %collective-permute-start.2 = (bf16[128,1152]{1,0:T(8,128)(2,1)S(1)}, bf16[128,1152]{1,0:T(8,128)(2,1)S(1)}, u32[]{:S(2)}, u32[]{:S(2)}) collective-permute-start(bf16[128,1152]{1,0:T(8,128)(2,1)S(1)} %get-tuple-element.35), channel_id=1, source_target_pairs={{0,4},{4,0},{8,12},{12,8},{16,20},{20,16},{24,28},{28,24},{1,5},{5... | collective-permute-start | bytes 884744 | tf_op jit(solution)/shard_map/ppermute | solution.py:535
  38.9 15.9 %collective-permute-start.11 = (bf16[32,1152]{1,0:T(8,128)(2,1)S(1)}, bf16[32,1152]{1,0:T(8,128)(2,1)S(1)}, u32[]{:S(2)}, u32[]{:S(2)}) collective-permute-start(bf16[32,1152]{1,0:T(8,128)(2,1)S(1)} %get-tuple-element.44), channel_id=1, source_target_pairs={{0,16},{4,20},{8,24},{12,28},{16,0},{20,4},{24,8},{28,12},{1,17},{... | collective-permute-start | bytes 221192 | tf_op jit(solution)/shard_map/ppermute | solution.py:535
  41.5 13.2 %collective-permute-start.12 = (bf16[32,1152]{1,0:T(8,128)(2,1)S(1)}, bf16[32,1152]{1,0:T(8,128)(2,1)S(1)}, u32[]{:S(2)}, u32[]{:S(2)}) collective-permute-start(bf16[32,1152]{1,0:T(8,128)(2,1)S(1)} %get-tuple-element.45), channel_id=1, source_target_pairs={{0,8},{4,12},{8,0},{12,4},{16,24},{20,28},{24,16},{28,20},{1,9},{5... | collective-permute-start | bytes 221192 | tf_op jit(solution)/shard_map/ppermute | solution.py:535
  46.6 8.2 %collective-permute-start.13 = (bf16[32,1152]{1,0:T(8,128)(2,1)S(1)}, bf16[32,1152]{1,0:T(8,128)(2,1)S(1)}, u32[]{:S(2)}, u32[]{:S(2)}) collective-permute-start(bf16[32,1152]{1,0:T(8,128)(2,1)S(1)} %get-tuple-element.46), channel_id=1, source_target_pairs={{0,24},{4,28},{8,16},{12,20},{16,8},{20,12},{24,0},{28,4},{1,25},{... | collective-permute-start | bytes 221192 | tf_op jit(solution)/shard_map/ppermute | solution.py:535
  47.2 12.4 %collective-permute-start.3 = (bf16[32,1152]{1,0:T(8,128)(2,1)S(1)}, bf16[32,1152]{1,0:T(8,128)(2,1)S(1)}, u32[]{:S(2)}, u32[]{:S(2)}) collective-permute-start(bf16[32,1152]{1,0:T(8,128)(2,1)S(1)} %get-tuple-element.37), channel_id=1, source_target_pairs={{0,16},{4,20},{8,24},{12,28},{16,0},{20,4},{24,8},{28,12},{1,17},{... | collective-permute-start | bytes 221192 | tf_op jit(solution)/shard_map/ppermute | solution.py:535
  49.4 11.2 %collective-permute-start.4 = (bf16[32,1152]{1,0:T(8,128)(2,1)S(1)}, bf16[32,1152]{1,0:T(8,128)(2,1)S(1)}, u32[]{:S(2)}, u32[]{:S(2)}) collective-permute-start(bf16[32,1152]{1,0:T(8,128)(2,1)S(1)} %get-tuple-element.38), channel_id=1, source_target_pairs={{0,8},{4,12},{8,0},{12,4},{16,24},{20,28},{24,16},{28,20},{1,9},{5... | collective-permute-start | bytes 221192 | tf_op jit(solution)/shard_map/ppermute | solution.py:535
  54.8 6.3 %collective-permute-start.5 = (bf16[32,1152]{1,0:T(8,128)(2,1)S(1)}, bf16[32,1152]{1,0:T(8,128)(2,1)S(1)}, u32[]{:S(2)}, u32[]{:S(2)}) collective-permute-start(bf16[32,1152]{1,0:T(8,128)(2,1)S(1)} %get-tuple-element.39), channel_id=1, source_target_pairs={{0,24},{4,28},{8,16},{12,20},{16,8},{20,12},{24,0},{28,4},{1,25},{... | collective-permute-start | bytes 221192 | tf_op jit(solution)/shard_map/ppermute | solution.py:535
  55.1 9.5 %collective-permute-start.14 = (bf16[32,1024]{1,0:T(8,128)(2,1)S(1)}, bf16[32,1024]{1,0:T(8,128)(2,1)S(1)}, u32[]{:S(2)}, u32[]{:S(2)}) collective-permute-start(bf16[32,1024]{1,0:T(8,128)(2,1)S(1)} %merge4.3.refs_5_), channel_id=1, source_target_pairs={{0,16},{4,20},{8,24},{12,28},{16,0},{20,4},{24,8},{28,12},{1,17},{... | collective-permute-start | bytes 196616 | tf_op jit(solution)/shard_map/ppermute | solution.py:535
  56.7 10.0 %collective-permute-start.15 = (bf16[32,1024]{1,0:T(8,128)(2,1)S(1)}, bf16[32,1024]{1,0:T(8,128)(2,1)S(1)}, u32[]{:S(2)}, u32[]{:S(2)}) collective-permute-start(bf16[32,1024]{1,0:T(8,128)(2,1)S(1)} %merge4.3.refs_5_), channel_id=1, source_target_pairs={{0,8},{4,12},{8,0},{12,4},{16,24},{20,28},{24,16},{28,20},{1,9},{5... | collective-permute-start | bytes 196616 | tf_op jit(solution)/shard_map/ppermute | solution.py:535
  59.6 7.1 %collective-permute-start.16 = (bf16[32,1024]{1,0:T(8,128)(2,1)S(1)}, bf16[32,1024]{1,0:T(8,128)(2,1)S(1)}, u32[]{:S(2)}, u32[]{:S(2)}) collective-permute-start(bf16[32,1024]{1,0:T(8,128)(2,1)S(1)} %merge4.3.refs_5_), channel_id=1, source_target_pairs={{0,24},{4,28},{8,16},{12,20},{16,8},{20,12},{24,0},{28,4},{1,25},{... | collective-permute-start | bytes 196616 | tf_op jit(solution)/shard_map/ppermute | solution.py:535
  61.4 7.5 %collective-permute-start.6 = (bf16[32,1024]{1,0:T(8,128)(2,1)S(1)}, bf16[32,1024]{1,0:T(8,128)(2,1)S(1)}, u32[]{:S(2)}, u32[]{:S(2)}) collective-permute-start(bf16[32,1024]{1,0:T(8,128)(2,1)S(1)} %merge4.2.refs_0_), channel_id=1, source_target_pairs={{0,16},{4,20},{8,24},{12,28},{16,0},{20,4},{24,8},{28,12},{1,17},{... | collective-permute-start | bytes 196616 | tf_op jit(solution)/shard_map/ppermute | solution.py:535
  64.5 4.7 %collective-permute-start.7 = (bf16[32,1024]{1,0:T(8,128)(2,1)S(1)}, bf16[32,1024]{1,0:T(8,128)(2,1)S(1)}, u32[]{:S(2)}, u32[]{:S(2)}) collective-permute-start(bf16[32,1024]{1,0:T(8,128)(2,1)S(1)} %merge4.2.refs_0_), channel_id=1, source_target_pairs={{0,8},{4,12},{8,0},{12,4},{16,24},{20,28},{24,16},{28,20},{1,9},{5... | collective-permute-start | bytes 196616 | tf_op jit(solution)/shard_map/ppermute | solution.py:535
  64.7 6.2 %collective-permute-start.8 = (bf16[32,1024]{1,0:T(8,128)(2,1)S(1)}, bf16[32,1024]{1,0:T(8,128)(2,1)S(1)}, u32[]{:S(2)}, u32[]{:S(2)}) collective-permute-start(bf16[32,1024]{1,0:T(8,128)(2,1)S(1)} %merge4.2.refs_0_), channel_id=1, source_target_pairs={{0,24},{4,28},{8,16},{12,20},{16,8},{20,12},{24,0},{28,4},{1,25},{... | collective-permute-start | bytes 196616 | tf_op jit(solution)/shard_map/ppermute | solution.py:535
  66.7 8.0 %collective-permute-start.17 = (bf16[128,1024]{1,0:T(8,128)(2,1)S(1)}, bf16[128,1024]{1,0:T(8,128)(2,1)S(1)}, u32[]{:S(2)}, u32[]{:S(2)}) collective-permute-start(bf16[128,1024]{1,0:T(8,128)(2,1)S(1)} %pad_maximum_fusion.1), channel_id=1, source_target_pairs={{0,4},{4,0},{8,12},{12,8},{16,20},{20,16},{24,28},{28,24},{1,5},{5... | collective-permute-start | bytes 786440 | tf_op jit(solution)/shard_map/ppermute | solution.py:535
  70.8 6.6 %collective-permute-start.9 = (bf16[128,1024]{1,0:T(8,128)(2,1)S(1)}, bf16[128,1024]{1,0:T(8,128)(2,1)S(1)}, u32[]{:S(2)}, u32[]{:S(2)}) collective-permute-start(bf16[128,1024]{1,0:T(8,128)(2,1)S(1)} %pad_maximum_fusion), channel_id=1, source_target_pairs={{0,4},{4,0},{8,12},{12,8},{16,20},{20,16},{24,28},{28,24},{1,5},{5... | collective-permute-start | bytes 786440 | tf_op jit(solution)/shard_map/ppermute | solution.py:535
  78.8 1.6 %collective-permute-start.18 = (bf16[128,1024]{1,0:T(8,128)(2,1)S(1)}, bf16[128,1024]{1,0:T(8,128)(2,1)S(1)}, u32[]{:S(2)}, u32[]{:S(2)}) collective-permute-start(bf16[128,1024]{1,0:T(8,128)(2,1)S(1)} %get-tuple-element.48), channel_id=1, source_target_pairs={{0,1},{1,0},{2,3},{3,2},{4,5},{5,4},{6,7},{7,6},{8,9},{9,8},{10,11... | collective-permute-start | bytes 786440 | tf_op jit(solution)/shard_map/ppermute | solution.py:535
  80.5 5.6 %collective-permute-start.19 = (bf16[1,64,1024]{2,1,0:T(8,128)(2,1)S(1)}, bf16[1,64,1024]{2,1,0:T(8,128)(2,1)S(1)}, u32[]{:S(2)}, u32[]{:S(2)}) collective-permute-start(bf16[1,64,1024]{2,1,0:T(8,128)(2,1)S(1)} %fusion.1), channel_id=1, source_target_pairs={{0,2},{1,3},{2,0},{3,1},{4,6},{5,7},{6,4},{7,5},{8,10},{9,11},{10,... | collective-permute-start | bytes 393224 | tf_op jit(solution)/shard_map/ppermute | solution.py:535
